TPU v7x, 128 devices: a whole 4x4x4 slice. The times are simulated.
128 devices in a mesh: row: 8 (over x, core), col: 16 (over y, z).
Axes of the slice: x: 4, y: 4, z: 4, core: 2. Of those that a mesh axis runs over, the one named last changes fastest.
Arguments:
- features: bfloat16 [256, 256, 1280], P('row', 'col'), may hold values from -6 to 6
- known: bfloat16 [256, 256, 1280], P('row', 'col'), may hold values from -6 to 6
- known_mask: int32 [256, 256], P('row', 'col'), may hold values 0 or 1
- w_query: bfloat16 [1280, 1024], replicated, may hold values from -2 to 2
- w_keyval: bfloat16 [1280, 2048], replicated, may hold values from -2 to 2
- w_out: bfloat16 [1024, 1280], replicated, may hold values from -0.75 to 0.75
- win_anchor: int32 [8, 16, 6, 2], P('row', 'col'), may hold values from -8 to 24, as said below
- win_weight: int32 [8, 16, 6], P('row', 'col'), may hold values from 0 to 3, as said below
Outputs:
- output: bfloat16 [256, 256, 1280], P('row', 'col')
Inputs may be any that keep to these rules, and one draw needn't show every extreme that they name: `win_anchor`: A window of 16 x 16 cells starting at its anchor lies inside the canvas and within 8 cells of its tile on every side. `win_weight`: in each tile's list the slots of nonzero weight come first; every tile has 1 to 6 of them, and some tile has all 6.
All inputs are finite; a program needn't handle non-finite values. No bound on the sum of `known_mask` on one device may be relied on, other than what follows from the above.
Results may differ from a plain program's by a relative error of at most 0.012.
Values may be sent and summed in bfloat16 or wider, within the bound.
No kernel may reach another device: no remote copies, remote signals or barrier semaphores. Data moves between devices by JAX's collectives and lax.ppermute only.
A program may use at most 128 MiB of HBM per device.

v0:
```python
import math

import jax
import jax.numpy as jnp
from jax import lax
from jax.sharding import PartitionSpec as P

HD = 64
STRIDE = 4
WIN = 16
HALO = 8


def padded(x, sides, width):
    for axis, dim in sides:
        peers, length = (lax.axis_size(axis), x.shape[dim])
        up = [(i, (i + 1) % peers) for i in range(peers - 1)]
        down = [(j, i) for i, j in up]
        last = lax.slice_in_dim(x, length - width, length, axis=dim)
        initial = lax.slice_in_dim(x, 0, width, axis=dim)
        before = lax.ppermute(last, axis, up)
        after = lax.ppermute(initial, axis, down)
        x = jnp.concatenate([before, x, after], axis=dim)
    return x


def softmax_mix(queries, keys, values):
    scores = jnp.einsum("qhd,khd->hqk", queries, keys, preferred_element_type=jnp.float32) * HD ** (
        -0.5
    )
    highest = jnp.max(scores, axis=-1, keepdims=True)
    expsum = jnp.exp(scores - highest)
    weights_bf = (expsum / jnp.sum(expsum, axis=-1, keepdims=True)).astype(jnp.bfloat16)
    return jnp.einsum("hqk,khd->qhd", weights_bf, values, preferred_element_type=jnp.float32)


def lattice_attend(queries, keys, values):
    row_count, head_count, head_dim = queries.shape
    block_rows = math.gcd(row_count, 512)
    grouped = queries.reshape(row_count // block_rows, block_rows, head_count, head_dim)

    def one_block(query_block):
        return softmax_mix(query_block, keys, values).astype(jnp.bfloat16)

    return lax.map(one_block, grouped).reshape(row_count, head_count * head_dim)


def lattice_pieces(field):
    tile_rows, tile_cols, last_dim = field.shape
    shaped = field.reshape(tile_rows // STRIDE, STRIDE, tile_cols // STRIDE, STRIDE, last_dim)
    return jnp.transpose(shaped, (1, 3, 0, 2, 4)).reshape(STRIDE * STRIDE, -1, last_dim)


def send_out(pieces):
    device_count, row_count, last_dim = pieces.shape
    moved = lax.all_to_all(
        pieces.reshape(device_count, 1, row_count, last_dim),
        ("row", "col"),
        split_axis=0,
        concat_axis=1,
        tiled=True,
    )
    return moved.reshape(device_count * row_count, last_dim)


def send_back(pieces):
    device_count, row_count, last_dim = pieces.shape
    moved = lax.all_to_all(
        pieces.reshape(device_count, 1, row_count, last_dim),
        ("row", "col"),
        split_axis=0,
        concat_axis=1,
        tiled=True,
    )
    return moved.reshape(device_count, row_count, last_dim)


def fold_rims(summed, coverage, margin):
    tile_rows = summed.shape[0] - 2 * margin
    rims = jnp.concatenate([summed[:margin], summed[tile_rows + margin :]], 0)
    rim_cover = jnp.concatenate([coverage[:margin], coverage[tile_rows + margin :]], 0)
    arrived, arrived_cover = (
        padded(rims.astype(jnp.bfloat16), (("row", 0),), margin).astype(rims.dtype),
        padded(rim_cover.astype(jnp.bfloat16), (("row", 0),), margin).astype(rim_cover.dtype),
    )
    middle = summed[margin : tile_rows + margin]
    middle = (
        middle.at[:margin].add(arrived[:margin]).at[tile_rows - margin :].add(arrived[3 * margin :])
    )
    middle_cover = coverage[margin : tile_rows + margin]
    middle_cover = (
        middle_cover.at[:margin]
        .add(arrived_cover[:margin])
        .at[tile_rows - margin :]
        .add(arrived_cover[3 * margin :])
    )
    tile_cols = summed.shape[1] - 2 * margin
    side_rims = jnp.concatenate([middle[:, :margin], middle[:, tile_cols + margin :]], 1)
    side_cover = jnp.concatenate(
        [middle_cover[:, :margin], middle_cover[:, tile_cols + margin :]], 1
    )
    beside, beside_cover = (
        padded(side_rims.astype(jnp.bfloat16), (("col", 1),), margin).astype(side_rims.dtype),
        padded(side_cover.astype(jnp.bfloat16), (("col", 1),), margin).astype(side_cover.dtype),
    )
    inside = middle[:, margin : tile_cols + margin]
    inside = (
        inside.at[:, :margin]
        .add(beside[:, :margin])
        .at[:, tile_cols - margin :]
        .add(beside[:, 3 * margin :])
    )
    inside_cover = middle_cover[:, margin : tile_cols + margin]
    inside_cover = (
        inside_cover.at[:, :margin]
        .add(beside_cover[:, :margin])
        .at[:, tile_cols - margin :]
        .add(beside_cover[:, 3 * margin :])
    )
    return (inside, inside_cover)


def on_device(features, known, known_mask, w_query, w_keyval, w_out, win_anchor, win_weight):
    tile_rows, tile_cols, channels = features.shape
    inner = w_query.shape[1]
    head_count = inner // HD
    groups = lax.axis_size("row") * lax.axis_size("col") // (STRIDE * STRIDE)
    per_group = head_count // groups
    span = per_group * HD
    flat = features.reshape(tile_rows * tile_cols, channels)
    queries = jnp.dot(flat, w_query, preferred_element_type=jnp.float32).astype(jnp.bfloat16)
    keyvals = jnp.dot(flat, w_keyval, preferred_element_type=jnp.float32).astype(jnp.bfloat16)
    stacked = jnp.concatenate([queries, keyvals], 1).reshape(tile_rows, tile_cols, 3 * inner)
    split_heads = stacked.reshape(tile_rows, tile_cols, 3, groups, span)
    split_heads = jnp.transpose(split_heads, (0, 1, 3, 2, 4)).reshape(
        tile_rows, tile_cols, groups * 3 * span
    )
    pieces = lattice_pieces(split_heads)
    piece_rows = pieces.shape[1]
    pieces = pieces.reshape(STRIDE * STRIDE, piece_rows, groups, 3 * span)
    pieces = jnp.transpose(pieces, (0, 2, 1, 3)).reshape(
        STRIDE * STRIDE * groups, piece_rows, 3 * span
    )
    gathered = send_out(pieces).reshape(-1, 3, per_group, HD)
    lattice_q = gathered[:, 0]
    lattice_k = gathered[:, 1]
    lattice_v = gathered[:, 2]
    mixed = lattice_attend(lattice_q, lattice_k, lattice_v)
    returned = send_back(mixed.reshape(STRIDE * STRIDE * groups, piece_rows, span))
    returned = returned.reshape(
        STRIDE, STRIDE, groups, tile_rows // STRIDE, tile_cols // STRIDE, span
    )
    dilated = jnp.transpose(returned, (3, 0, 4, 1, 2, 5)).reshape(tile_rows, tile_cols, inner)
    extended = padded(stacked, (("row", 0), ("col", 1)), HALO)
    anchors = win_anchor.reshape(-1, 2)
    slot_weights = win_weight.reshape(-1)
    live_slots = jnp.sum((slot_weights > 0).astype(jnp.int32))

    def add_window(slot, carry):
        summed, coverage = carry
        top_row = anchors[slot, 0] + HALO
        left_col = anchors[slot, 1] + HALO
        factor = slot_weights[slot].astype(jnp.float32)
        window = lax.dynamic_slice(extended, (top_row, left_col, 0), (WIN, WIN, 3 * inner)).reshape(
            WIN * WIN, 3, head_count, HD
        )
        result = softmax_mix(window[:, 0], window[:, 1], window[:, 2]).reshape(WIN, WIN, inner)
        current = lax.dynamic_slice(summed, (top_row, left_col, 0), (WIN, WIN, inner))
        summed = lax.dynamic_update_slice(summed, current + factor * result, (top_row, left_col, 0))
        cover_now = lax.dynamic_slice(coverage, (top_row, left_col), (WIN, WIN))
        coverage = lax.dynamic_update_slice(coverage, cover_now + factor, (top_row, left_col))
        return (summed, coverage)

    start_sum = jnp.zeros((tile_rows + 2 * HALO, tile_cols + 2 * HALO, inner), jnp.float32)
    start_cover = jnp.zeros((tile_rows + 2 * HALO, tile_cols + 2 * HALO), jnp.float32)
    summed, coverage = lax.fori_loop(0, live_slots, add_window, (start_sum, start_cover))
    accum, cover_tile = fold_rims(summed, coverage, HALO)
    blended = ((dilated.astype(jnp.float32) + accum) / (1.0 + cover_tile)[..., None]).astype(
        jnp.bfloat16
    )
    projected = jnp.dot(
        blended.reshape(tile_rows * tile_cols, inner), w_out, preferred_element_type=jnp.float32
    )
    computed = (
        features.astype(jnp.float32) + projected.reshape(tile_rows, tile_cols, channels)
    ).astype(jnp.bfloat16)
    return jnp.where(known_mask[..., None] == 1, known, computed)


def solution(mesh):
    in_specs = (
        P("row", "col", None),
        P("row", "col", None),
        P("row", "col"),
        P(),
        P(),
        P(),
        P("row", "col", None, None),
        P("row", "col", None),
    )
    out_specs = P("row", "col", None)
    return jax.shard_map(
        on_device, mesh=mesh, in_specs=in_specs, out_specs=out_specs, check_vma=False
    )
```

profile of v0, /device:TPU:1, one launch (start us, length us, event | category | flops | bytes accessed | tf_op | source)
XLA Modules:
  0.0 683.8 jit_solution(1381876112337777097)
XLA Ops:
  22.9 9.3 %reshape_reshape.17 = bf16[8,4,4,4,3072]{4,3,2,1,0:T(4,128)(2,1)} reshape(bf16[32,16,8,3,128]{4,3,2,1,0:T(4,128)(2,1)} %bitcast.108) | data formatting | bytes 6291456 | tf_op jit(solution)/shard_map/reshape;reshape | solution.py:50
  47.8 10.5 %all-to-all-start = ((bf16[128,1,32,384]{3,2,1,0:T(8,128)(2,1)}), bf16[128,1,32,384]{3,2,1,0:T(8,128)(2,1)}, u32[]{:S(2)}, u32[]{:S(2)}) async-start(bf16[128,1,32,384]{3,2,1,0:T(8,128)(2,1)} %bitcast.111), calls=%async_computation | async-start | bytes 6291456 | tf_op jit(solution)/shard_map/all_to_all | solution.py:56
  71.6 27.3 %all-to-all-done = bf16[128,1,32,384]{3,2,1,0:T(8,128)(2,1)} async-done(((bf16[128,1,32,384]{3,2,1,0:T(8,128)(2,1)}), bf16[128,1,32,384]{3,2,1,0:T(8,128)(2,1)}, u32[]{:S(2)}, u32[]{:S(2)}) %all-to-all-start) | async-done | bytes 3145760 | tf_op jit(solution)/shard_map/all_to_all | solution.py:56
  98.9 11.8 %reshape_reshape.20 = bf16[4096,3,2,64]{3,2,1,0:T(2,128)(2,1)} reshape(bf16[128,1,32,384]{3,2,1,0:T(8,128)(2,1)} %all-to-all-done) | data formatting | bytes 6291456 | tf_op jit(solution)/shard_map/reshape;reshape | solution.py:144
  157.7 48.0 %while.33 = (s32[]{:T(128)}, f32[48,32,1024]{2,1,0:T(8,128)}, f32[48,32]{1,0:T(8,128)S(1)}, s32[]{:T(128)}, s32[6,2]{0,1:T(2,128)S(1)}, /*index=5*/s32[6]{0:T(12...) while((s32[]{:T(128)}, f32[48,32,1024]{2,1,0:T(8,128)}, ...), condition=%wide.region_8.9_spmd, body=%wide.region_5.8_spmd.sunk | while | flops 275251712 | bytes 43553132 | solution.py:176
  205.8 50.3 %collective-permute-start.8 = (bf16[8,32]{1,0:T(8,128)(2,1)S(1)}, bf16[8,32]{1,0:T(8,128)(2,1)S(1)}, u32[]{:S(2)}, u32[]{:S(2)}) collective-permute-start(bf16[8,32]{1,0:T(8,128)(2,1)S(1)} %get-tuple-element.286), channel_id=1, source_target_pairs={{0,16},{16,32},{32,48},{48,64},{64,80},{80,96},{96,112},{1,17},{17... | collective-permute-start | bytes 1544 | tf_op jit(solution)/shard_map/ppermute | solution.py:21
  258.3 155.0 %while.32 = (s32[]{:T(128)}, bf16[8,512,2,64]{1,3,2,0:T(8,128)(2,1)}, bf16[8,512,2,64]{1,3,2,0:T(8,128)(2,1)}, bf16[4096,2,64]{0,2,1:T(8,128)(2,1)}, bf16[4096,2,64]{0,2,1:T(8,128)(2,1)}, /*index=5*/s32[]{:T(128)}) while((s32[]{:T(128)}, bf16[8,512,2,64]{1,3,2,0:T(8,128)(2,1)}, bf16[8,512,2,64]{1,3,2,0:T(8,128)(2,1)}, ...), condition=%wide.region_3.4_spmd, body=%wide.region_0.3_spmd.sunk | while | flops 1094782976 | bytes 35922004 | solution.py:45
  258.3 10.0 %fusion.88 = (f32[2,512]{1,0:T(2,128)S(1)}, f32[2,512,4096]{2,1,0:T(8,128)}) fusion(bf16[4096,2,64]{0,2,1:T(8,128)(2,1)} %get-tuple-element.398, bf16[8,512,2,64]{1,3,2,0:T(8,128)(2,1)} %get-tuple-element.397, s32[]{:T(128)S(6)} %copy.86), kind=kOutput, calls=%fused_computation.89.clone.1 | convolution fusion | flops 549457920 | bytes 17960964 | tf_op jit(solution)/shard_map/while/body/eval_jaxpr/sub | solution.py:32
  268.3 9.4 %fusion.89 = bf16[8,512,2,64]{1,3,2,0:T(8,128)(2,1)} fusion(bf16[8,512,2,64]{1,3,2,0:T(8,128)(2,1)} %get-tuple-element.390, s32[]{:T(128)S(6)} %copy.86, bf16[4096,2,64]{0,2,1:T(8,128)(2,1)} %get-tuple-element.399, f32[2,512,4096]{2,1,0:T(8,128)} %get-tuple-element.367, f32[2,512]{1,0:T(2,128)S(1)} %get-tuple-element.368), kind=kOutput, calls=%fused_computation.10.clone.1 | convolution fusion | flops 545325056 | bytes 17960964 | tf_op jit(solution)/shard_map/while/body/eval_jaxpr/hqk,khd->qhd/dot_general | solution.py:34
  277.7 10.0 %fusion.88 = (f32[2,512]{1,0:T(2,128)S(1)}, f32[2,512,4096]{2,1,0:T(8,128)}) fusion(bf16[4096,2,64]{0,2,1:T(8,128)(2,1)} %get-tuple-element.398, bf16[8,512,2,64]{1,3,2,0:T(8,128)(2,1)} %get-tuple-element.397, s32[]{:T(128)S(6)} %copy.86), kind=kOutput, calls=%fused_computation.89.clone.1 | convolution fusion | flops 549457920 | bytes 17960964 | tf_op jit(solution)/shard_map/while/body/eval_jaxpr/sub | solution.py:32
  287.7 9.4 %fusion.89 = bf16[8,512,2,64]{1,3,2,0:T(8,128)(2,1)} fusion(bf16[8,512,2,64]{1,3,2,0:T(8,128)(2,1)} %get-tuple-element.390, s32[]{:T(128)S(6)} %copy.86, bf16[4096,2,64]{0,2,1:T(8,128)(2,1)} %get-tuple-element.399, f32[2,512,4096]{2,1,0:T(8,128)} %get-tuple-element.367, f32[2,512]{1,0:T(2,128)S(1)} %get-tuple-element.368), kind=kOutput, calls=%fused_computation.10.clone.1 | convolution fusion | flops 545325056 | bytes 17960964 | tf_op jit(solution)/shard_map/while/body/eval_jaxpr/hqk,khd->qhd/dot_general | solution.py:34
  297.0 10.0 %fusion.88 = (f32[2,512]{1,0:T(2,128)S(1)}, f32[2,512,4096]{2,1,0:T(8,128)}) fusion(bf16[4096,2,64]{0,2,1:T(8,128)(2,1)} %get-tuple-element.398, bf16[8,512,2,64]{1,3,2,0:T(8,128)(2,1)} %get-tuple-element.397, s32[]{:T(128)S(6)} %copy.86), kind=kOutput, calls=%fused_computation.89.clone.1 | convolution fusion | flops 549457920 | bytes 17960964 | tf_op jit(solution)/shard_map/while/body/eval_jaxpr/sub | solution.py:32
  307.0 9.4 %fusion.89 = bf16[8,512,2,64]{1,3,2,0:T(8,128)(2,1)} fusion(bf16[8,512,2,64]{1,3,2,0:T(8,128)(2,1)} %get-tuple-element.390, s32[]{:T(128)S(6)} %copy.86, bf16[4096,2,64]{0,2,1:T(8,128)(2,1)} %get-tuple-element.399, f32[2,512,4096]{2,1,0:T(8,128)} %get-tuple-element.367, f32[2,512]{1,0:T(2,128)S(1)} %get-tuple-element.368), kind=kOutput, calls=%fused_computation.10.clone.1 | convolution fusion | flops 545325056 | bytes 17960964 | tf_op jit(solution)/shard_map/while/body/eval_jaxpr/hqk,khd->qhd/dot_general | solution.py:34
  316.4 10.0 %fusion.88 = (f32[2,512]{1,0:T(2,128)S(1)}, f32[2,512,4096]{2,1,0:T(8,128)}) fusion(bf16[4096,2,64]{0,2,1:T(8,128)(2,1)} %get-tuple-element.398, bf16[8,512,2,64]{1,3,2,0:T(8,128)(2,1)} %get-tuple-element.397, s32[]{:T(128)S(6)} %copy.86), kind=kOutput, calls=%fused_computation.89.clone.1 | convolution fusion | flops 549457920 | bytes 17960964 | tf_op jit(solution)/shard_map/while/body/eval_jaxpr/sub | solution.py:32
  326.4 9.4 %fusion.89 = bf16[8,512,2,64]{1,3,2,0:T(8,128)(2,1)} fusion(bf16[8,512,2,64]{1,3,2,0:T(8,128)(2,1)} %get-tuple-element.390, s32[]{:T(128)S(6)} %copy.86, bf16[4096,2,64]{0,2,1:T(8,128)(2,1)} %get-tuple-element.399, f32[2,512,4096]{2,1,0:T(8,128)} %get-tuple-element.367, f32[2,512]{1,0:T(2,128)S(1)} %get-tuple-element.368), kind=kOutput, calls=%fused_computation.10.clone.1 | convolution fusion | flops 545325056 | bytes 17960964 | tf_op jit(solution)/shard_map/while/body/eval_jaxpr/hqk,khd->qhd/dot_general | solution.py:34
  335.8 10.0 %fusion.88 = (f32[2,512]{1,0:T(2,128)S(1)}, f32[2,512,4096]{2,1,0:T(8,128)}) fusion(bf16[4096,2,64]{0,2,1:T(8,128)(2,1)} %get-tuple-element.398, bf16[8,512,2,64]{1,3,2,0:T(8,128)(2,1)} %get-tuple-element.397, s32[]{:T(128)S(6)} %copy.86), kind=kOutput, calls=%fused_computation.89.clone.1 | convolution fusion | flops 549457920 | bytes 17960964 | tf_op jit(solution)/shard_map/while/body/eval_jaxpr/sub | solution.py:32
  345.8 9.4 %fusion.89 = bf16[8,512,2,64]{1,3,2,0:T(8,128)(2,1)} fusion(bf16[8,512,2,64]{1,3,2,0:T(8,128)(2,1)} %get-tuple-element.390, s32[]{:T(128)S(6)} %copy.86, bf16[4096,2,64]{0,2,1:T(8,128)(2,1)} %get-tuple-element.399, f32[2,512,4096]{2,1,0:T(8,128)} %get-tuple-element.367, f32[2,512]{1,0:T(2,128)S(1)} %get-tuple-element.368), kind=kOutput, calls=%fused_computation.10.clone.1 | convolution fusion | flops 545325056 | bytes 17960964 | tf_op jit(solution)/shard_map/while/body/eval_jaxpr/hqk,khd->qhd/dot_general | solution.py:34
  355.1 10.0 %fusion.88 = (f32[2,512]{1,0:T(2,128)S(1)}, f32[2,512,4096]{2,1,0:T(8,128)}) fusion(bf16[4096,2,64]{0,2,1:T(8,128)(2,1)} %get-tuple-element.398, bf16[8,512,2,64]{1,3,2,0:T(8,128)(2,1)} %get-tuple-element.397, s32[]{:T(128)S(6)} %copy.86), kind=kOutput, calls=%fused_computation.89.clone.1 | convolution fusion | flops 549457920 | bytes 17960964 | tf_op jit(solution)/shard_map/while/body/eval_jaxpr/sub | solution.py:32
  365.1 9.4 %fusion.89 = bf16[8,512,2,64]{1,3,2,0:T(8,128)(2,1)} fusion(bf16[8,512,2,64]{1,3,2,0:T(8,128)(2,1)} %get-tuple-element.390, s32[]{:T(128)S(6)} %copy.86, bf16[4096,2,64]{0,2,1:T(8,128)(2,1)} %get-tuple-element.399, f32[2,512,4096]{2,1,0:T(8,128)} %get-tuple-element.367, f32[2,512]{1,0:T(2,128)S(1)} %get-tuple-element.368), kind=kOutput, calls=%fused_computation.10.clone.1 | convolution fusion | flops 545325056 | bytes 17960964 | tf_op jit(solution)/shard_map/while/body/eval_jaxpr/hqk,khd->qhd/dot_general | solution.py:34
  374.5 10.0 %fusion.88 = (f32[2,512]{1,0:T(2,128)S(1)}, f32[2,512,4096]{2,1,0:T(8,128)}) fusion(bf16[4096,2,64]{0,2,1:T(8,128)(2,1)} %get-tuple-element.398, bf16[8,512,2,64]{1,3,2,0:T(8,128)(2,1)} %get-tuple-element.397, s32[]{:T(128)S(6)} %copy.86), kind=kOutput, calls=%fused_computation.89.clone.1 | convolution fusion | flops 549457920 | bytes 17960964 | tf_op jit(solution)/shard_map/while/body/eval_jaxpr/sub | solution.py:32
  384.5 9.4 %fusion.89 = bf16[8,512,2,64]{1,3,2,0:T(8,128)(2,1)} fusion(bf16[8,512,2,64]{1,3,2,0:T(8,128)(2,1)} %get-tuple-element.390, s32[]{:T(128)S(6)} %copy.86, bf16[4096,2,64]{0,2,1:T(8,128)(2,1)} %get-tuple-element.399, f32[2,512,4096]{2,1,0:T(8,128)} %get-tuple-element.367, f32[2,512]{1,0:T(2,128)S(1)} %get-tuple-element.368), kind=kOutput, calls=%fused_computation.10.clone.1 | convolution fusion | flops 545325056 | bytes 17960964 | tf_op jit(solution)/shard_map/while/body/eval_jaxpr/hqk,khd->qhd/dot_general | solution.py:34
  393.9 10.0 %fusion.88 = (f32[2,512]{1,0:T(2,128)S(1)}, f32[2,512,4096]{2,1,0:T(8,128)}) fusion(bf16[4096,2,64]{0,2,1:T(8,128)(2,1)} %get-tuple-element.398, bf16[8,512,2,64]{1,3,2,0:T(8,128)(2,1)} %get-tuple-element.397, s32[]{:T(128)S(6)} %copy.86), kind=kOutput, calls=%fused_computation.89.clone.1 | convolution fusion | flops 549457920 | bytes 17960964 | tf_op jit(solution)/shard_map/while/body/eval_jaxpr/sub | solution.py:32
  403.9 9.4 %fusion.89 = bf16[8,512,2,64]{1,3,2,0:T(8,128)(2,1)} fusion(bf16[8,512,2,64]{1,3,2,0:T(8,128)(2,1)} %get-tuple-element.390, s32[]{:T(128)S(6)} %copy.86, bf16[4096,2,64]{0,2,1:T(8,128)(2,1)} %get-tuple-element.399, f32[2,512,4096]{2,1,0:T(8,128)} %get-tuple-element.367, f32[2,512]{1,0:T(2,128)S(1)} %get-tuple-element.368), kind=kOutput, calls=%fused_computation.10.clone.1 | convolution fusion | flops 545325056 | bytes 17960964 | tf_op jit(solution)/shard_map/while/body/eval_jaxpr/hqk,khd->qhd/dot_general | solution.py:34
  424.0 199.9 %all-to-all-start.1 = ((bf16[128,1,32,128]{3,2,1,0:T(8,128)(2,1)}), bf16[128,1,32,128]{3,2,1,0:T(8,128)(2,1)}, u32[]{:S(2)}, u32[]{:S(2)}) async-start(bf16[128,1,32,128]{3,2,1,0:T(8,128)(2,1)} %bitcast.114), calls=%async_computation.1 | async-start | bytes 2097152 | tf_op jit(solution)/shard_map/all_to_all | solution.py:68
  (124 shorter events, 214.9 us)
Async XLA Ops:
  0.0 679.3 %copy-start = (bf16[1024,1280]{1,0:T(8,128)(2,1)S(1)}, bf16[1024,1280]{1,0:T(8,128)(2,1)}, u32[]{:S(2)}) copy-start(bf16[1024,1280]{1,0:T(8,128)(2,1)} %param.33) | copy-start | bytes 7864324
  0.0 3.8 copy-start.7
  0.0 4.2 copy-start.9
  8.6 49.7 %collective-permute-start.1 = (bf16[8,16,3072]{2,1,0:T(8,128)(2,1)}, bf16[8,16,3072]{2,1,0:T(8,128)(2,1)S(1)}, u32[]{:S(2)}, u32[]{:S(2)}) collective-permute-start(bf16[8,16,3072]{2,1,0:T(8,128)(2,1)} %bitcast.28), channel_id=1, source_target_pairs={{16,0},{32,16},{48,32},{64,48},{80,64},{96,80},{112,96},{17,1},{33... | collective-permute-start | bytes 2359304 | tf_op jit(solution)/shard_map/ppermute | solution.py:22
  11.9 46.4 %collective-permute-start = (bf16[8,16,3072]{2,1,0:T(8,128)(2,1)}, bf16[8,16,3072]{2,1,0:T(8,128)(2,1)}, u32[]{:S(2)}, u32[]{:S(2)}) collective-permute-start(bf16[8,16,3072]{2,1,0:T(8,128)(2,1)} %bitcast.26), channel_id=1, source_target_pairs={{0,16},{16,32},{32,48},{48,64},{64,80},{80,96},{96,112},{1,17},{17... | collective-permute-start | bytes 2359304 | tf_op jit(solution)/shard_map/ppermute | solution.py:21
  47.8 51.1 %all-to-all-start = ((bf16[128,1,32,384]{3,2,1,0:T(8,128)(2,1)}), bf16[128,1,32,384]{3,2,1,0:T(8,128)(2,1)}, u32[]{:S(2)}, u32[]{:S(2)}) async-start(bf16[128,1,32,384]{3,2,1,0:T(8,128)(2,1)} %bitcast.111), calls=%async_computation | async-start | bytes 6291456 | tf_op jit(solution)/shard_map/all_to_all | solution.py:56
  60.7 8.9 %copy-start.5 = (s32[32,16]{0,1:T(8,128)S(1)}, s32[32,16]{0,1:T(8,128)}, u32[]{:S(2)}) copy-start(s32[32,16]{0,1:T(8,128)} %param.30) | copy-start | bytes 6148
  60.7 10.2 %copy-start.11 = (s32[1,1,6]{2,1,0:T(1,128)S(1)}, s32[1,1,6]{2,1,0:T(1,128)}, u32[]{:S(2)}) copy-start(s32[1,1,6]{2,1,0:T(1,128)} %param.35) | copy-start | bytes 76
  63.3 79.6 %collective-permute-start.2 = (bf16[48,8,3072]{2,1,0:T(8,128)(2,1)}, bf16[48,8,3072]{2,1,0:T(8,128)(2,1)}, u32[]{:S(2)}, u32[]{:S(2)}) collective-permute-start(bf16[48,8,3072]{2,1,0:T(8,128)(2,1)} %get-tuple-element.276), channel_id=1, source_target_pairs={{0,1},{1,2},{2,3},{3,4},{4,5},{5,6},{6,7},{7,8},{8,9},{9,10},{10,1... | collective-permute-start | bytes 7077896 | tf_op jit(solution)/shard_map/ppermute | solution.py:21
  68.1 77.2 %collective-permute-start.3 = (bf16[48,8,3072]{2,1,0:T(8,128)(2,1)}, bf16[48,8,3072]{2,1,0:T(8,128)(2,1)}, u32[]{:S(2)}, u32[]{:S(2)}) collective-permute-start(bf16[48,8,3072]{2,1,0:T(8,128)(2,1)} %get-tuple-element.277), channel_id=1, source_target_pairs={{1,0},{2,1},{3,2},{4,3},{5,4},{6,5},{7,6},{8,7},{9,8},{10,9},{11,1... | collective-permute-start | bytes 7077896 | tf_op jit(solution)/shard_map/ppermute | solution.py:22
  154.3 3.4 copy-start.4
  205.8 421.6 %collective-permute-start.8 = (bf16[8,32]{1,0:T(8,128)(2,1)S(1)}, bf16[8,32]{1,0:T(8,128)(2,1)S(1)}, u32[]{:S(2)}, u32[]{:S(2)}) collective-permute-start(bf16[8,32]{1,0:T(8,128)(2,1)S(1)} %get-tuple-element.286), channel_id=1, source_target_pairs={{0,16},{16,32},{32,48},{48,64},{64,80},{80,96},{96,112},{1,17},{17... | collective-permute-start | bytes 1544 | tf_op jit(solution)/shard_map/ppermute | solution.py:21
  256.1 371.3 %collective-permute-start.9 = (bf16[8,32]{1,0:T(8,128)(2,1)S(1)}, bf16[8,32]{1,0:T(8,128)(2,1)S(1)}, u32[]{:S(2)}, u32[]{:S(2)}) collective-permute-start(bf16[8,32]{1,0:T(8,128)(2,1)S(1)} %get-tuple-element.287), channel_id=1, source_target_pairs={{16,0},{32,16},{48,32},{64,48},{80,64},{96,80},{112,96},{17,1},{33... | collective-permute-start | bytes 1544 | tf_op jit(solution)/shard_map/ppermute | solution.py:22
  424.0 242.8 %all-to-all-start.1 = ((bf16[128,1,32,128]{3,2,1,0:T(8,128)(2,1)}), bf16[128,1,32,128]{3,2,1,0:T(8,128)(2,1)}, u32[]{:S(2)}, u32[]{:S(2)}) async-start(bf16[128,1,32,128]{3,2,1,0:T(8,128)(2,1)} %bitcast.114), calls=%async_computation.1 | async-start | bytes 2097152 | tf_op jit(solution)/shard_map/all_to_all | solution.py:68
  623.9 9.3 %slice-start = ((s8[6291456]{0:T(1024)(128)(4,1)}), s8[4194304]{0:T(1024)(128)(4,1)S(1)}, s32[]{:S(2)}) async-start(s8[6291456]{0:T(1024)(128)(4,1)} %bitcast.104), calls=%async_computation.2 | async-start | bytes 8388608
  623.9 9.3 %slice-start.1 = ((s8[6291456]{0:T(1024)(128)(4,1)}), s8[2097152]{0:T(1024)(128)(4,1)S(1)}, s32[]{:S(2)}) async-start(s8[6291456]{0:T(1024)(128)(4,1)} %bitcast.104), calls=%async_computation.3 | async-start | bytes 4194304
  627.5 13.7 %collective-permute-start.10 = (bf16[32,8]{1,0:T(8,128)(2,1)S(1)}, bf16[32,8]{1,0:T(8,128)(2,1)S(1)}, u32[]{:S(2)}, u32[]{:S(2)}) collective-permute-start(bf16[32,8]{1,0:T(8,128)(2,1)S(1)} %get-tuple-element.288), channel_id=1, source_target_pairs={{0,1},{1,2},{2,3},{3,4},{4,5},{5,6},{6,7},{7,8},{8,9},{9,10},{10,1... | collective-permute-start | bytes 1544 | tf_op jit(solution)/shard_map/ppermute | solution.py:21
  631.1 10.2 %collective-permute-start.11 = (bf16[32,8]{1,0:T(8,128)(2,1)S(1)}, bf16[32,8]{1,0:T(8,128)(2,1)S(1)}, u32[]{:S(2)}, u32[]{:S(2)}) collective-permute-start(bf16[32,8]{1,0:T(8,128)(2,1)S(1)} %get-tuple-element.289), channel_id=1, source_target_pairs={{1,0},{2,1},{3,2},{4,3},{5,4},{6,5},{7,6},{8,7},{9,8},{10,9},{11,1... | collective-permute-start | bytes 1544 | tf_op jit(solution)/shard_map/ppermute | solution.py:22
  635.6 9.7 %collective-permute-start.4 = (bf16[8,32,1024]{2,1,0:T(8,128)(2,1)S(1)}, bf16[8,32,1024]{2,1,0:T(8,128)(2,1)}, u32[]{:S(2)}, u32[]{:S(2)}) collective-permute-start(bf16[8,32,1024]{2,1,0:T(8,128)(2,1)S(1)} %get-tuple-element.278), channel_id=1, source_target_pairs={{0,16},{16,32},{32,48},{48,64},{64,80},{80,96},{96,112},{1,17},{17... | collective-permute-start | bytes 1572872 | tf_op jit(solution)/shard_map/ppermute | solution.py:21
  639.3 10.8 %collective-permute-start.5 = (bf16[8,32,1024]{2,1,0:T(8,128)(2,1)}, bf16[8,32,1024]{2,1,0:T(8,128)(2,1)}, u32[]{:S(2)}, u32[]{:S(2)}) collective-permute-start(bf16[8,32,1024]{2,1,0:T(8,128)(2,1)} %get-tuple-element.279), channel_id=1, source_target_pairs={{16,0},{32,16},{48,32},{64,48},{80,64},{96,80},{112,96},{17,1},{33... | collective-permute-start | bytes 1572872 | tf_op jit(solution)/shard_map/ppermute | solution.py:22
  655.1 10.2 %copy-start.1 = (f32[32,32,1024]{2,1,0:T(8,128)S(1)}, f32[32,32,1024]{2,1,0:T(8,128)}, u32[]{:S(2)}) copy-start(f32[32,32,1024]{2,1,0:T(8,128)} %fusion.45) | copy-start | bytes 12582916
  658.7 14.3 %collective-permute-start.6 = (bf16[32,8,1024]{2,1,0:T(8,128)(2,1)S(1)}, bf16[32,8,1024]{2,1,0:T(8,128)(2,1)}, u32[]{:S(2)}, u32[]{:S(2)}) collective-permute-start(bf16[32,8,1024]{2,1,0:T(8,128)(2,1)S(1)} %get-tuple-element.284), channel_id=1, source_target_pairs={{0,1},{1,2},{2,3},{3,4},{4,5},{5,6},{6,7},{7,8},{8,9},{9,10},{10,1... | collective-permute-start | bytes 1572872 | tf_op jit(solution)/shard_map/ppermute | solution.py:21
  663.8 10.2 %collective-permute-start.7 = (bf16[32,8,1024]{2,1,0:T(8,128)(2,1)}, bf16[32,8,1024]{2,1,0:T(8,128)(2,1)}, u32[]{:S(2)}, u32[]{:S(2)}) collective-permute-start(bf16[32,8,1024]{2,1,0:T(8,128)(2,1)} %get-tuple-element.285), channel_id=1, source_target_pairs={{1,0},{2,1},{3,2},{4,3},{5,4},{6,5},{7,6},{8,7},{9,8},{10,9},{11,1... | collective-permute-start | bytes 1572872 | tf_op jit(solution)/shard_map/ppermute | solution.py:22
  674.0 5.3 copy-start.10
  (4 other events, 11.2 us)
where the time goes:
time: 695 us; the launch traced here: 684 us
  starting transfers between devices  293 us (42%)
  matrix products  170 us (24%)
  local copies, waits for them, and re-layouts  131 us (19%)
  waiting for transfers between devices  46 us (7%)
  other arithmetic  40.4 us (6%)
    all_to_all x1, starting transfers between devices, send_back(): lax.all_to_all(pieces.reshape(device_count, 1, row_count, last_dim), ('ro...  200 us
    sub x8, matrix products, softmax_mix(): expsum = jnp.exp(scores - highest)  79.9 us
    dot_general x9, matrix products, softmax_mix(): jnp.einsum('hqk,khd->qhd', weights_bf, values, preferred_element_type=jnp...  76.6 us
    ppermute x6, starting transfers between devices, padded(): before = lax.ppermute(last, axis, up)  70.5 us
    all_to_all x1, waiting for transfers between devices, send_out(): lax.all_to_all(pieces.reshape(device_count, 1, row_count, last_dim), ('ro...  27.3 us
    while x4, local copies, waits for them, and re-layouts, lattice_attend(): return lax.map(one_block, grouped).reshape(row_count, head_count * head_dim)  22.8 us
  transfers between devices with their start and end apart: 14, of which 6 were waited for; matrix products, arithmetic and copies ran while one was open for 39% of the time, Pallas kernels for 0%

commit v1 on v0

v1 whole, which is shorter than its diff:
```python
import functools
import math

import jax
import jax.numpy as jnp
from jax import lax
from jax.experimental import pallas as pl
from jax.experimental.pallas import tpu as pltpu
from jax.sharding import PartitionSpec as P

HD = 64
STRIDE = 4
WIN = 16
HALO = 8
SUBS = STRIDE * STRIDE
LANES = 128
SCALE = HD**-0.5 * math.log2(math.e)
FREE_RANGE = 100.0
VROWS = 80
QBLOCK = 1024
KBLOCK = 256
BF16 = jnp.bfloat16
F32 = jnp.float32
VMEM_LIMIT = 58 * 2**20


def dot(a, b):
    return jnp.dot(a, b, preferred_element_type=F32)


def dot_nt(a, b):
    return lax.dot_general(a, b, (((1,), (1,)), ((), ())), preferred_element_type=F32)


def whole(shape):
    return pl.BlockSpec(shape, lambda *_: (0,) * len(shape))


def lattice_order(count, by_row):
    lattice = lax.broadcasted_iota(jnp.int32, (count, count), 0 if by_row else 1)
    cell = lax.broadcasted_iota(jnp.int32, (count, count), 1 if by_row else 0)
    per_sub = count // SUBS
    tile_cols = 16
    sub, place = lattice // per_sub, lattice % per_sub
    across = tile_cols // STRIDE
    row = (place // across) * STRIDE + sub // STRIDE
    col = (place % across) * STRIDE + sub % STRIDE
    return jnp.where(cell == row * tile_cols + col, 1.0, 0.0).astype(BF16)


def project_kernel(x_ref, wq_ref, wk_ref, wv_ref, out_ref, ordered):
    count = x_ref.shape[0]

    @pl.when(pl.program_id(0) == 0)
    def _():
        ordered[...] = dot(lattice_order(count, True), x_ref[...]).astype(BF16)

    x = ordered[...]
    for part, w_ref in enumerate((wq_ref, wk_ref, wv_ref)):
        y = dot(x, w_ref[...]).astype(BF16)
        for g in range(2):
            out_ref[:, g, :, part * LANES : (part + 1) * LANES] = y[
                :, g * LANES : (g + 1) * LANES
            ].reshape(SUBS, count // SUBS, LANES)


def project(x, w_query, w_keyval):
    count, channels = x.shape
    inner = w_query.shape[1]
    groups = inner // LANES
    steps = groups // 2
    per_sub = count // SUBS
    return pl.pallas_call(
        project_kernel,
        grid=(steps,),
        in_specs=[
            whole(x.shape),
            pl.BlockSpec((channels, 2 * LANES), lambda g: (0, g)),
            pl.BlockSpec((channels, 2 * LANES), lambda g: (0, g)),
            pl.BlockSpec((channels, 2 * LANES), lambda g: (0, g + steps)),
        ],
        out_specs=pl.BlockSpec((SUBS, 2, per_sub, 3 * LANES), lambda g: (0, g, 0, 0)),
        out_shape=jax.ShapeDtypeStruct((SUBS, groups, per_sub, 3 * LANES), BF16),
        scratch_shapes=[pltpu.VMEM((count, channels), BF16)],
        compiler_params=pltpu.CompilerParams(vmem_limit_bytes=VMEM_LIMIT),
        cost_estimate=pl.CostEstimate(
            flops=2 * count * channels * 3 * inner,
            bytes_accessed=2 * (3 * channels * inner + count * channels + 3 * count * inner),
            transcendentals=0,
        ),
        name="project",
    )(x, w_query, w_keyval, w_keyval)


def lattice_kernel(x_ref, o_ref, keys, queries_t, values_t, free):
    count = x_ref.shape[0]
    step = pl.program_id(0)
    block = o_ref.shape[0]

    @pl.when(step == 0)
    def _():
        q_t = x_ref[:, 0:LANES].astype(F32).T
        k_all = x_ref[:, LANES : 2 * LANES].astype(F32)
        v_t = x_ref[:, 2 * LANES : 3 * LANES].astype(F32).T.astype(BF16)
        worst = jnp.float32(0)
        for h in range(2):
            head = slice(h * HD, (h + 1) * HD)
            q, k = q_t[head, :], k_all[:, head]
            bound = jnp.max(jnp.sum(q * q, axis=0)) * jnp.max(jnp.sum(k * k, axis=1))
            worst = jnp.maximum(worst, bound)
            queries_t[h] = q.astype(BF16)
            keys[h] = k.astype(BF16)
            values_t[h, 0:HD] = v_t[head, :]
            values_t[h, HD:VROWS] = jnp.ones((VROWS - HD, count), BF16)
        free[0] = (worst * (SCALE * SCALE) <= FREE_RANGE * FREE_RANGE).astype(jnp.int32)

    cols = pl.ds(pl.multiple_of(step * block, block), block)

    def finish(sums):
        out = jnp.concatenate([s[:HD] / s[HD : HD + 1] for s in sums], 0)
        o_ref[...] = out.T.astype(BF16)

    @pl.when(free[0] == 1)
    def _():
        items = [(h, c) for h in range(2) for c in range(0, count, KBLOCK)]

        def score(i):
            h, c = items[i]
            return dot(keys[h, c : c + KBLOCK, :], queries_t[h, :, cols])

        sums = [None, None]
        later = score(0)
        for i, (h, c) in enumerate(items):
            now = later
            if i + 1 < len(items):
                later = score(i + 1)
            weights = jnp.exp2(now * SCALE).astype(BF16)
            part = dot(values_t[h, :, c : c + KBLOCK], weights)
            sums[h] = part if sums[h] is None else sums[h] + part
        finish(sums)

    @pl.when(free[0] == 0)
    def _():
        chunks = count // KBLOCK
        sums = []
        for h in range(2):
            q = queries_t[h, :, cols]

            def score(c, h=h, q=q):
                return dot(keys[h, pl.ds(pl.multiple_of(c * KBLOCK, KBLOCK), KBLOCK), :], q)

            def top(c, m, score=score):
                return jnp.maximum(m, jnp.max(score(c), axis=0, keepdims=True))

            m = lax.fori_loop(0, chunks, top, jnp.full((1, block), -jnp.inf, F32))

            def add(c, total, score=score, m=m, h=h):
                weights = jnp.exp2((score(c) - m) * SCALE).astype(BF16)
                rows = pl.ds(pl.multiple_of(c * KBLOCK, KBLOCK), KBLOCK)
                return total + dot(values_t[h, :, rows], weights)

            sums.append(lax.fori_loop(0, chunks, add, jnp.zeros((VROWS, block), F32)))
        finish(sums)


def lattice_attend(x):
    count = x.shape[0]
    return pl.pallas_call(
        lattice_kernel,
        grid=(count // QBLOCK,),
        in_specs=[whole(x.shape)],
        out_specs=pl.BlockSpec((QBLOCK, LANES), lambda i: (i, 0)),
        out_shape=jax.ShapeDtypeStruct((count, LANES), BF16),
        scratch_shapes=[
            pltpu.VMEM((2, count, HD), BF16),
            pltpu.VMEM((2, HD, count), BF16),
            pltpu.VMEM((2, VROWS, count), BF16),
            pltpu.SMEM((1,), jnp.int32),
        ],
        compiler_params=pltpu.CompilerParams(vmem_limit_bytes=VMEM_LIMIT),
        cost_estimate=pl.CostEstimate(
            flops=8 * 4 * count * count * HD,
            bytes_accessed=8 * count * LANES,
            transcendentals=2 * count * count,
        ),
        name="lattice_attend",
    )(x)


def windows_kernel(
    anchor, weight, mid_ref, side_ref, wq_ref, wkv_ref, top_out, bottom_out, mid_out, side_out,
    mid_sum, side_sum, results,
):
    inner = wq_ref.shape[1]
    channels = wq_ref.shape[0]
    cells = WIN * WIN
    wide = inner + LANES
    tile_rows = mid_out.shape[0]
    mid_sum[...] = jnp.zeros(mid_sum.shape, F32)
    side_sum[...] = jnp.zeros(side_sum.shape, F32)
    results[:, inner:wide] = jnp.ones((cells, LANES), BF16)
    slots = weight.shape[0]
    live = sum((weight[s] > 0).astype(jnp.int32) for s in range(slots))
    first = lax.broadcasted_iota(jnp.int32, (cells, LANES), 1) < HD
    ones = jnp.ones((cells, LANES), BF16)

    def one_hot(window_dim, left, offset):
        window = lax.broadcasted_iota(jnp.int32, (cells, cells), window_dim)
        source = lax.broadcasted_iota(jnp.int32, (cells, cells), 1 - window_dim)
        place = ((window & (WIN - 1)) + left) & (2 * WIN - 1)
        same = ((window >> 4) == (source >> 4)) & (place == (source & (WIN - 1)) + offset)
        return jnp.where(same, 1.0, 0.0)

    def one_window(slot, carry):
        top = anchor[slot, 0] + HALO
        left = anchor[slot, 1]
        factor = weight[slot].astype(F32)
        rows = pl.ds(top, WIN)
        mid = mid_ref[rows].reshape(cells, channels)
        side = side_ref[rows].reshape(cells, channels)
        x = dot(one_hot(0, left, 0).astype(BF16), mid) + dot(one_hot(0, left, WIN).astype(BF16), side)
        x = x.astype(BF16)
        for g in range(0, inner, 2 * LANES):
            q2 = dot(x, wq_ref[:, g : g + 2 * LANES]).astype(BF16)
            k2 = dot(x, wkv_ref[:, g : g + 2 * LANES]).astype(BF16)
            v2 = dot(x, wkv_ref[:, inner + g : inner + g + 2 * LANES]).astype(BF16)
            for pair in range(2):
                lanes = slice(pair * LANES, (pair + 1) * LANES)
                q, k, v = q2[:, lanes], k2[:, lanes], v2[:, lanes]
                v = jnp.concatenate([v, ones], 1)
                mixed = []
                for h in range(2):
                    own = jnp.where(first if h == 0 else ~first, q, jnp.zeros_like(q))
                    s = dot_nt(own, k)
                    e = jnp.exp2((s - jnp.max(s, axis=1, keepdims=True)) * SCALE).astype(BF16)
                    o = dot(e, v)
                    mixed.append(o[:, :LANES] / o[:, LANES:])
                results[:, g + pair * LANES : g + (pair + 1) * LANES] = jnp.where(
                    first, mixed[0], mixed[1]
                ).astype(BF16)
        r = results[...]
        to_mid = (one_hot(1, left, 0) * factor).astype(BF16)
        to_side = (one_hot(1, left, WIN) * factor).astype(BF16)
        mid_sum[rows] += dot(to_mid, r).reshape(WIN, WIN, wide)
        side_sum[rows] += dot(to_side, r).reshape(WIN, WIN, wide)
        return carry

    lax.fori_loop(0, live, one_window, 0)
    end = tile_rows + HALO
    top_out[:, 0:WIN] = mid_sum[0:HALO].astype(BF16)
    top_out[:, WIN : 2 * WIN] = side_sum[0:HALO].astype(BF16)
    bottom_out[:, 0:WIN] = mid_sum[end : end + HALO].astype(BF16)
    bottom_out[:, WIN : 2 * WIN] = side_sum[end : end + HALO].astype(BF16)
    mid_out[...] = mid_sum[HALO:end]
    side_out[...] = side_sum[HALO:end]


def windows(mid, side, w_query, w_keyval, anchor, weight):
    high, tile_cols, channels = mid.shape
    inner = w_query.shape[1]
    wide = inner + LANES
    tile_rows = high - 2 * HALO
    vmem = pl.BlockSpec(memory_space=pltpu.VMEM)
    smem = pl.BlockSpec(memory_space=pltpu.SMEM)
    rim = jax.ShapeDtypeStruct((HALO, 2 * WIN, wide), BF16)
    inside = jax.ShapeDtypeStruct((tile_rows, WIN, wide), F32)
    slots = weight.shape[0]
    cells = WIN * WIN
    return pl.pallas_call(
        windows_kernel,
        in_specs=[smem, smem, vmem, vmem, vmem, vmem],
        out_specs=[vmem] * 4,
        out_shape=[rim, rim, inside, inside],
        scratch_shapes=[
            pltpu.VMEM((high, WIN, wide), F32),
            pltpu.VMEM((high, WIN, wide), F32),
            pltpu.VMEM((cells, wide), BF16),
        ],
        compiler_params=pltpu.CompilerParams(vmem_limit_bytes=VMEM_LIMIT),
        cost_estimate=pl.CostEstimate(
            flops=slots * 2 * cells * 3 * inner * (channels + 2 * cells),
            bytes_accessed=6 * channels * inner + 4 * high * tile_cols * channels,
            transcendentals=slots * cells * cells * inner // HD,
        ),
        name="windows",
    )(anchor, weight, mid, side, w_query, w_keyval)


def blend_kernel(
    x_ref, known_ref, mask_ref, mixed_ref, mid_ref, above_ref, below_ref, beside_ref, w_ref, out_ref,
    blended,
):
    count = x_ref.shape[0]
    inner = blended.shape[1]
    wide = inner + LANES

    @pl.when(pl.program_id(0) == 0)
    def _():
        groups = mixed_ref.shape[1]
        tile_rows = mid_ref.shape[0]
        back = lattice_order(count, False)

        def total(lanes):
            upper = above_ref[:, 0:WIN, lanes].astype(F32)
            lower = below_ref[:, 0:WIN, lanes].astype(F32)
            middle = mid_ref[:, :, lanes] + beside_ref[:, :, lanes].astype(F32)
            parts = [
                middle[:HALO] + upper,
                middle[HALO : tile_rows - HALO],
                middle[tile_rows - HALO :] + lower,
            ]
            return jnp.concatenate(parts, 0).reshape(count, -1)

        share = 1.0 / (1.0 + total(slice(inner, wide)))
        share = jnp.concatenate([share, share], 1)
        for g in range(0, groups, 2):
            lanes = slice(g * LANES, (g + 2) * LANES)
            mixed = jnp.concatenate(
                [mixed_ref[:, g + j].reshape(count, LANES) for j in range(2)], 1
            )
            blended[:, lanes] = ((dot(back, mixed) + total(lanes)) * share).astype(BF16)

    width = out_ref.shape[1]
    y = (x_ref[...].astype(F32) + dot(blended[...], w_ref[...])).astype(BF16)
    mask = jnp.concatenate([mask_ref[...]] * (width // LANES), 1)
    out_ref[...] = jnp.where(mask == 1, known_ref[...], y)


def blend(x, known, mask, mixed, mid, above, below, beside, w_out):
    count, channels = x.shape
    inner = w_out.shape[0]
    width = 2 * LANES
    by_cols = pl.BlockSpec((count, width), lambda i: (0, i))
    return pl.pallas_call(
        blend_kernel,
        grid=(channels // width,),
        in_specs=[by_cols, by_cols]
        + [whole(a.shape) for a in (mask, mixed, mid, above, below, beside)]
        + [pl.BlockSpec((inner, width), lambda i: (0, i))],
        out_specs=by_cols,
        out_shape=jax.ShapeDtypeStruct((count, channels), BF16),
        scratch_shapes=[pltpu.VMEM((count, inner), BF16)],
        compiler_params=pltpu.CompilerParams(vmem_limit_bytes=VMEM_LIMIT),
        cost_estimate=pl.CostEstimate(
            flops=2 * count * inner * (channels + count),
            bytes_accessed=2 * inner * channels + 6 * count * channels,
            transcendentals=0,
        ),
        name="blend",
    )(x, known, mask, mixed, mid, above, below, beside, w_out)


def exchange(pieces):
    return lax.all_to_all(pieces, ("row", "col"), split_axis=0, concat_axis=0, tiled=True)


def neighbours(axis):
    peers = lax.axis_size(axis)
    onward = [(i, i + 1) for i in range(peers - 1)]
    return onward, [(j, i) for i, j in onward]


def on_device(features, known, known_mask, w_query, w_keyval, w_out, win_anchor, win_weight):
    tile_rows, tile_cols, channels = features.shape
    count = tile_rows * tile_cols
    per_sub = count // SUBS
    inner = w_query.shape[1]
    devices = lax.axis_size("row") * lax.axis_size("col")
    down, up = neighbours("row")
    right, left = neighbours("col")
    x = features.reshape(count, channels)

    before = lax.ppermute(features[tile_rows - HALO :], "row", down)
    after = lax.ppermute(features[:HALO], "row", up)
    pieces = project(x, w_query, w_keyval).reshape(devices, per_sub, 3 * LANES)
    mid = jnp.concatenate([before, features, after], 0)
    from_right = lax.ppermute(mid[:, :HALO], "col", left)
    from_left = lax.ppermute(mid[:, tile_cols - HALO :], "col", right)
    side = jnp.concatenate([from_right, from_left], 1)

    gathered = exchange(pieces).reshape(devices * per_sub, 3 * LANES)

    top, bottom, inside, beside = windows(
        mid, side, w_query, w_keyval, win_anchor.reshape(-1, 2), win_weight.reshape(-1)
    )
    above = lax.ppermute(bottom, "row", down)
    below = lax.ppermute(top, "row", up)
    beside = jnp.concatenate(
        [
            beside[:HALO] + above[:, WIN:].astype(F32),
            beside[HALO : tile_rows - HALO],
            beside[tile_rows - HALO :] + below[:, WIN:].astype(F32),
        ],
        0,
    ).astype(BF16)
    on_first = lax.ppermute(beside[:, :HALO], "col", right)
    on_last = lax.ppermute(beside[:, HALO:], "col", left)
    arrived = jnp.concatenate([on_first, on_last], 1)

    mixed = lattice_attend(gathered)
    returned = exchange(mixed.reshape(devices, per_sub, LANES))
    returned = returned.reshape(SUBS, devices // SUBS, per_sub, LANES)
    mask = jnp.broadcast_to(known_mask.reshape(count, 1), (count, LANES))
    out = blend(
        x, known.reshape(count, channels), mask, returned, inside, above, below, arrived, w_out
    )
    return out.reshape(tile_rows, tile_cols, channels)


def solution(mesh):
    in_specs = (
        P("row", "col", None),
        P("row", "col", None),
        P("row", "col"),
        P(),
        P(),
        P(),
        P("row", "col", None, None),
        P("row", "col", None),
    )
    out_specs = P("row", "col", None)
    return jax.shard_map(
        on_device, mesh=mesh, in_specs=in_specs, out_specs=out_specs, check_vma=False
    )
```

time: 695 us -> 279 us (0.40)
  starting transfers between devices: 293 us -> 62.2 us
  matrix products: 170 us -> 0 us
  Pallas kernels: 0 us -> 145 us
  local copies, waits for them, and re-layouts: 131 us -> 6.06 us
  other arithmetic: 40.4 us -> 5.47 us
  waiting for transfers between devices: 46 us -> 55 us
    all_to_all x2, starting transfers between devices: 210 us -> 40.1 us  [exchange(): lax.all_to_all(pieces, ('row', 'col'), split_axis=0, concat_axis=0, tiled...]
    pallas_call x0 -> x4, Pallas kernels: none -> 145 us  [the longest x1 100 us: lattice_attend(): pl.pallas_call(lattice_kernel, grid=(count // QBLOCK,), in_specs=[whole(x...]
    dot_general x13 -> x0, matrix products: 89.7 us -> none  [the longest x9 76.6 us: softmax_mix(): jnp.einsum('hqk,khd->qhd', weights_bf, values, preferred_element_type=jnp...]
    sub x8 -> x0, matrix products: 79.9 us -> none  [softmax_mix(): expsum = jnp.exp(scores - highest)]
    ppermute x12 -> x8, starting transfers between devices: 82.1 us -> 22.1 us  [the longest x1 5.13 us: on_device(): from_left = lax.ppermute(mid[:, tile_cols - HALO:], 'col', right)]
    another operation x5 -> x0, local copies, waits for them, and re-layouts: 36.5 us -> none  [the longest x1 11.8 us: on_device(): gathered = send_out(pieces).reshape(-1, 3, per_group, HD)]
    ppermute x12 -> x8, waiting for transfers between devices: 18.7 us -> 55 us  [the longest x1 22.3 us: on_device(): below = lax.ppermute(top, 'row', up)]
    while x9 -> x0, local copies, waits for them, and re-layouts: 30.3 us -> none  [the longest x4 22.8 us: lattice_attend(): return lax.map(one_block, grouped).reshape(row_count, head_count * head_dim)]
  transfers between devices with their start and end apart: 14 -> 10, of which waited for: 6 -> 6; matrix products, arithmetic and copies ran while one was open for 39% -> 3% of each run, Pallas kernels for 0% -> 13%
where the time goes in v1:
time: 279 us; the launch traced here: 273 us
  Pallas kernels  145 us (52%)
  starting transfers between devices  62.2 us (22%)
  waiting for transfers between devices  55 us (20%)
  local copies, waits for them, and re-layouts  6.06 us (2%)
  other arithmetic  5.47 us (2%)
    pallas_call x1, Pallas kernels, lattice_attend(): pl.pallas_call(lattice_kernel, grid=(count // QBLOCK,), in_specs=[whole(x...  100 us
    all_to_all x2, starting transfers between devices, exchange(): lax.all_to_all(pieces, ('row', 'col'), split_axis=0, concat_axis=0, tiled...  40.1 us
    pallas_call x1, Pallas kernels, windows(): pl.pallas_call(windows_kernel, in_specs=[smem, smem, vmem, vmem, vmem, vm...  26.4 us
    ppermute x1, waiting for transfers between devices, on_device(): below = lax.ppermute(top, 'row', up)  22.3 us
    ppermute x1, waiting for transfers between devices, on_device(): on_first = lax.ppermute(beside[:, :HALO], 'col', right)  20.1 us
    pallas_call x1, Pallas kernels, project(): pl.pallas_call(project_kernel, grid=(steps,), in_specs=[whole(x.shape), p...  9.55 us
    pallas_call x1, Pallas kernels, blend(): pl.pallas_call(blend_kernel, grid=(channels // width,), in_specs=[by_cols...  8.57 us
  transfers between devices with their start and end apart: 10, of which 6 were waited for; matrix products, arithmetic and copies ran while one was open for 3% of the time, Pallas kernels for 13%

profile of v1, /device:TPU:1, one launch (start us, length us, event | category | flops | bytes accessed | tf_op | source)
XLA Modules:
  0.0 273.5 jit_solution(15446223771514816276)
XLA Ops:
  0.0 1.2 fusion.1
  1.2 4.5 %collective-permute-start = (bf16[8,16,1280]{2,1,0:T(8,128)(2,1)S(1)}, bf16[8,16,1280]{2,1,0:T(8,128)(2,1)S(1)}, u32[]{:S(2)}, u32[]{:S(2)}) collective-permute-start(bf16[8,16,1280]{2,1,0:T(8,128)(2,1)S(1)} %get-tuple-element.18), channel_id=1, source_target_pairs={{0,16},{16,32},{32,48},{48,64},{64,80},{80,96},{96,112},{1,17},{17... | collective-permute-start | bytes 983048 | tf_op jit(solution)/shard_map/ppermute | solution.py:373
  5.7 1.9 collective-permute-start.1
  7.7 2.1 collective-permute-done
  9.9 4.3 %collective-permute-done.1 = bf16[8,16,1280]{2,1,0:T(8,128)(2,1)S(1)} collective-permute-done((bf16[8,16,1280]{2,1,0:T(8,128)(2,1)S(1)}, bf16[8,16,1280]{2,1,0:T(8,128)(2,1)S(1)}, u32[]{:S(2)}, u32[]{:S(2)}) %collective-permute-start.1) | collective-permute-done | bytes 327712 | tf_op jit(solution)/shard_map/ppermute | solution.py:374
  15.5 1.3 collective-permute-start.2
  16.8 5.1 %collective-permute-start.3 = (bf16[48,8,1280]{2,1,0:T(8,128)(2,1)S(1)}, bf16[48,8,1280]{2,1,0:T(8,128)(2,1)}, u32[]{:S(2)}, u32[]{:S(2)}) collective-permute-start(bf16[48,8,1280]{2,1,0:T(8,128)(2,1)S(1)} %get-tuple-element.16), channel_id=1, source_target_pairs={{0,1},{1,2},{2,3},{3,4},{4,5},{5,6},{6,7},{7,8},{8,9},{9,10},{10,1... | collective-permute-start | bytes 2949128 | tf_op jit(solution)/shard_map/ppermute | solution.py:378
  21.9 9.6 %project.1 = bf16[16,8,32,384]{3,2,1,0:T(8,128)(2,1)} custom-call(bf16[512,1280]{1,0:T(8,128)(2,1)} %bitcast.9, bf16[1280,1024]{1,0:T(8,128)(2,1)} %wq_ref.3, bf16[1280,2048]{1,0:T(8,128)(2,1)} %wkv_ref.1, bf16[1280,2048]{1,0:T(8,128)(2,1)} %wkv_ref.1), custom_call_target="tpu_custom_call" | custom-call | flops 4026531840 | bytes 12320768 | tf_op jit(solution)/shard_map/project/pallas_call | solution.py:73
  31.5 11.2 %all-to-all-start = ((bf16[128,32,384]{2,1,0:T(8,128)(2,1)}), bf16[128,32,384]{2,1,0:T(8,128)(2,1)}, u32[]{:S(2)}, u32[]{:S(2)}) async-start(bf16[128,32,384]{2,1,0:T(8,128)(2,1)} %bitcast.11), calls=%async_computation | async-start | bytes 6291456 | tf_op jit(solution)/shard_map/all_to_all | solution.py:354
  43.4 2.6 pad_maximum_fusion.side_ref
  46.0 26.4 %windows.1 = (bf16[8,32,1152]{2,1,0:T(8,128)(2,1)}, bf16[8,32,1152]{2,1,0:T(8,128)(2,1)}, f32[32,16,1152]{2,1,0:T(8,128)}, f32[32,16,1152]{2,1,0:T(8,128)}) custom-call(s32[6,2]{1,0:T(8,128)} %copy.11.anchor, s32[6]{0:T(128)} %bitcast.16, bf16[48,16,1280]{2,1,0:T(8,128)(2,1)} %copy-done.2, bf16[48,16,1280]{2,1,0:T(8,128)(2,1)} %pad_maximum_fusion.side_ref, ...), custom_call_target="tpu_custom_call" | custom-call | flops 16911433728 | bytes 11796480 | tf_op jit(solution)/shard_map/windows/pallas_call | solution.py:269
  72.5 1.9 collective-permute-start.4
  74.4 2.6 collective-permute-start.5
  77.0 1.3 slice.57
  78.3 4.0 %collective-permute-done.4.above_ref = bf16[8,32,1152]{2,1,0:T(8,128)(2,1)S(1)} collective-permute-done((bf16[8,32,1152]{2,1,0:T(8,128)(2,1)}, bf16[8,32,1152]{2,1,0:T(8,128)(2,1)S(1)}, u32[]{:S(2)}, u32[]{:S(2)}) %collective-permute-start.4) | collective-permute-done | bytes 589856 | tf_op jit(solution)/shard_map/ppermute | solution.py:386
  82.3 22.3 %collective-permute-done.5.below_ref = bf16[8,32,1152]{2,1,0:T(8,128)(2,1)S(1)} collective-permute-done((bf16[8,32,1152]{2,1,0:T(8,128)(2,1)}, bf16[8,32,1152]{2,1,0:T(8,128)(2,1)S(1)}, u32[]{:S(2)}, u32[]{:S(2)}) %collective-permute-start.5) | collective-permute-done | bytes 589856 | tf_op jit(solution)/shard_map/ppermute | solution.py:387
  104.6 1.6 add_convert_fusion.1
  106.4 100.0 %lattice_attend.1 = bf16[4096,128]{1,0:T(8,128)(2,1)} custom-call(bf16[4096,384]{1,0:T(8,128)(2,1)} %bitcast.3.x_ref), custom_call_target="tpu_custom_call" | custom-call | flops 34359738368 | bytes 4194304 | tf_op jit(solution)/shard_map/lattice_attend/pallas_call | solution.py:168
  206.4 28.9 %all-to-all-start.1 = ((bf16[128,32,128]{2,1,0:T(8,128)(2,1)}), bf16[128,32,128]{2,1,0:T(8,128)(2,1)S(1)}, u32[]{:S(2)}, u32[]{:S(2)}) async-start(bf16[128,32,128]{2,1,0:T(8,128)(2,1)} %bitcast.14), calls=%async_computation.1 | async-start | bytes 2097152 | tf_op jit(solution)/shard_map/all_to_all | solution.py:354
  235.4 3.4 %collective-permute-start.6 = (bf16[32,8,1152]{2,1,0:T(8,128)(2,1)S(1)}, bf16[32,8,1152]{2,1,0:T(8,128)(2,1)S(1)}, u32[]{:S(2)}, u32[]{:S(2)}) collective-permute-start(bf16[32,8,1152]{2,1,0:T(8,128)(2,1)S(1)} %get-tuple-element.19), channel_id=1, source_target_pairs={{0,1},{1,2},{2,3},{3,4},{4,5},{5,6},{6,7},{7,8},{8,9},{9,10},{10,1... | collective-permute-start | bytes 1769480 | tf_op jit(solution)/shard_map/ppermute | solution.py:396
  238.9 1.3 collective-permute-start.7
  240.4 20.1 %collective-permute-done.6 = bf16[32,8,1152]{2,1,0:T(8,128)(2,1)S(1)} collective-permute-done((bf16[32,8,1152]{2,1,0:T(8,128)(2,1)S(1)}, bf16[32,8,1152]{2,1,0:T(8,128)(2,1)S(1)}, u32[]{:S(2)}, u32[]{:S(2)}) %collective-permute-start.6) | collective-permute-done | bytes 589856 | tf_op jit(solution)/shard_map/ppermute | solution.py:396
  260.4 2.2 collective-permute-done.7
  264.9 8.6 %blend.1 = bf16[512,1280]{1,0:T(8,128)(2,1)} custom-call(bf16[512,1280]{1,0:T(8,128)(2,1)} %bitcast.10, bf16[512,1280]{1,0:T(8,128)(2,1)} %bitcast.13, s32[512,128]{1,0:T(8,128)} %broadcast_in_dim.8.mask_ref, bf16[16,8,32,128]{3,2,1,0:T(8,128)(2,1)} %bitcast.12, f32[32,16,1152]{2,1,0:T(8,128)} %get-tuple-element.9.mid_ref, bf16[8,32,1152]{2,1,0:T(8,128)(2,1)} %copy-done.3, ...), custom_call_target="tpu_custom_call" | custom-call | flops 1879048192 | bytes 6553600 | tf_op jit(solution)/shard_map/blend/pallas_call | solution.py:334
  (29 shorter events, 4.8 us)
Async XLA Ops:
  0.0 9.8 %copy-start = (bf16[32,16,1280]{2,1,0:T(8,128)(2,1)S(1)}, bf16[32,16,1280]{2,1,0:T(8,128)(2,1)}, u32[]{:S(2)}) copy-start(bf16[32,16,1280]{2,1,0:T(8,128)(2,1)} %param.8) | copy-start | bytes 3932164
  1.2 8.5 %collective-permute-start = (bf16[8,16,1280]{2,1,0:T(8,128)(2,1)S(1)}, bf16[8,16,1280]{2,1,0:T(8,128)(2,1)S(1)}, u32[]{:S(2)}, u32[]{:S(2)}) collective-permute-start(bf16[8,16,1280]{2,1,0:T(8,128)(2,1)S(1)} %get-tuple-element.18), channel_id=1, source_target_pairs={{0,16},{16,32},{32,48},{48,64},{64,80},{80,96},{96,112},{1,17},{17... | collective-permute-start | bytes 983048 | tf_op jit(solution)/shard_map/ppermute | solution.py:373
  5.7 8.4 %collective-permute-start.1 = (bf16[8,16,1280]{2,1,0:T(8,128)(2,1)S(1)}, bf16[8,16,1280]{2,1,0:T(8,128)(2,1)S(1)}, u32[]{:S(2)}, u32[]{:S(2)}) collective-permute-start(bf16[8,16,1280]{2,1,0:T(8,128)(2,1)S(1)} %get-tuple-element.17), channel_id=1, source_target_pairs={{16,0},{32,16},{48,32},{64,48},{80,64},{96,80},{112,96},{17,1},{33... | collective-permute-start | bytes 983048 | tf_op jit(solution)/shard_map/ppermute | solution.py:374
  14.2 1.4 copy-start.2
  15.5 27.9 %collective-permute-start.2 = (bf16[48,8,1280]{2,1,0:T(8,128)(2,1)S(1)}, bf16[48,8,1280]{2,1,0:T(8,128)(2,1)S(1)}, u32[]{:S(2)}, u32[]{:S(2)}) collective-permute-start(bf16[48,8,1280]{2,1,0:T(8,128)(2,1)S(1)} %get-tuple-element.15), channel_id=1, source_target_pairs={{1,0},{2,1},{3,2},{4,3},{5,4},{6,5},{7,6},{8,7},{9,8},{10,9},{11,1... | collective-permute-start | bytes 2949128 | tf_op jit(solution)/shard_map/ppermute | solution.py:377
  16.8 26.6 %collective-permute-start.3 = (bf16[48,8,1280]{2,1,0:T(8,128)(2,1)S(1)}, bf16[48,8,1280]{2,1,0:T(8,128)(2,1)}, u32[]{:S(2)}, u32[]{:S(2)}) collective-permute-start(bf16[48,8,1280]{2,1,0:T(8,128)(2,1)S(1)} %get-tuple-element.16), channel_id=1, source_target_pairs={{0,1},{1,2},{2,3},{3,4},{4,5},{5,6},{6,7},{7,8},{8,9},{9,10},{10,1... | collective-permute-start | bytes 2949128 | tf_op jit(solution)/shard_map/ppermute | solution.py:378
  31.5 11.2 %copy-start.6 = (s32[1,1,6,2]{2,3,1,0:T(2,128)S(1)}, s32[1,1,6,2]{2,3,1,0:T(2,128)}, u32[]{:S(2)}) copy-start(s32[1,1,6,2]{2,3,1,0:T(2,128)} %param.14) | copy-start | bytes 148
  31.5 74.9 %all-to-all-start = ((bf16[128,32,384]{2,1,0:T(8,128)(2,1)}), bf16[128,32,384]{2,1,0:T(8,128)(2,1)}, u32[]{:S(2)}, u32[]{:S(2)}) async-start(bf16[128,32,384]{2,1,0:T(8,128)(2,1)} %bitcast.11), calls=%async_computation | async-start | bytes 6291456 | tf_op jit(solution)/shard_map/all_to_all | solution.py:354
  72.5 9.8 %collective-permute-start.4 = (bf16[8,32,1152]{2,1,0:T(8,128)(2,1)}, bf16[8,32,1152]{2,1,0:T(8,128)(2,1)S(1)}, u32[]{:S(2)}, u32[]{:S(2)}) collective-permute-start(bf16[8,32,1152]{2,1,0:T(8,128)(2,1)} %get-tuple-element.10), channel_id=1, source_target_pairs={{0,16},{16,32},{32,48},{48,64},{64,80},{80,96},{96,112},{1,17},{17... | collective-permute-start | bytes 1769480 | tf_op jit(solution)/shard_map/ppermute | solution.py:386
  74.4 30.3 %collective-permute-start.5 = (bf16[8,32,1152]{2,1,0:T(8,128)(2,1)}, bf16[8,32,1152]{2,1,0:T(8,128)(2,1)S(1)}, u32[]{:S(2)}, u32[]{:S(2)}) collective-permute-start(bf16[8,32,1152]{2,1,0:T(8,128)(2,1)} %get-tuple-element.11), channel_id=1, source_target_pairs={{16,0},{32,16},{48,32},{64,48},{80,64},{96,80},{112,96},{17,1},{33... | collective-permute-start | bytes 1769480 | tf_op jit(solution)/shard_map/ppermute | solution.py:387
  82.3 24.1 %copy-start.3 = (bf16[8,32,1152]{2,1,0:T(8,128)(2,1)}, bf16[8,32,1152]{2,1,0:T(8,128)(2,1)S(1)}, u32[]{:S(2)}) copy-start(bf16[8,32,1152]{2,1,0:T(8,128)(2,1)S(1)} %collective-permute-done.4.above_ref) | copy-start | bytes 1769476
  104.6 1.8 copy-start.4
  206.4 33.8 %copy-start.5 = (s32[32,16]{0,1:T(8,128)S(1)}, s32[32,16]{0,1:T(8,128)}, u32[]{:S(2)}) copy-start(s32[32,16]{0,1:T(8,128)} %param.10) | copy-start | bytes 6148
  206.4 57.4 %all-to-all-start.1 = ((bf16[128,32,128]{2,1,0:T(8,128)(2,1)}), bf16[128,32,128]{2,1,0:T(8,128)(2,1)S(1)}, u32[]{:S(2)}, u32[]{:S(2)}) async-start(bf16[128,32,128]{2,1,0:T(8,128)(2,1)} %bitcast.14), calls=%async_computation.1 | async-start | bytes 2097152 | tf_op jit(solution)/shard_map/all_to_all | solution.py:354
  235.4 25.0 %collective-permute-start.6 = (bf16[32,8,1152]{2,1,0:T(8,128)(2,1)S(1)}, bf16[32,8,1152]{2,1,0:T(8,128)(2,1)S(1)}, u32[]{:S(2)}, u32[]{:S(2)}) collective-permute-start(bf16[32,8,1152]{2,1,0:T(8,128)(2,1)S(1)} %get-tuple-element.19), channel_id=1, source_target_pairs={{0,1},{1,2},{2,3},{3,4},{4,5},{5,6},{6,7},{7,8},{8,9},{9,10},{10,1... | collective-permute-start | bytes 1769480 | tf_op jit(solution)/shard_map/ppermute | solution.py:396
  238.9 23.8 %collective-permute-start.7 = (bf16[32,8,1152]{2,1,0:T(8,128)(2,1)S(1)}, bf16[32,8,1152]{2,1,0:T(8,128)(2,1)S(1)}, u32[]{:S(2)}, u32[]{:S(2)}) collective-permute-start(bf16[32,8,1152]{2,1,0:T(8,128)(2,1)S(1)} %get-tuple-element.20), channel_id=1, source_target_pairs={{1,0},{2,1},{3,2},{4,3},{5,4},{6,5},{7,6},{8,7},{9,8},{10,9},{11,1... | collective-permute-start | bytes 1769480 | tf_op jit(solution)/shard_map/ppermute | solution.py:397
  263.8 1.1 copy-start.1

commit v2 on v1

--- a/solution.py
+++ b/solution.py
@@ -21,7 +21,6 @@
 KBLOCK = 256
 BF16 = jnp.bfloat16
 F32 = jnp.float32
-VMEM_LIMIT = 58 * 2**20
 
 
 def dot(a, b):
@@ -33,7 +32,10 @@
 
 
 def whole(shape):
-    return pl.BlockSpec(shape, lambda *_: (0,) * len(shape))
+    return pl.BlockSpec(shape, lambda *_: (0,) * len(shape), pipeline_mode=pl.Buffered(1))
+
+
+PARAMS = pltpu.CompilerParams(vmem_limit_bytes=58 * 2**20)
 
 
 def lattice_order(count, by_row):
@@ -82,7 +84,7 @@
         out_specs=pl.BlockSpec((SUBS, 2, per_sub, 3 * LANES), lambda g: (0, g, 0, 0)),
         out_shape=jax.ShapeDtypeStruct((SUBS, groups, per_sub, 3 * LANES), BF16),
         scratch_shapes=[pltpu.VMEM((count, channels), BF16)],
-        compiler_params=pltpu.CompilerParams(vmem_limit_bytes=VMEM_LIMIT),
+        compiler_params=PARAMS,
         cost_estimate=pl.CostEstimate(
             flops=2 * count * channels * 3 * inner,
             bytes_accessed=2 * (3 * channels * inner + count * channels + 3 * count * inner),
@@ -177,7 +179,7 @@
             pltpu.VMEM((2, VROWS, count), BF16),
             pltpu.SMEM((1,), jnp.int32),
         ],
-        compiler_params=pltpu.CompilerParams(vmem_limit_bytes=VMEM_LIMIT),
+        compiler_params=PARAMS,
         cost_estimate=pl.CostEstimate(
             flops=8 * 4 * count * count * HD,
             bytes_accessed=8 * count * LANES,
@@ -188,27 +190,33 @@
 
 
 def windows_kernel(
-    anchor, weight, mid_ref, side_ref, wq_ref, wkv_ref, top_out, bottom_out, mid_out, side_out,
-    mid_sum, side_sum, results,
+    anchor, weight, before_ref, ext_ref, after_ref, wq_ref, wkv_ref, top_out, bottom_out, mid_out,
+    side_out, held, mid_sum, side_sum, results_t,
 ):
     inner = wq_ref.shape[1]
     channels = wq_ref.shape[0]
     cells = WIN * WIN
     wide = inner + LANES
     tile_rows = mid_out.shape[0]
+    end = tile_rows + HALO
+    held[0:HALO] = before_ref[...]
+    held[HALO:end] = ext_ref[...]
+    held[end:] = after_ref[...]
     mid_sum[...] = jnp.zeros(mid_sum.shape, F32)
     side_sum[...] = jnp.zeros(side_sum.shape, F32)
-    results[:, inner:wide] = jnp.ones((cells, LANES), BF16)
+    results_t[inner:wide] = jnp.ones((LANES, cells), BF16)
     slots = weight.shape[0]
     live = sum((weight[s] > 0).astype(jnp.int32) for s in range(slots))
     first = lax.broadcasted_iota(jnp.int32, (cells, LANES), 1) < HD
-    ones = jnp.ones((cells, LANES), BF16)
-
-    def one_hot(window_dim, left, offset):
-        window = lax.broadcasted_iota(jnp.int32, (cells, cells), window_dim)
-        source = lax.broadcasted_iota(jnp.int32, (cells, cells), 1 - window_dim)
+    ones = jnp.ones((VROWS - HD, cells), BF16)
+
+    def one_hot(window_dim, left):
+        shape = (cells, 2 * cells) if window_dim == 0 else (2 * cells, cells)
+        window = lax.broadcasted_iota(jnp.int32, shape, window_dim)
+        source = lax.broadcasted_iota(jnp.int32, shape, 1 - window_dim)
         place = ((window & (WIN - 1)) + left) & (2 * WIN - 1)
-        same = ((window >> 4) == (source >> 4)) & (place == (source & (WIN - 1)) + offset)
+        held = (source & (WIN - 1)) + ((source >> 8) << 4)
+        same = (((window ^ source) & (cells - WIN)) == 0) & (place == held)
         return jnp.where(same, 1.0, 0.0)
 
     def one_window(slot, carry):
@@ -216,37 +224,46 @@
         left = anchor[slot, 1]
         factor = weight[slot].astype(F32)
         rows = pl.ds(top, WIN)
-        mid = mid_ref[rows].reshape(cells, channels)
-        side = side_ref[rows].reshape(cells, channels)
-        x = dot(one_hot(0, left, 0).astype(BF16), mid) + dot(one_hot(0, left, WIN).astype(BF16), side)
-        x = x.astype(BF16)
+        source = jnp.concatenate(
+            [
+                held[rows, 0:WIN].reshape(cells, channels),
+                held[rows, WIN : 2 * WIN].reshape(cells, channels),
+            ],
+            0,
+        )
+        x = dot(one_hot(0, left).astype(BF16), source).astype(BF16)
+
+        def project(g):
+            q = dot(x, wq_ref[:, g : g + 2 * LANES]).astype(BF16)
+            k = dot(x, wkv_ref[:, g : g + 2 * LANES]).astype(BF16)
+            v = dot(x, wkv_ref[:, inner + g : inner + g + 2 * LANES])
+            return q, k, v.T.astype(BF16)
+
+        def scores(q, k, j):
+            lanes = slice(j // 2 * LANES, (j // 2 + 1) * LANES)
+            own = jnp.where(first if j % 2 == 0 else ~first, q[:, lanes], jnp.zeros((), BF16))
+            return dot_nt(k[:, lanes], own)
+
+        def mix(s, v_t, g, j):
+            e = jnp.exp2((s - jnp.max(s, axis=0, keepdims=True)) * SCALE).astype(BF16)
+            o = dot(jnp.concatenate([v_t[j * HD : (j + 1) * HD], ones], 0), e)
+            at = g + j * HD
+            results_t[at : at + HD] = (o[:HD] / o[HD : HD + 1]).astype(BF16)
+
+        later = project(0)
         for g in range(0, inner, 2 * LANES):
-            q2 = dot(x, wq_ref[:, g : g + 2 * LANES]).astype(BF16)
-            k2 = dot(x, wkv_ref[:, g : g + 2 * LANES]).astype(BF16)
-            v2 = dot(x, wkv_ref[:, inner + g : inner + g + 2 * LANES]).astype(BF16)
-            for pair in range(2):
-                lanes = slice(pair * LANES, (pair + 1) * LANES)
-                q, k, v = q2[:, lanes], k2[:, lanes], v2[:, lanes]
-                v = jnp.concatenate([v, ones], 1)
-                mixed = []
-                for h in range(2):
-                    own = jnp.where(first if h == 0 else ~first, q, jnp.zeros_like(q))
-                    s = dot_nt(own, k)
-                    e = jnp.exp2((s - jnp.max(s, axis=1, keepdims=True)) * SCALE).astype(BF16)
-                    o = dot(e, v)
-                    mixed.append(o[:, :LANES] / o[:, LANES:])
-                results[:, g + pair * LANES : g + (pair + 1) * LANES] = jnp.where(
-                    first, mixed[0], mixed[1]
-                ).astype(BF16)
-        r = results[...]
-        to_mid = (one_hot(1, left, 0) * factor).astype(BF16)
-        to_side = (one_hot(1, left, WIN) * factor).astype(BF16)
-        mid_sum[rows] += dot(to_mid, r).reshape(WIN, WIN, wide)
-        side_sum[rows] += dot(to_side, r).reshape(WIN, WIN, wide)
+            q, k, v_t = later
+            now = [scores(q, k, j) for j in range(4)]
+            if g + 2 * LANES < inner:
+                later = project(g + 2 * LANES)
+            for j in range(4):
+                mix(now[j], v_t, g, j)
+        placed = dot_nt((one_hot(1, left) * factor).astype(BF16), results_t[...])
+        mid_sum[rows] += placed[:cells].reshape(WIN, WIN, wide)
+        side_sum[rows] += placed[cells:].reshape(WIN, WIN, wide)
         return carry
 
     lax.fori_loop(0, live, one_window, 0)
-    end = tile_rows + HALO
     top_out[:, 0:WIN] = mid_sum[0:HALO].astype(BF16)
     top_out[:, WIN : 2 * WIN] = side_sum[0:HALO].astype(BF16)
     bottom_out[:, 0:WIN] = mid_sum[end : end + HALO].astype(BF16)
@@ -255,11 +272,11 @@
     side_out[...] = side_sum[HALO:end]
 
 
-def windows(mid, side, w_query, w_keyval, anchor, weight):
-    high, tile_cols, channels = mid.shape
+def windows(before, ext, after, w_query, w_keyval, anchor, weight):
+    tile_rows, _, channels = ext.shape
+    high = tile_rows + 2 * HALO
     inner = w_query.shape[1]
     wide = inner + LANES
-    tile_rows = high - 2 * HALO
     vmem = pl.BlockSpec(memory_space=pltpu.VMEM)
     smem = pl.BlockSpec(memory_space=pltpu.SMEM)
     rim = jax.ShapeDtypeStruct((HALO, 2 * WIN, wide), BF16)
@@ -268,57 +285,81 @@
     cells = WIN * WIN
     return pl.pallas_call(
         windows_kernel,
-        in_specs=[smem, smem, vmem, vmem, vmem, vmem],
+        in_specs=[smem, smem] + [vmem] * 5,
         out_specs=[vmem] * 4,
         out_shape=[rim, rim, inside, inside],
         scratch_shapes=[
+            pltpu.VMEM((high, 2 * WIN, channels), BF16),
             pltpu.VMEM((high, WIN, wide), F32),
             pltpu.VMEM((high, WIN, wide), F32),
-            pltpu.VMEM((cells, wide), BF16),
+            pltpu.VMEM((wide, cells), BF16),
         ],
-        compiler_params=pltpu.CompilerParams(vmem_limit_bytes=VMEM_LIMIT),
+        compiler_params=PARAMS,
         cost_estimate=pl.CostEstimate(
-            flops=slots * 2 * cells * 3 * inner * (channels + 2 * cells),
-            bytes_accessed=6 * channels * inner + 4 * high * tile_cols * channels,
+            flops=8 * slots * 2 * cells * 3 * inner * (channels + 2 * cells),
+            bytes_accessed=6 * channels * inner + 4 * high * WIN * channels,
             transcendentals=slots * cells * cells * inner // HD,
         ),
         name="windows",
-    )(anchor, weight, mid, side, w_query, w_keyval)
-
-
-def blend_kernel(
-    x_ref, known_ref, mask_ref, mixed_ref, mid_ref, above_ref, below_ref, beside_ref, w_ref, out_ref,
-    blended,
-):
+    )(anchor, weight, before, ext, after, w_query, w_keyval)
+
+
+def settle_kernel(mid_ref, above_ref, below_ref, beside_ref, sum_ref, share_ref):
+    count, inner = sum_ref.shape
+    tile_rows = mid_ref.shape[0]
+
+    def total(lanes):
+        upper = above_ref[:, 0:WIN, lanes].astype(F32)
+        lower = below_ref[:, 0:WIN, lanes].astype(F32)
+        middle = mid_ref[:, :, lanes] + beside_ref[:, :, lanes].astype(F32)
+        parts = [
+            middle[:HALO] + upper,
+            middle[HALO : tile_rows - HALO],
+            middle[tile_rows - HALO :] + lower,
+        ]
+        return jnp.concatenate(parts, 0).reshape(count, LANES)
+
+    share = 1.0 / (1.0 + total(slice(inner, inner + LANES)))
+    share_ref[...] = share
+    for g in range(0, inner, LANES):
+        lanes = slice(g, g + LANES)
+        sum_ref[:, lanes] = total(lanes) * share
+
+
+def settle(mid, above, below, beside):
+    tile_rows, tile_cols, wide = mid.shape
+    count = tile_rows * tile_cols
+    vmem = pl.BlockSpec(memory_space=pltpu.VMEM)
+    return pl.pallas_call(
+        settle_kernel,
+        in_specs=[vmem] * 4,
+        out_specs=[vmem] * 2,
+        out_shape=[
+            jax.ShapeDtypeStruct((count, wide - LANES), F32),
+            jax.ShapeDtypeStruct((count, LANES), F32),
+        ],
+        compiler_params=PARAMS,
+        cost_estimate=pl.CostEstimate(
+            flops=4 * count * wide, bytes_accessed=12 * count * wide, transcendentals=0
+        ),
+        name="settle",
+    )(mid, above, below, beside)
+
+
+def blend_kernel(x_ref, known_ref, mask_ref, mixed_ref, sum_ref, share_ref, w_ref, out_ref, blended):
     count = x_ref.shape[0]
-    inner = blended.shape[1]
-    wide = inner + LANES
 
     @pl.when(pl.program_id(0) == 0)
     def _():
         groups = mixed_ref.shape[1]
-        tile_rows = mid_ref.shape[0]
         back = lattice_order(count, False)
-
-        def total(lanes):
-            upper = above_ref[:, 0:WIN, lanes].astype(F32)
-            lower = below_ref[:, 0:WIN, lanes].astype(F32)
-            middle = mid_ref[:, :, lanes] + beside_ref[:, :, lanes].astype(F32)
-            parts = [
-                middle[:HALO] + upper,
-                middle[HALO : tile_rows - HALO],
-                middle[tile_rows - HALO :] + lower,
-            ]
-            return jnp.concatenate(parts, 0).reshape(count, -1)
-
-        share = 1.0 / (1.0 + total(slice(inner, wide)))
-        share = jnp.concatenate([share, share], 1)
+        share = jnp.concatenate([share_ref[...]] * 2, 1)
         for g in range(0, groups, 2):
             lanes = slice(g * LANES, (g + 2) * LANES)
             mixed = jnp.concatenate(
                 [mixed_ref[:, g + j].reshape(count, LANES) for j in range(2)], 1
             )
-            blended[:, lanes] = ((dot(back, mixed) + total(lanes)) * share).astype(BF16)
+            blended[:, lanes] = (dot(back, mixed) * share + sum_ref[:, lanes]).astype(BF16)
 
     width = out_ref.shape[1]
     y = (x_ref[...].astype(F32) + dot(blended[...], w_ref[...])).astype(BF16)
@@ -326,7 +367,7 @@
     out_ref[...] = jnp.where(mask == 1, known_ref[...], y)
 
 
-def blend(x, known, mask, mixed, mid, above, below, beside, w_out):
+def blend(x, known, mask, mixed, windowed, share, w_out):
     count, channels = x.shape
     inner = w_out.shape[0]
     width = 2 * LANES
@@ -335,19 +376,19 @@
         blend_kernel,
         grid=(channels // width,),
         in_specs=[by_cols, by_cols]
-        + [whole(a.shape) for a in (mask, mixed, mid, above, below, beside)]
+        + [whole(a.shape) for a in (mask, mixed, windowed, share)]
         + [pl.BlockSpec((inner, width), lambda i: (0, i))],
         out_specs=by_cols,
         out_shape=jax.ShapeDtypeStruct((count, channels), BF16),
         scratch_shapes=[pltpu.VMEM((count, inner), BF16)],
-        compiler_params=pltpu.CompilerParams(vmem_limit_bytes=VMEM_LIMIT),
+        compiler_params=PARAMS,
         cost_estimate=pl.CostEstimate(
             flops=2 * count * inner * (channels + count),
             bytes_accessed=2 * inner * channels + 6 * count * channels,
             transcendentals=0,
         ),
         name="blend",
-    )(x, known, mask, mixed, mid, above, below, beside, w_out)
+    )(x, known, mask, mixed, windowed, share, w_out)
 
 
 def exchange(pieces):
@@ -370,18 +411,22 @@
     right, left = neighbours("col")
     x = features.reshape(count, channels)
 
-    before = lax.ppermute(features[tile_rows - HALO :], "row", down)
-    after = lax.ppermute(features[:HALO], "row", up)
+    from_right = lax.ppermute(features[:, :HALO], "col", left)
+    from_left = lax.ppermute(features[:, tile_cols - HALO :], "col", right)
     pieces = project(x, w_query, w_keyval).reshape(devices, per_sub, 3 * LANES)
-    mid = jnp.concatenate([before, features, after], 0)
-    from_right = lax.ppermute(mid[:, :HALO], "col", left)
-    from_left = lax.ppermute(mid[:, tile_cols - HALO :], "col", right)
-    side = jnp.concatenate([from_right, from_left], 1)
+    from_right, from_left, _ = lax.optimization_barrier((from_right, from_left, pieces))
+
+    def rows_of_halo(rows):
+        return jnp.concatenate([features[rows], from_right[rows], from_left[rows]], 1)
+
+    before = lax.ppermute(rows_of_halo(slice(tile_rows - HALO, None)), "row", down)
+    after = lax.ppermute(rows_of_halo(slice(0, HALO)), "row", up)
+    ext = rows_of_halo(slice(None))
 
     gathered = exchange(pieces).reshape(devices * per_sub, 3 * LANES)
 
     top, bottom, inside, beside = windows(
-        mid, side, w_query, w_keyval, win_anchor.reshape(-1, 2), win_weight.reshape(-1)
+        before, ext, after, w_query, w_keyval, win_anchor.reshape(-1, 2), win_weight.reshape(-1)
     )
     above = lax.ppermute(bottom, "row", down)
     below = lax.ppermute(top, "row", up)
@@ -393,17 +438,17 @@
         ],
         0,
     ).astype(BF16)
+    gathered, beside = lax.optimization_barrier((gathered, beside))
     on_first = lax.ppermute(beside[:, :HALO], "col", right)
     on_last = lax.ppermute(beside[:, HALO:], "col", left)
+    mixed = lattice_attend(gathered)
+    mixed, on_first, on_last = lax.optimization_barrier((mixed, on_first, on_last))
+    returned = exchange(mixed.reshape(devices, per_sub, LANES))
     arrived = jnp.concatenate([on_first, on_last], 1)
-
-    mixed = lattice_attend(gathered)
-    returned = exchange(mixed.reshape(devices, per_sub, LANES))
+    windowed, share = settle(inside, above, below, arrived)
+    mask = jnp.broadcast_to(known_mask.reshape(count, 1), (count, LANES))
     returned = returned.reshape(SUBS, devices // SUBS, per_sub, LANES)
-    mask = jnp.broadcast_to(known_mask.reshape(count, 1), (count, LANES))
-    out = blend(
-        x, known.reshape(count, channels), mask, returned, inside, above, below, arrived, w_out
-    )
+    out = blend(x, known.reshape(count, channels), mask, returned, windowed, share, w_out)
     return out.reshape(tile_rows, tile_cols, channels)
 
 

time: 279 us -> 237 us (0.85); the launches traced: 273 us -> 237 us
  waiting for transfers between devices: 55 us -> 28.7 us
  Pallas kernels: 145 us -> 138 us
  starting transfers between devices: 62.2 us -> 59.4 us
    ppermute x1, waiting for transfers between devices: 22.3 us -> 1.89 us  [on_device(): below = lax.ppermute(top, 'row', up)]
    ppermute x1, waiting for transfers between devices: 20.1 us -> 0.01 us  [on_device(): on_first = lax.ppermute(beside[:, :HALO], 'col', right)]
    all_to_all x2, starting transfers between devices: 40.1 us -> 24 us  [exchange(): lax.all_to_all(pieces, ('row', 'col'), split_axis=0, concat_axis=0, tiled...]
    all_to_all x2, waiting for transfers between devices: 0.01 us -> 13.6 us  [exchange(): lax.all_to_all(pieces, ('row', 'col'), split_axis=0, concat_axis=0, tiled...]
    ppermute x1, starting transfers between devices: 3.45 us -> 11.4 us  [on_device(): on_first = lax.ppermute(beside[:, :HALO], 'col', right)]
    pallas_call x1 -> x2, Pallas kernels: 26.4 us -> 20.4 us  [the longest x1 16.4 us: windows(): pl.pallas_call(windows_kernel, in_specs=[smem, smem] + [vmem] * 5, out_sp...]
    ppermute x1, starting transfers between devices: 1.91 us -> 7.74 us  [on_device(): above = lax.ppermute(bottom, 'row', down)]
    ppermute x1, waiting for transfers between devices: 3.97 us -> 9.63 us  [on_device(): above = lax.ppermute(bottom, 'row', down)]
  transfers between devices with their start and end apart: 10 -> 10, of which waited for: 6 -> 5; matrix products, arithmetic and copies ran while one was open for 3% -> 3% of each run, Pallas kernels for 13% -> 55%
where the time goes in v2:
time: 237 us
  Pallas kernels  138 us (58%)
  starting transfers between devices  59.4 us (25%)
  waiting for transfers between devices  28.7 us (12%)
  other arithmetic  5.65 us (2%)
  local copies, waits for them, and re-layouts  4.8 us (2%)
    pallas_call x1, Pallas kernels, lattice_attend(): pl.pallas_call(lattice_kernel, grid=(count // QBLOCK,), in_specs=[whole(x...  100 us
    all_to_all x2, starting transfers between devices, exchange(): lax.all_to_all(pieces, ('row', 'col'), split_axis=0, concat_axis=0, tiled...  24 us
    pallas_call x1, Pallas kernels, windows(): pl.pallas_call(windows_kernel, in_specs=[smem, smem] + [vmem] * 5, out_sp...  16.4 us
    all_to_all x2, waiting for transfers between devices, exchange(): lax.all_to_all(pieces, ('row', 'col'), split_axis=0, concat_axis=0, tiled...  13.6 us
    ppermute x1, starting transfers between devices, on_device(): on_first = lax.ppermute(beside[:, :HALO], 'col', right)  11.4 us
    ppermute x1, waiting for transfers between devices, on_device(): above = lax.ppermute(bottom, 'row', down)  9.63 us
    pallas_call x1, Pallas kernels, project(): pl.pallas_call(project_kernel, grid=(steps,), in_specs=[whole(x.shape), p...  9.61 us
    pallas_call x1, Pallas kernels, blend(): pl.pallas_call(blend_kernel, grid=(channels // width,), in_specs=[by_cols...  7.85 us
  transfers between devices with their start and end apart: 10, of which 5 were waited for; matrix products, arithmetic and copies ran while one was open for 3% of the time, Pallas kernels for 55%

profile of v2, /device:TPU:1, one launch (start us, length us, event | category | flops | bytes accessed | tf_op | source)
XLA Modules:
  0.0 236.8 jit_solution(495876056197559490)
XLA Ops:
  0.0 1.4 fusion.1
  1.4 1.3 collective-permute-start
  2.7 5.0 %collective-permute-start.1 = (bf16[32,8,1280]{2,1,0:T(8,128)(2,1)S(1)}, bf16[32,8,1280]{2,1,0:T(8,128)(2,1)S(1)}, u32[]{:S(2)}, u32[]{:S(2)}) collective-permute-start(bf16[32,8,1280]{2,1,0:T(8,128)(2,1)S(1)} %get-tuple-element.35), channel_id=1, source_target_pairs={{0,1},{1,2},{2,3},{3,4},{4,5},{5,6},{6,7},{7,8},{8,9},{9,10},{10,1... | collective-permute-start | bytes 1966088 | tf_op jit(solution)/shard_map/ppermute | solution.py:415
  7.7 9.6 %project.1 = bf16[16,8,32,384]{3,2,1,0:T(8,128)(2,1)} custom-call(bf16[512,1280]{1,0:T(8,128)(2,1)} %bitcast.9, bf16[1280,1024]{1,0:T(8,128)(2,1)} %wq_ref.3, bf16[1280,2048]{1,0:T(8,128)(2,1)} %wkv_ref.1, bf16[1280,2048]{1,0:T(8,128)(2,1)} %wkv_ref.1), custom_call_target="tpu_custom_call" | custom-call | flops 4026531840 | bytes 12320768 | tf_op jit(solution)/shard_map/project/pallas_call | solution.py:75
  17.4 2.8 %collective-permute-done = bf16[32,8,1280]{2,1,0:T(8,128)(2,1)S(1)} collective-permute-done((bf16[32,8,1280]{2,1,0:T(8,128)(2,1)S(1)}, bf16[32,8,1280]{2,1,0:T(8,128)(2,1)S(1)}, u32[]{:S(2)}, u32[]{:S(2)}) %collective-permute-start) | collective-permute-done | bytes 655392 | tf_op jit(solution)/shard_map/ppermute | solution.py:414
  21.1 3.5 %collective-permute-start.3 = (bf16[8,32,1280]{2,1,0:T(8,128)(2,1)S(1)}, bf16[8,32,1280]{2,1,0:T(8,128)(2,1)}, u32[]{:S(2)}, u32[]{:S(2)}) collective-permute-start(bf16[8,32,1280]{2,1,0:T(8,128)(2,1)S(1)} %pad_maximum_fusion.4), channel_id=1, source_target_pairs={{16,0},{32,16},{48,32},{64,48},{80,64},{96,80},{112,96},{17,1},{33... | collective-permute-start | bytes 1966088 | tf_op jit(solution)/shard_map/ppermute | solution.py:423
  25.5 3.1 %collective-permute-start.2 = (bf16[8,32,1280]{2,1,0:T(8,128)(2,1)}, bf16[8,32,1280]{2,1,0:T(8,128)(2,1)}, u32[]{:S(2)}, u32[]{:S(2)}) collective-permute-start(bf16[8,32,1280]{2,1,0:T(8,128)(2,1)} %pad_maximum_fusion.3), channel_id=1, source_target_pairs={{0,16},{16,32},{32,48},{48,64},{64,80},{80,96},{96,112},{1,17},{17... | collective-permute-start | bytes 1966088 | tf_op jit(solution)/shard_map/ppermute | solution.py:422
  28.7 13.3 %all-to-all-start = ((bf16[128,32,384]{2,1,0:T(8,128)(2,1)}), bf16[128,32,384]{2,1,0:T(8,128)(2,1)}, u32[]{:S(2)}, u32[]{:S(2)}) async-start(bf16[128,32,384]{2,1,0:T(8,128)(2,1)} %bitcast.11), calls=%async_computation | async-start | bytes 6291456 | tf_op jit(solution)/shard_map/all_to_all | solution.py:395
  42.7 1.9 pad_maximum_fusion.ext_ref
  44.6 16.4 %windows.1 = (bf16[8,32,1152]{2,1,0:T(8,128)(2,1)}, bf16[8,32,1152]{2,1,0:T(8,128)(2,1)}, f32[32,16,1152]{2,1,0:T(8,128)}, f32[32,16,1152]{2,1,0:T(8,128)}) custom-call(s32[6,2]{1,0:T(8,128)} %copy.11.anchor, s32[6]{0:T(128)} %bitcast.16, bf16[8,32,1280]{2,1,0:T(8,128)(2,1)} %collective-permute-done.2.before_ref, ...), custom_call_target="tpu_custom_call" | custom-call | flops 135291469824 | bytes 11796480 | tf_op jit(solution)/shard_map/windows/pallas_call | solution.py:286
  60.9 7.7 %collective-permute-start.4 = (bf16[8,32,1152]{2,1,0:T(8,128)(2,1)}, bf16[8,32,1152]{2,1,0:T(8,128)(2,1)S(1)}, u32[]{:S(2)}, u32[]{:S(2)}) collective-permute-start(bf16[8,32,1152]{2,1,0:T(8,128)(2,1)} %get-tuple-element.21), channel_id=1, source_target_pairs={{0,16},{16,32},{32,48},{48,64},{64,80},{80,96},{96,112},{1,17},{17... | collective-permute-start | bytes 1769480 | tf_op jit(solution)/shard_map/ppermute | solution.py:431
  68.7 1.9 collective-permute-start.5
  70.6 1.3 slice.69
  72.0 9.6 %collective-permute-done.4.above_ref = bf16[8,32,1152]{2,1,0:T(8,128)(2,1)S(1)} collective-permute-done((bf16[8,32,1152]{2,1,0:T(8,128)(2,1)}, bf16[8,32,1152]{2,1,0:T(8,128)(2,1)S(1)}, u32[]{:S(2)}, u32[]{:S(2)}) %collective-permute-start.4) | collective-permute-done | bytes 589856 | tf_op jit(solution)/shard_map/ppermute | solution.py:431
  81.6 1.9 collective-permute-done.5.below_ref
  83.5 1.6 add_convert_fusion.1
  85.4 11.4 %collective-permute-start.6 = (bf16[32,8,1152]{2,1,0:T(8,128)(2,1)S(1)}, bf16[32,8,1152]{2,1,0:T(8,128)(2,1)S(1)}, u32[]{:S(2)}, u32[]{:S(2)}) collective-permute-start(bf16[32,8,1152]{2,1,0:T(8,128)(2,1)S(1)} %get-tuple-element.38), channel_id=1, source_target_pairs={{0,1},{1,2},{2,3},{3,4},{4,5},{5,6},{6,7},{7,8},{8,9},{9,10},{10,1... | collective-permute-start | bytes 1769480 | tf_op jit(solution)/shard_map/ppermute | solution.py:442
  96.8 1.5 collective-permute-start.7
  98.2 100.0 %lattice_attend.1 = bf16[4096,128]{1,0:T(8,128)(2,1)} custom-call(bf16[4096,384]{1,0:T(8,128)(2,1)} %bitcast.3.x_ref), custom_call_target="tpu_custom_call" | custom-call | flops 34359738368 | bytes 4194304 | tf_op jit(solution)/shard_map/lattice_attend/pallas_call | solution.py:170
  198.3 10.6 %all-to-all-start.1 = ((bf16[128,32,128]{2,1,0:T(8,128)(2,1)}), bf16[128,32,128]{2,1,0:T(8,128)(2,1)S(1)}, u32[]{:S(2)}, u32[]{:S(2)}) async-start(bf16[128,32,128]{2,1,0:T(8,128)(2,1)} %bitcast.14), calls=%async_computation.1 | async-start | bytes 2097152 | tf_op jit(solution)/shard_map/all_to_all | solution.py:395
  209.1 1.1 pad_maximum_fusion.2.beside_ref
  210.2 4.1 %settle.1 = (f32[512,1024]{1,0:T(8,128)}, f32[512,128]{1,0:T(8,128)}) custom-call(f32[32,16,1152]{2,1,0:T(8,128)} %get-tuple-element.26.mid_ref, bf16[8,32,1152]{2,1,0:T(8,128)(2,1)} %copy-done.2, bf16[8,32,1152]{2,1,0:T(8,128)(2,1)} %copy-done.3, bf16[32,16,1152]{2,1,0:T(8,128)(2,1)} %pad_maximum_fusion.2.beside_ref), custom_call_target="tpu_custom_call" | custom-call | flops 2359296 | bytes 7077888 | tf_op jit(solution)/shard_map/settle/pallas_call | solution.py:333
  214.3 13.6 %all-to-all-done.1 = bf16[128,32,128]{2,1,0:T(8,128)(2,1)S(1)} async-done(((bf16[128,32,128]{2,1,0:T(8,128)(2,1)}), bf16[128,32,128]{2,1,0:T(8,128)(2,1)S(1)}, u32[]{:S(2)}, u32[]{:S(2)}) %all-to-all-start.1) | async-done | bytes 1048608 | tf_op jit(solution)/shard_map/all_to_all | solution.py:395
  228.9 7.9 %blend.1 = bf16[512,1280]{1,0:T(8,128)(2,1)} custom-call(bf16[512,1280]{1,0:T(8,128)(2,1)} %bitcast.10, bf16[512,1280]{1,0:T(8,128)(2,1)} %bitcast.13, s32[512,128]{1,0:T(8,128)} %broadcast_in_dim.8.mask_ref, bf16[16,8,32,128]{3,2,1,0:T(8,128)(2,1)} %bitcast.12, f32[512,1024]{1,0:T(8,128)} %get-tuple-element.29.sum_ref, ...), custom_call_target="tpu_custom_call" | custom-call | flops 1879048192 | bytes 6553600 | tf_op jit(solution)/shard_map/blend/pallas_call | solution.py:375
  (28 shorter events, 4.1 us)
Async XLA Ops:
  1.4 18.8 %collective-permute-start = (bf16[32,8,1280]{2,1,0:T(8,128)(2,1)S(1)}, bf16[32,8,1280]{2,1,0:T(8,128)(2,1)S(1)}, u32[]{:S(2)}, u32[]{:S(2)}) collective-permute-start(bf16[32,8,1280]{2,1,0:T(8,128)(2,1)S(1)} %get-tuple-element.36), channel_id=1, source_target_pairs={{1,0},{2,1},{3,2},{4,3},{5,4},{6,5},{7,6},{8,7},{9,8},{10,9},{11,1... | collective-permute-start | bytes 1966088 | tf_op jit(solution)/shard_map/ppermute | solution.py:414
  2.7 18.4 %collective-permute-start.1 = (bf16[32,8,1280]{2,1,0:T(8,128)(2,1)S(1)}, bf16[32,8,1280]{2,1,0:T(8,128)(2,1)S(1)}, u32[]{:S(2)}, u32[]{:S(2)}) collective-permute-start(bf16[32,8,1280]{2,1,0:T(8,128)(2,1)S(1)} %get-tuple-element.35), channel_id=1, source_target_pairs={{0,1},{1,2},{2,3},{3,4},{4,5},{5,6},{6,7},{7,8},{8,9},{9,10},{10,1... | collective-permute-start | bytes 1966088 | tf_op jit(solution)/shard_map/ppermute | solution.py:415
  7.7 9.6 %copy-start = (bf16[32,16,1280]{2,1,0:T(8,128)(2,1)S(1)}, bf16[32,16,1280]{2,1,0:T(8,128)(2,1)}, u32[]{:S(2)}) copy-start(bf16[32,16,1280]{2,1,0:T(8,128)(2,1)} %param.8) | copy-start | bytes 3932164
  21.1 23.4 %collective-permute-start.3 = (bf16[8,32,1280]{2,1,0:T(8,128)(2,1)S(1)}, bf16[8,32,1280]{2,1,0:T(8,128)(2,1)}, u32[]{:S(2)}, u32[]{:S(2)}) collective-permute-start(bf16[8,32,1280]{2,1,0:T(8,128)(2,1)S(1)} %pad_maximum_fusion.4), channel_id=1, source_target_pairs={{16,0},{32,16},{48,32},{64,48},{80,64},{96,80},{112,96},{17,1},{33... | collective-permute-start | bytes 1966088 | tf_op jit(solution)/shard_map/ppermute | solution.py:423
  25.5 16.5 %copy-start.5 = (s32[1,1,6,2]{2,3,1,0:T(2,128)S(1)}, s32[1,1,6,2]{2,3,1,0:T(2,128)}, u32[]{:S(2)}) copy-start(s32[1,1,6,2]{2,3,1,0:T(2,128)} %param.14) | copy-start | bytes 148
  25.5 19.1 %collective-permute-start.2 = (bf16[8,32,1280]{2,1,0:T(8,128)(2,1)}, bf16[8,32,1280]{2,1,0:T(8,128)(2,1)}, u32[]{:S(2)}, u32[]{:S(2)}) collective-permute-start(bf16[8,32,1280]{2,1,0:T(8,128)(2,1)} %pad_maximum_fusion.3), channel_id=1, source_target_pairs={{0,16},{16,32},{32,48},{48,64},{64,80},{80,96},{96,112},{1,17},{17... | collective-permute-start | bytes 1966088 | tf_op jit(solution)/shard_map/ppermute | solution.py:422
  28.7 56.6 %all-to-all-start = ((bf16[128,32,384]{2,1,0:T(8,128)(2,1)}), bf16[128,32,384]{2,1,0:T(8,128)(2,1)}, u32[]{:S(2)}, u32[]{:S(2)}) async-start(bf16[128,32,384]{2,1,0:T(8,128)(2,1)} %bitcast.11), calls=%async_computation | async-start | bytes 6291456 | tf_op jit(solution)/shard_map/all_to_all | solution.py:395
  60.9 20.6 %collective-permute-start.4 = (bf16[8,32,1152]{2,1,0:T(8,128)(2,1)}, bf16[8,32,1152]{2,1,0:T(8,128)(2,1)S(1)}, u32[]{:S(2)}, u32[]{:S(2)}) collective-permute-start(bf16[8,32,1152]{2,1,0:T(8,128)(2,1)} %get-tuple-element.21), channel_id=1, source_target_pairs={{0,16},{16,32},{32,48},{48,64},{64,80},{80,96},{96,112},{1,17},{17... | collective-permute-start | bytes 1769480 | tf_op jit(solution)/shard_map/ppermute | solution.py:431
  68.7 14.8 %collective-permute-start.5 = (bf16[8,32,1152]{2,1,0:T(8,128)(2,1)}, bf16[8,32,1152]{2,1,0:T(8,128)(2,1)S(1)}, u32[]{:S(2)}, u32[]{:S(2)}) collective-permute-start(bf16[8,32,1152]{2,1,0:T(8,128)(2,1)} %get-tuple-element.22), channel_id=1, source_target_pairs={{16,0},{32,16},{48,32},{64,48},{80,64},{96,80},{112,96},{17,1},{33... | collective-permute-start | bytes 1769480 | tf_op jit(solution)/shard_map/ppermute | solution.py:432
  81.6 3.6 %copy-start.2 = (bf16[8,32,1152]{2,1,0:T(8,128)(2,1)}, bf16[8,32,1152]{2,1,0:T(8,128)(2,1)S(1)}, u32[]{:S(2)}) copy-start(bf16[8,32,1152]{2,1,0:T(8,128)(2,1)S(1)} %collective-permute-done.4.above_ref) | copy-start | bytes 1769476
  83.5 1.8 copy-start.3
  85.4 112.9 %collective-permute-start.6 = (bf16[32,8,1152]{2,1,0:T(8,128)(2,1)S(1)}, bf16[32,8,1152]{2,1,0:T(8,128)(2,1)S(1)}, u32[]{:S(2)}, u32[]{:S(2)}) collective-permute-start(bf16[32,8,1152]{2,1,0:T(8,128)(2,1)S(1)} %get-tuple-element.38), channel_id=1, source_target_pairs={{0,1},{1,2},{2,3},{3,4},{4,5},{5,6},{6,7},{7,8},{8,9},{9,10},{10,1... | collective-permute-start | bytes 1769480 | tf_op jit(solution)/shard_map/ppermute | solution.py:442
  96.8 101.5 %collective-permute-start.7 = (bf16[32,8,1152]{2,1,0:T(8,128)(2,1)S(1)}, bf16[32,8,1152]{2,1,0:T(8,128)(2,1)S(1)}, u32[]{:S(2)}, u32[]{:S(2)}) collective-permute-start(bf16[32,8,1152]{2,1,0:T(8,128)(2,1)S(1)} %get-tuple-element.37), channel_id=1, source_target_pairs={{1,0},{2,1},{3,2},{4,3},{5,4},{6,5},{7,6},{8,7},{9,8},{10,9},{11,1... | collective-permute-start | bytes 1769480 | tf_op jit(solution)/shard_map/ppermute | solution.py:443
  198.3 10.6 %copy-start.4 = (s32[32,16]{0,1:T(8,128)S(1)}, s32[32,16]{0,1:T(8,128)}, u32[]{:S(2)}) copy-start(s32[32,16]{0,1:T(8,128)} %param.10) | copy-start | bytes 6148
  198.3 29.5 %all-to-all-start.1 = ((bf16[128,32,128]{2,1,0:T(8,128)(2,1)}), bf16[128,32,128]{2,1,0:T(8,128)(2,1)S(1)}, u32[]{:S(2)}, u32[]{:S(2)}) async-start(bf16[128,32,128]{2,1,0:T(8,128)(2,1)} %bitcast.14), calls=%async_computation.1 | async-start | bytes 2097152 | tf_op jit(solution)/shard_map/all_to_all | solution.py:395
  227.8 1.1 copy-start.1

commit v3 on v2

v3 whole, which is shorter than its diff:
```python
import functools
import math

import jax
import jax.numpy as jnp
from jax import lax
from jax.experimental import pallas as pl
from jax.experimental.pallas import tpu as pltpu
from jax.sharding import PartitionSpec as P

HD = 64
STRIDE = 4
WIN = 16
HALO = 8
SUBS = STRIDE * STRIDE
LANES = 128
SCALE = HD**-0.5 * math.log2(math.e)
FREE_RANGE = 100.0
VROWS = 80
QBLOCK = 2048
KBLOCK = 256
QPART = 256
AHEAD = 8
BF16 = jnp.bfloat16
F32 = jnp.float32


def dot(a, b):
    return jnp.dot(a, b, preferred_element_type=F32)


def dot_nt(a, b):
    return lax.dot_general(a, b, (((1,), (1,)), ((), ())), preferred_element_type=F32)


def whole(shape):
    return pl.BlockSpec(shape, lambda *_: (0,) * len(shape), pipeline_mode=pl.Buffered(1))


PARAMS = pltpu.CompilerParams(vmem_limit_bytes=60 * 2**20)


def lattice_order(count, by_row):
    lattice = lax.broadcasted_iota(jnp.int32, (count, count), 0 if by_row else 1)
    cell = lax.broadcasted_iota(jnp.int32, (count, count), 1 if by_row else 0)
    per_sub = count // SUBS
    tile_cols = 16
    sub, place = lattice // per_sub, lattice % per_sub
    across = tile_cols // STRIDE
    row = (place // across) * STRIDE + sub // STRIDE
    col = (place % across) * STRIDE + sub % STRIDE
    return jnp.where(cell == row * tile_cols + col, 1.0, 0.0).astype(BF16)


def project_kernel(x_ref, wq_ref, wk_ref, wv_ref, out_ref, ordered):
    count = x_ref.shape[0]

    @pl.when(pl.program_id(0) == 0)
    def _():
        ordered[...] = dot(lattice_order(count, True), x_ref[...]).astype(BF16)

    x = ordered[...]
    q, k, v = (dot(x, w_ref[...]) for w_ref in (wq_ref, wk_ref, wv_ref))
    for g in range(2):
        at = g * LANES
        parts = [
            jnp.concatenate([q[:, at : at + HD], k[:, at : at + HD]], 1),
            v[:, at : at + LANES],
            jnp.concatenate([q[:, at + HD : at + LANES], k[:, at + HD : at + LANES]], 1),
        ]
        for j, part in enumerate(parts):
            out_ref[:, g, :, j * LANES : (j + 1) * LANES] = part.astype(BF16).reshape(
                SUBS, count // SUBS, LANES
            )


def project(x, w_query, w_keyval):
    count, channels = x.shape
    inner = w_query.shape[1]
    groups = inner // LANES
    steps = groups // 2
    per_sub = count // SUBS
    return pl.pallas_call(
        project_kernel,
        grid=(steps,),
        in_specs=[
            whole(x.shape),
            pl.BlockSpec((channels, 2 * LANES), lambda g: (0, g)),
            pl.BlockSpec((channels, 2 * LANES), lambda g: (0, g)),
            pl.BlockSpec((channels, 2 * LANES), lambda g: (0, g + steps)),
        ],
        out_specs=pl.BlockSpec((SUBS, 2, per_sub, 3 * LANES), lambda g: (0, g, 0, 0)),
        out_shape=jax.ShapeDtypeStruct((SUBS, groups, per_sub, 3 * LANES), BF16),
        scratch_shapes=[pltpu.VMEM((count, channels), BF16)],
        compiler_params=PARAMS,
        cost_estimate=pl.CostEstimate(
            flops=2 * count * channels * 3 * inner,
            bytes_accessed=2 * (3 * channels * inner + count * channels + 3 * count * inner),
            transcendentals=0,
        ),
        name="project",
    )(x, w_query, w_keyval, w_keyval)


def lattice_kernel(head, qk_ref, v_ref, *refs):
    if head == 0:
        o_ref, queries_t, values_t, free = refs
    else:
        other_ref, o_ref, queries_t, values_t, free = refs
    count = qk_ref.shape[0]
    block = o_ref.shape[1 - head]
    step = pl.program_id(0)

    @pl.when(step == 0)
    def _():
        both = qk_ref[...].astype(F32)
        q_t = both.T[:HD]
        lane = lax.broadcasted_iota(jnp.int32, both.shape, 1)
        k_norms = jnp.sum(jnp.where(lane < HD, 0.0, both * both), axis=1)
        bound = jnp.max(jnp.sum(q_t * q_t, axis=0)) * jnp.max(k_norms)
        free[0] = (bound * (SCALE * SCALE) <= FREE_RANGE * FREE_RANGE).astype(jnp.int32)
        queries_t[0:HD] = jnp.zeros((HD, count), BF16)
        queries_t[HD:LANES] = q_t.astype(BF16)
        v_t = v_ref[...].astype(F32).T
        values_t[0:HD] = v_t[head * HD : (head + 1) * HD].astype(BF16)
        values_t[HD:VROWS] = jnp.ones((VROWS - HD, count), BF16)

    cols = pl.ds(pl.multiple_of(step * block, block), block)

    def finish(total):
        out = total[:HD] / total[HD : HD + 1]
        if head == 0:
            o_ref[...] = out.astype(BF16)
        else:
            o_ref[...] = jnp.concatenate([other_ref[...].astype(F32), out], 0).T.astype(BF16)

    @pl.when(free[0] == 1)
    def _():
        parts = block // QPART
        items = [(c, j) for c in range(0, count, KBLOCK) for j in range(parts)]
        queries = [
            queries_t[:, pl.ds(pl.multiple_of(step * block + j * QPART, QPART), QPART)]
            for j in range(parts)
        ]

        def score(i):
            c, j = items[i]
            return dot(qk_ref[c : c + KBLOCK, :], queries[j])

        totals = [None] * parts
        ahead = [score(i) for i in range(AHEAD)]
        for i, (c, j) in enumerate(items):
            now = ahead.pop(0)
            if i + AHEAD < len(items):
                ahead.append(score(i + AHEAD))
            weights = jnp.exp2(now * SCALE).astype(BF16)
            part = dot(values_t[:, c : c + KBLOCK], weights)
            totals[j] = part if totals[j] is None else totals[j] + part
        finish(jnp.concatenate(totals, 1))

    @pl.when(free[0] == 0)
    def _():
        chunks = count // KBLOCK
        q = queries_t[:, cols]

        def score(c):
            return dot(qk_ref[pl.ds(pl.multiple_of(c * KBLOCK, KBLOCK), KBLOCK), :], q)

        def top(c, m):
            return jnp.maximum(m, jnp.max(score(c), axis=0, keepdims=True))

        m = lax.fori_loop(0, chunks, top, jnp.full((1, block), -jnp.inf, F32))

        def add(c, total):
            weights = jnp.exp2((score(c) - m) * SCALE).astype(BF16)
            rows = pl.ds(pl.multiple_of(c * KBLOCK, KBLOCK), KBLOCK)
            return total + dot(values_t[:, rows], weights)

        finish(lax.fori_loop(0, chunks, add, jnp.zeros((VROWS, block), F32)))


def lattice_attend(head, x, other=None):
    count = x.shape[0]
    in_specs = [
        pl.BlockSpec((count, LANES), lambda i: (0, 2 * head), pipeline_mode=pl.Buffered(1)),
        pl.BlockSpec((count, LANES), lambda i: (0, 1), pipeline_mode=pl.Buffered(1)),
    ]
    args = [x, x]
    if head == 0:
        out_spec = pl.BlockSpec((HD, QBLOCK), lambda i: (0, i))
        out_shape = (HD, count)
    else:
        in_specs.append(pl.BlockSpec((HD, QBLOCK), lambda i: (0, i)))
        args.append(other)
        out_spec = pl.BlockSpec((QBLOCK, LANES), lambda i: (i, 0))
        out_shape = (count, LANES)
    return pl.pallas_call(
        functools.partial(lattice_kernel, head),
        grid=(count // QBLOCK,),
        in_specs=in_specs,
        out_specs=out_spec,
        out_shape=jax.ShapeDtypeStruct(out_shape, BF16),
        scratch_shapes=[
            pltpu.VMEM((LANES, count), BF16),
            pltpu.VMEM((VROWS, count), BF16),
            pltpu.SMEM((1,), jnp.int32),
        ],
        compiler_params=PARAMS,
        cost_estimate=pl.CostEstimate(
            flops=4 * 4 * count * count * HD,
            bytes_accessed=6 * count * LANES,
            transcendentals=count * count,
        ),
        name="lattice_attend_" + str(head),
    )(*args)


def windows_kernel(
    anchor, weight, mid_hbm, before_hbm, after_hbm, side_before_hbm, side_after_hbm, right_ref, left_ref,
    wq_hbm, wkv_hbm, top_out, bottom_out, mid_out, right_out, left_out, held, wq_ref, wkv_ref, mid_sum, side_sum, results_t, sems,
):
    channels, inner = wq_ref.shape
    cells = WIN * WIN
    wide = inner + LANES
    tile_rows = mid_hbm.shape[0]
    end = tile_rows + HALO
    pair_lanes = 2 * LANES
    copies = [
        pltpu.make_async_copy(source, target, sems.at[i])
        for i, (source, target) in enumerate(
            (
                (mid_hbm, held.at[HALO:end, 0:WIN]),
                (before_hbm, held.at[0:HALO, 0:WIN]),
                (after_hbm, held.at[end : end + HALO, 0:WIN]),
                (side_before_hbm, held.at[0:HALO, WIN : 2 * WIN]),
                (side_after_hbm, held.at[end : end + HALO, WIN : 2 * WIN]),
            )
        )
    ]
    weight_copies = {}
    for g in range(0, inner, pair_lanes):
        for part, (source, target, at) in enumerate(
            ((wq_hbm, wq_ref, g), (wkv_hbm, wkv_ref, g), (wkv_hbm, wkv_ref, inner + g))
        ):
            cols = slice(at, at + pair_lanes)
            sem = sems.at[len(copies) + 3 * (g // pair_lanes) + part]
            weight_copies.setdefault(g, []).append(
                pltpu.make_async_copy(source.at[:, cols], target.at[:, cols], sem)
            )
    for copy in copies + sum(weight_copies.values(), []):
        copy.start()
    mid_sum[...] = jnp.zeros(mid_sum.shape, F32)
    side_sum[...] = jnp.zeros(side_sum.shape, F32)
    results_t[inner:wide] = jnp.ones((LANES, cells), BF16)
    for row in range(0, tile_rows, HALO):
        rows = slice(row, row + HALO)
        pair = (right_ref[rows].astype(F32), left_ref[rows].astype(F32))
        held[HALO + row : 2 * HALO + row, WIN : 2 * WIN] = jnp.concatenate(pair, 1).astype(BF16)
    for copy in copies:
        copy.wait()
    slots = weight.shape[0]
    live = sum((weight[s] > 0).astype(jnp.int32) for s in range(slots))
    first = lax.broadcasted_iota(jnp.int32, (cells, LANES), 1) < HD
    ones = jnp.ones((VROWS - HD, cells), BF16)

    def one_hot(window_dim, left):
        shape = (cells, 2 * cells) if window_dim == 0 else (2 * cells, cells)
        window = lax.broadcasted_iota(jnp.int32, shape, window_dim)
        source = lax.broadcasted_iota(jnp.int32, shape, 1 - window_dim)
        place = ((window & (WIN - 1)) + left) & (2 * WIN - 1)
        held = (source & (WIN - 1)) + ((source >> 8) << 4)
        same = (((window ^ source) & (cells - WIN)) == 0) & (place == held)
        return jnp.where(same, 1.0, 0.0)

    def one_window(slot, arriving):
        top = anchor[slot, 0] + HALO
        left = anchor[slot, 1]
        factor = weight[slot].astype(F32)
        rows = pl.ds(top, WIN)
        source = jnp.concatenate(
            [
                held[rows, 0:WIN].reshape(cells, channels),
                held[rows, WIN : 2 * WIN].reshape(cells, channels),
            ],
            0,
        )
        x = dot(one_hot(0, left).astype(BF16), source).astype(BF16)

        def project(g):
            for copy in arriving.get(g, ()):
                copy.wait()
            q = dot(x, wq_ref[:, g : g + 2 * LANES]).astype(BF16)
            k = dot(x, wkv_ref[:, g : g + 2 * LANES]).astype(BF16)
            v = dot(x, wkv_ref[:, inner + g : inner + g + 2 * LANES])
            return q, k, v.T.astype(BF16)

        def scores(q, k, j):
            lanes = slice(j // 2 * LANES, (j // 2 + 1) * LANES)
            own = jnp.where(first if j % 2 == 0 else ~first, q[:, lanes], jnp.zeros((), BF16))
            return dot_nt(k[:, lanes], own)

        def mix(s, v_t, g, j):
            e = jnp.exp2((s - jnp.max(s, axis=0, keepdims=True)) * SCALE).astype(BF16)
            o = dot(jnp.concatenate([v_t[j * HD : (j + 1) * HD], ones], 0), e)
            at = g + j * HD
            results_t[at : at + HD] = (o[:HD] / o[HD : HD + 1]).astype(BF16)

        later = project(0)
        for g in range(0, inner, 2 * LANES):
            q, k, v_t = later
            now = [scores(q, k, j) for j in range(4)]
            if g + 2 * LANES < inner:
                later = project(g + 2 * LANES)
            for j in range(4):
                mix(now[j], v_t, g, j)
        placed = dot_nt((one_hot(1, left) * factor).astype(BF16), results_t[...])
        mid_sum[rows] += placed[:cells].reshape(WIN, WIN, wide)
        side_sum[rows] += placed[cells:].reshape(WIN, WIN, wide)

    def later_window(slot, carry):
        one_window(slot, {})
        return carry

    one_window(0, weight_copies)
    lax.fori_loop(1, live, later_window, 0)
    top_out[:, 0:WIN] = mid_sum[0:HALO].astype(BF16)
    top_out[:, WIN : 2 * WIN] = side_sum[0:HALO].astype(BF16)
    bottom_out[:, 0:WIN] = mid_sum[end : end + HALO].astype(BF16)
    bottom_out[:, WIN : 2 * WIN] = side_sum[end : end + HALO].astype(BF16)
    mid_out[...] = mid_sum[HALO:end].astype(BF16)
    right_out[...] = side_sum[HALO:end, 0:HALO].astype(BF16)
    left_out[...] = side_sum[HALO:end, HALO : 2 * HALO].astype(BF16)


def windows(
    mid, before, after, side_before, side_after, from_right, from_left, w_query, w_keyval, anchor, weight
):
    tile_rows, _, channels = mid.shape
    high = tile_rows + 2 * HALO
    inner = w_query.shape[1]
    wide = inner + LANES
    vmem = pl.BlockSpec(memory_space=pltpu.VMEM)
    smem = pl.BlockSpec(memory_space=pltpu.SMEM)
    free = pl.BlockSpec(memory_space=pl.ANY)
    rim = jax.ShapeDtypeStruct((HALO, 2 * WIN, wide), BF16)
    inside = jax.ShapeDtypeStruct((tile_rows, WIN, wide), BF16)
    edge = jax.ShapeDtypeStruct((tile_rows, HALO, wide), BF16)
    slots = weight.shape[0]
    cells = WIN * WIN
    return pl.pallas_call(
        windows_kernel,
        in_specs=[smem, smem] + [free] * 5 + [vmem] * 2 + [free] * 2,
        out_specs=[vmem] * 5,
        out_shape=[rim, rim, inside, edge, edge],
        scratch_shapes=[
            pltpu.VMEM((high, 2 * WIN, channels), BF16),
            pltpu.VMEM(w_query.shape, BF16),
            pltpu.VMEM(w_keyval.shape, BF16),
            pltpu.VMEM((high, WIN, wide), F32),
            pltpu.VMEM((high, WIN, wide), F32),
            pltpu.VMEM((wide, cells), BF16),
            pltpu.SemaphoreType.DMA((5 + 3 * (inner // (2 * LANES)),)),
        ],
        compiler_params=PARAMS,
        cost_estimate=pl.CostEstimate(
            flops=8 * slots * 2 * cells * 3 * inner * (channels + 2 * cells),
            bytes_accessed=6 * channels * inner + 4 * high * WIN * channels,
            transcendentals=slots * cells * cells * inner // HD,
        ),
        name="windows",
    )(
        anchor, weight, mid, before, after, side_before, side_after, from_right, from_left,
        w_query, w_keyval,
    )


def fold_kernel(right_ref, left_ref, above_ref, below_ref, right_out, left_out):
    tile_rows = right_ref.shape[0]
    sides = [ref[:, WIN : 2 * WIN].astype(F32) for ref in (above_ref, below_ref)]
    for j, (source, target) in enumerate(((right_ref, right_out), (left_ref, left_out))):
        upper, lower = [side[:, j * HALO : (j + 1) * HALO] for side in sides]
        target[0:HALO] = (source[0:HALO].astype(F32) + upper).astype(BF16)
        target[HALO : tile_rows - HALO] = source[HALO : tile_rows - HALO]
        last = slice(tile_rows - HALO, tile_rows)
        target[last] = (source[last].astype(F32) + lower).astype(BF16)


def fold(on_right, on_left, above, below):
    vmem = pl.BlockSpec(memory_space=pltpu.VMEM)
    return pl.pallas_call(
        fold_kernel,
        in_specs=[vmem] * 4,
        out_specs=[vmem] * 2,
        out_shape=[jax.ShapeDtypeStruct(a.shape, a.dtype) for a in (on_right, on_left)],
        compiler_params=PARAMS,
        cost_estimate=pl.CostEstimate(
            flops=on_right.size, bytes_accessed=12 * on_right.size, transcendentals=0
        ),
        name="fold",
    )(on_right, on_left, above, below)


def settle_kernel(
    mid_ref, above_ref, below_ref, beside_ref, mask_ref, sum_ref, share_ref, wide_mask_ref
):
    count, inner = sum_ref.shape
    tile_rows, tile_cols = mask_ref.shape
    cell = lax.broadcasted_iota(jnp.int32, (count, tile_rows), 0)
    row = lax.broadcasted_iota(jnp.int32, (count, tile_rows), 1)
    pick_row = jnp.where(cell // tile_cols == row, 1.0, 0.0).astype(BF16)
    in_row = dot(pick_row, mask_ref[...].astype(BF16))
    cell = lax.broadcasted_iota(jnp.int32, (count, tile_cols), 0)
    col = lax.broadcasted_iota(jnp.int32, (count, tile_cols), 1)
    own = jnp.sum(jnp.where(cell % tile_cols == col, in_row, 0.0), axis=1, keepdims=True)
    wide_mask_ref[...] = jnp.broadcast_to(own, wide_mask_ref.shape)

    def total(lanes):
        upper = above_ref[:, 0:WIN, lanes].astype(F32)
        lower = below_ref[:, 0:WIN, lanes].astype(F32)
        middle = mid_ref[:, :, lanes].astype(F32) + beside_ref[:, :, lanes].astype(F32)
        parts = [
            middle[:HALO] + upper,
            middle[HALO : tile_rows - HALO],
            middle[tile_rows - HALO :] + lower,
        ]
        return jnp.concatenate(parts, 0).reshape(count, LANES)

    share = 1.0 / (1.0 + total(slice(inner, inner + LANES)))
    share_ref[...] = share
    for g in range(0, inner, LANES):
        lanes = slice(g, g + LANES)
        sum_ref[:, lanes] = total(lanes) * share


def settle(mid, above, below, beside, mask):
    tile_rows, tile_cols, wide = mid.shape
    count = tile_rows * tile_cols
    vmem = pl.BlockSpec(memory_space=pltpu.VMEM)
    return pl.pallas_call(
        settle_kernel,
        in_specs=[vmem] * 5,
        out_specs=[vmem] * 3,
        out_shape=[
            jax.ShapeDtypeStruct((count, wide - LANES), F32),
            jax.ShapeDtypeStruct((count, LANES), F32),
            jax.ShapeDtypeStruct((count, LANES), F32),
        ],
        compiler_params=PARAMS,
        cost_estimate=pl.CostEstimate(
            flops=2**17 * count * wide, bytes_accessed=12 * count * wide, transcendentals=0
        ),
        name="settle",
    )(mid, above, below, beside, mask)


def blend_kernel(
    x_hbm, known_hbm, mask_hbm, mixed_hbm, sum_hbm, share_hbm, w_hbm, out_hbm,
    x_ref, known_ref, mask_ref, mixed_ref, sum_ref, share_ref, w_ref, out_ref, blended, sems, out_sems,
):
    count, channels = x_ref.shape
    groups = mixed_ref.shape[1]
    width = 2 * LANES
    blocks = [slice(c, c + width) for c in range(0, channels, width)]
    whole_copies = [
        pltpu.make_async_copy(source, target, sems.at[i])
        for i, (source, target) in enumerate(
            (
                (mixed_hbm, mixed_ref),
                (share_hbm, share_ref),
                (sum_hbm, sum_ref),
                (mask_hbm, mask_ref),
            )
        )
    ]
    block_copies = [
        [
            pltpu.make_async_copy(source.at[:, cols], target.at[:, cols], sems.at[4 + 3 * i + j])
            for j, (source, target) in enumerate(
                ((w_hbm, w_ref), (x_hbm, x_ref), (known_hbm, known_ref))
            )
        ]
        for i, cols in enumerate(blocks)
    ]
    for copy in whole_copies + sum(block_copies, []):
        copy.start()
    back = lattice_order(count, False)
    for copy in whole_copies:
        copy.wait()
    share = jnp.concatenate([share_ref[...]] * 2, 1)
    for g in range(0, groups, 2):
        lanes = slice(g * LANES, (g + 2) * LANES)
        mixed = jnp.concatenate([mixed_ref[:, g + j].reshape(count, LANES) for j in range(2)], 1)
        blended[:, lanes] = (dot(back, mixed) * share + sum_ref[:, lanes]).astype(BF16)
    known_cell = jnp.concatenate([mask_ref[...]] * 2, 1) == 1
    outs = []
    for i, cols in enumerate(blocks):
        for copy in block_copies[i]:
            copy.wait()
        y = (x_ref[:, cols].astype(F32) + dot(blended[...], w_ref[:, cols])).astype(BF16)
        out_ref[:, cols] = jnp.where(known_cell, known_ref[:, cols], y)
        outs.append(
            pltpu.make_async_copy(out_ref.at[:, cols], out_hbm.at[:, cols], out_sems.at[i])
        )
        outs[-1].start()
    for copy in outs:
        copy.wait()


def blend(x, known, mask, mixed, windowed, share, w_out):
    count, channels = x.shape
    inner = w_out.shape[0]
    arrays = (x, known, mask, mixed, windowed, share, w_out)
    free = pl.BlockSpec(memory_space=pl.ANY)
    blocks = channels // (2 * LANES)
    return pl.pallas_call(
        blend_kernel,
        in_specs=[free] * len(arrays),
        out_specs=free,
        out_shape=jax.ShapeDtypeStruct((count, channels), BF16),
        scratch_shapes=[pltpu.VMEM(a.shape, a.dtype) for a in arrays]
        + [
            pltpu.VMEM((count, channels), BF16),
            pltpu.VMEM((count, inner), BF16),
            pltpu.SemaphoreType.DMA((4 + 3 * blocks,)),
            pltpu.SemaphoreType.DMA((blocks,)),
        ],
        compiler_params=PARAMS,
        cost_estimate=pl.CostEstimate(
            flops=2 * count * inner * (channels + count),
            bytes_accessed=2 * inner * channels + 6 * count * channels,
            transcendentals=0,
        ),
        name="blend",
    )(*arrays)


def exchange(pieces):
    return lax.all_to_all(pieces, ("row", "col"), split_axis=0, concat_axis=0, tiled=True)


def neighbours(axis):
    peers = lax.axis_size(axis)
    onward = [(i, i + 1) for i in range(peers - 1)]
    return onward, [(j, i) for i, j in onward]


def on_device(features, known, known_mask, w_query, w_keyval, w_out, win_anchor, win_weight):
    tile_rows, tile_cols, channels = features.shape
    count = tile_rows * tile_cols
    per_sub = count // SUBS
    inner = w_query.shape[1]
    devices = lax.axis_size("row") * lax.axis_size("col")
    down, up = neighbours("row")
    right, left = neighbours("col")
    x = features.reshape(count, channels)

    from_right = lax.ppermute(features[:, :HALO], "col", left)
    from_left = lax.ppermute(features[:, tile_cols - HALO :], "col", right)
    before = lax.ppermute(features[tile_rows - HALO :], "row", down)
    after = lax.ppermute(features[:HALO], "row", up)
    pieces = project(x, w_query, w_keyval).reshape(devices, per_sub, 3 * LANES)
    from_right, from_left, mask, anchors, _ = lax.optimization_barrier(
        (from_right, from_left, known_mask.astype(F32), win_anchor.reshape(-1, 2), pieces)
    )

    def corners(rows):
        return jnp.concatenate([from_right[rows], from_left[rows]], 1)

    side_before = lax.ppermute(corners(slice(tile_rows - HALO, None)), "row", down)
    side_after = lax.ppermute(corners(slice(0, HALO)), "row", up)

    gathered = exchange(pieces).reshape(devices * per_sub, 3 * LANES)

    top, bottom, inside, on_right, on_left = windows(
        features,
        before,
        after,
        side_before,
        side_after,
        from_right,
        from_left,
        w_query,
        w_keyval,
        anchors,
        win_weight.reshape(-1),
    )
    above = lax.ppermute(bottom, "row", down)
    below = lax.ppermute(top, "row", up)
    half = lattice_attend(0, gathered)
    half, above, below = lax.optimization_barrier((half, above, below))
    on_right, on_left = fold(on_right, on_left, above, below)
    gathered, half, on_right, on_left = lax.optimization_barrier((gathered, half, on_right, on_left))
    on_first = lax.ppermute(on_right, "col", right)
    on_last = lax.ppermute(on_left, "col", left)
    mixed = lattice_attend(1, gathered, half)
    mixed, on_first, on_last = lax.optimization_barrier((mixed, on_first, on_last))
    returned = exchange(mixed.reshape(devices, per_sub, LANES))
    arrived = jnp.concatenate([on_first, on_last], 1)
    windowed, share, mask = settle(inside, above, below, arrived, mask)
    returned = returned.reshape(SUBS, devices // SUBS, per_sub, LANES)
    out = blend(x, known.reshape(count, channels), mask, returned, windowed, share, w_out)
    return out.reshape(tile_rows, tile_cols, channels)


def solution(mesh):
    in_specs = (
        P("row", "col", None),
        P("row", "col", None),
        P("row", "col"),
        P(),
        P(),
        P(),
        P("row", "col", None, None),
        P("row", "col", None),
    )
    out_specs = P("row", "col", None)
    return jax.shard_map(
        on_device, mesh=mesh, in_specs=in_specs, out_specs=out_specs, check_vma=False
    )
```

time: 237 us -> 207 us (0.87)
  Pallas kernels: 138 us -> 116 us
  starting transfers between devices: 59.4 us -> 46.1 us
  waiting for transfers between devices: 28.7 us -> 34.1 us
    pallas_call x4 -> x6, Pallas kernels: 128 us -> 106 us  [the longest x2 77.7 us: lattice_attend(): pl.pallas_call(functools.partial(lattice_kernel, head), grid=(count // QB...]
    all_to_all x2, waiting for transfers between devices: 13.6 us -> 34.1 us  [exchange(): lax.all_to_all(pieces, ('row', 'col'), split_axis=0, concat_axis=0, tiled...]
    ppermute x1, waiting for transfers between devices: 9.63 us -> 0.01 us  [on_device(): above = lax.ppermute(bottom, 'row', down)]
    ppermute x1, starting transfers between devices: 7.74 us -> 1.92 us  [on_device(): above = lax.ppermute(bottom, 'row', down)]
    ppermute x4 -> x6, starting transfers between devices: 19.5 us -> 15.2 us  [the longest x1 3.77 us: on_device(): lax.ppermute(corners(slice(tile_rows - HALO, None)), 'row', down)]
    all_to_all x2, starting transfers between devices: 24 us -> 20 us  [exchange(): lax.all_to_all(pieces, ('row', 'col'), split_axis=0, concat_axis=0, tiled...]
    ppermute x1, waiting for transfers between devices: 2.79 us -> 0.01 us  [on_device(): from_right = lax.ppermute(features[:, :HALO], 'col', left)]
    unnamed x13 -> x15, local copies, waits for them, and re-layouts: 0.2 us -> 2.7 us
  transfers between devices with their start and end apart: 10 -> 12, of which waited for: 5 -> 2; matrix products, arithmetic and copies ran while one was open for 3% -> 2% of each run, Pallas kernels for 55% -> 52%
where the time goes in v3:
time: 207 us; the launch traced here: 206 us
  Pallas kernels  116 us (56%)
  starting transfers between devices  46.1 us (22%)
  waiting for transfers between devices  34.1 us (16%)
  local copies, waits for them, and re-layouts  5.67 us (3%)
  other arithmetic  3.34 us (2%)
    pallas_call x2, Pallas kernels, lattice_attend(): pl.pallas_call(functools.partial(lattice_kernel, head), grid=(count // QB...  77.7 us
    all_to_all x2, waiting for transfers between devices, exchange(): lax.all_to_all(pieces, ('row', 'col'), split_axis=0, concat_axis=0, tiled...  34.1 us
    all_to_all x2, starting transfers between devices, exchange(): lax.all_to_all(pieces, ('row', 'col'), split_axis=0, concat_axis=0, tiled...  20 us
    pallas_call x1, Pallas kernels, windows(): pl.pallas_call(windows_kernel, in_specs=[smem, smem] + [free] * 5 + [vmem...  14.4 us
    pallas_call x1, Pallas kernels, project(): pl.pallas_call(project_kernel, grid=(steps,), in_specs=[whole(x.shape), p...  9.71 us
    pallas_call x1, Pallas kernels, blend(): pl.pallas_call(blend_kernel, in_specs=[free] * len(arrays), out_specs=fre...  7.39 us
    ppermute x1, starting transfers between devices, on_device(): from_left = lax.ppermute(features[:, tile_cols - HALO:], 'col', right)  4.41 us
    pallas_call x1, Pallas kernels, settle(): pl.pallas_call(settle_kernel, in_specs=[vmem] * 5, out_specs=[vmem] * 3,...  4.25 us
  transfers between devices with their start and end apart: 12, of which 2 were waited for; matrix products, arithmetic and copies ran while one was open for 2% of the time, Pallas kernels for 52%

profile of v3, /device:TPU:1, one launch (start us, length us, event | category | flops | bytes accessed | tf_op | source)
XLA Modules:
  0.0 205.8 jit_solution(1167108130929045970)
XLA Ops:
  0.0 1.5 fusion.1
  1.5 4.4 %collective-permute-start.1 = (bf16[32,8,1280]{2,1,0:T(8,128)(2,1)S(1)}, bf16[32,8,1280]{2,1,0:T(8,128)(2,1)S(1)}, u32[]{:S(2)}, u32[]{:S(2)}) collective-permute-start(bf16[32,8,1280]{2,1,0:T(8,128)(2,1)S(1)} %get-tuple-element.55), channel_id=1, source_target_pairs={{0,1},{1,2},{2,3},{3,4},{4,5},{5,6},{6,7},{7,8},{8,9},{9,10},{10,1... | collective-permute-start | bytes 1966088 | tf_op jit(solution)/shard_map/ppermute | solution.py:558
  5.9 1.3 collective-permute-start
  8.0 2.9 %collective-permute-start.3 = (bf16[8,16,1280]{2,1,0:T(8,128)(2,1)}, bf16[8,16,1280]{2,1,0:T(8,128)(2,1)}, u32[]{:S(2)}, u32[]{:S(2)}) collective-permute-start(bf16[8,16,1280]{2,1,0:T(8,128)(2,1)} %get-tuple-element.53), channel_id=1, source_target_pairs={{16,0},{32,16},{48,32},{64,48},{80,64},{96,80},{112,96},{17,1},{33... | collective-permute-start | bytes 983048 | tf_op jit(solution)/shard_map/ppermute | solution.py:560
  10.9 3.0 %collective-permute-start.2 = (bf16[8,16,1280]{2,1,0:T(8,128)(2,1)S(1)}, bf16[8,16,1280]{2,1,0:T(8,128)(2,1)}, u32[]{:S(2)}, u32[]{:S(2)}) collective-permute-start(bf16[8,16,1280]{2,1,0:T(8,128)(2,1)S(1)} %get-tuple-element.54), channel_id=1, source_target_pairs={{0,16},{16,32},{32,48},{48,64},{64,80},{80,96},{96,112},{1,17},{17... | collective-permute-start | bytes 983048 | tf_op jit(solution)/shard_map/ppermute | solution.py:559
  14.6 9.7 %project.1 = bf16[16,8,32,384]{3,2,1,0:T(8,128)(2,1)} custom-call(bf16[512,1280]{1,0:T(8,128)(2,1)} %bitcast.9, bf16[1280,1024]{1,0:T(8,128)(2,1)} %wq_hbm.1, bf16[1280,2048]{1,0:T(8,128)(2,1)} %wkv_hbm.1, bf16[1280,2048]{1,0:T(8,128)(2,1)} %wkv_hbm.1), custom_call_target="tpu_custom_call" | custom-call | flops 4026531840 | bytes 12320768 | tf_op jit(solution)/shard_map/project/pallas_call | solution.py:83
  25.2 3.8 %collective-permute-start.4 = (bf16[8,16,1280]{2,1,0:T(8,128)(2,1)}, bf16[8,16,1280]{2,1,0:T(8,128)(2,1)}, u32[]{:S(2)}, u32[]{:S(2)}) collective-permute-start(bf16[8,16,1280]{2,1,0:T(8,128)(2,1)} %pad_maximum_fusion.1), channel_id=1, source_target_pairs={{0,16},{16,32},{32,48},{48,64},{64,80},{80,96},{96,112},{1,17},{17... | collective-permute-start | bytes 983048 | tf_op jit(solution)/shard_map/ppermute | solution.py:569
  29.8 2.0 collective-permute-start.5
  31.8 10.9 %all-to-all-start = ((bf16[128,32,384]{2,1,0:T(8,128)(2,1)}), bf16[128,32,384]{2,1,0:T(8,128)(2,1)S(1)}, u32[]{:S(2)}, u32[]{:S(2)}) async-start(bf16[128,32,384]{2,1,0:T(8,128)(2,1)} %bitcast.11), calls=%async_computation | async-start | bytes 6291456 | tf_op jit(solution)/shard_map/all_to_all | solution.py:538
  43.5 14.4 %windows.1 = (bf16[8,32,1152]{2,1,0:T(8,128)(2,1)}, bf16[8,32,1152]{2,1,0:T(8,128)(2,1)}, bf16[32,16,1152]{2,1,0:T(8,128)(2,1)}, bf16[32,8,1152]{2,1,0:T(8,128)(2,1)}, bf16[32,8,1152]{2,1,0:T(8,128)(2,1)}) custom-call(s32[6,2]{1,0:T(8,128)} %copy.10.anchor, s32[6]{0:T(128)} %bitcast.20, bf16[32,16,1280]{2,1,0:T(8,128)(2,1)} %mid_hbm.1, ...), custom_call_target="tpu_custom_call" | custom-call | flops 135291469824 | bytes 11796480 | tf_op jit(solution)/shard_map/windows/pallas_call | solution.py:350
  57.8 1.9 collective-permute-start.6
  59.8 3.2 %collective-permute-start.7 = (bf16[8,32,1152]{2,1,0:T(8,128)(2,1)}, bf16[8,32,1152]{2,1,0:T(8,128)(2,1)}, u32[]{:S(2)}, u32[]{:S(2)}) collective-permute-start(bf16[8,32,1152]{2,1,0:T(8,128)(2,1)} %get-tuple-element.34), channel_id=1, source_target_pairs={{16,0},{32,16},{48,32},{64,48},{80,64},{96,80},{112,96},{17,1},{33... | collective-permute-start | bytes 1769480 | tf_op jit(solution)/shard_map/ppermute | solution.py:588
  63.0 20.6 %all-to-all-done = bf16[128,32,384]{2,1,0:T(8,128)(2,1)S(1)} async-done(((bf16[128,32,384]{2,1,0:T(8,128)(2,1)}), bf16[128,32,384]{2,1,0:T(8,128)(2,1)S(1)}, u32[]{:S(2)}, u32[]{:S(2)}) %all-to-all-start) | async-done | bytes 3145760 | tf_op jit(solution)/shard_map/all_to_all | solution.py:538
  83.6 1.6 copy-done.2
  85.2 38.6 %lattice_attend_0.1.refs_0_ = bf16[64,4096]{1,0:T(8,128)(2,1)} custom-call(bf16[4096,384]{1,0:T(8,128)(2,1)} %bitcast.13, bf16[4096,384]{1,0:T(8,128)(2,1)} %bitcast.14), custom_call_target="tpu_custom_call" | custom-call | flops 17179869184 | bytes 3145728 | tf_op jit(solution)/shard_map/lattice_attend_0/pallas_call | solution.py:197
  123.8 2.7 %fold.1 = (bf16[32,8,1152]{2,1,0:T(8,128)(2,1)}, bf16[32,8,1152]{2,1,0:T(8,128)(2,1)}) custom-call(bf16[32,8,1152]{2,1,0:T(8,128)(2,1)} %get-tuple-element.38.right_ref, bf16[32,8,1152]{2,1,0:T(8,128)(2,1)} %get-tuple-element.39.left_ref, bf16[8,32,1152]{2,1,0:T(8,128)(2,1)} %collective-permute-done.6.above_ref, ...), custom_call_target="tpu_custom_call" | custom-call | flops 294912 | bytes 3538944 | tf_op jit(solution)/shard_map/fold/pallas_call | solution.py:390
  126.5 2.0 collective-permute-start.8
  128.6 1.5 collective-permute-start.9
  130.1 39.1 %lattice_attend_1.1 = bf16[4096,128]{1,0:T(8,128)(2,1)} custom-call(bf16[4096,384]{1,0:T(8,128)(2,1)} %bitcast.15, bf16[4096,384]{1,0:T(8,128)(2,1)} %bitcast.16, bf16[64,4096]{1,0:T(8,128)(2,1)} %lattice_attend_0.1.refs_0_), custom_call_target="tpu_custom_call" | custom-call | flops 17179869184 | bytes 3145728 | tf_op jit(solution)/shard_map/lattice_attend_1/pallas_call | solution.py:197
  169.2 9.1 %all-to-all-start.1 = ((bf16[128,32,128]{2,1,0:T(8,128)(2,1)}), bf16[128,32,128]{2,1,0:T(8,128)(2,1)S(1)}, u32[]{:S(2)}, u32[]{:S(2)}) async-start(bf16[128,32,128]{2,1,0:T(8,128)(2,1)} %bitcast.18), calls=%async_computation.1 | async-start | bytes 2097152 | tf_op jit(solution)/shard_map/all_to_all | solution.py:538
  178.3 1.1 pad_maximum_fusion.beside_ref
  179.4 4.3 %settle.1 = (f32[512,1024]{1,0:T(8,128)}, f32[512,128]{1,0:T(8,128)}, f32[512,128]{1,0:T(8,128)}) custom-call(bf16[32,16,1152]{2,1,0:T(8,128)(2,1)} %get-tuple-element.32.mid_ref, bf16[8,32,1152]{2,1,0:T(8,128)(2,1)} %collective-permute-done.6.above_ref, bf16[8,32,1152]{2,1,0:T(8,128)(2,1)} %collective-permute-done.7.below_ref, ...), custom_call_target="tpu_custom_call" | custom-call | flops 77309411328 | bytes 7077888 | tf_op jit(solution)/shard_map/settle/pallas_call | solution.py:439
  183.7 13.5 %all-to-all-done.1 = bf16[128,32,128]{2,1,0:T(8,128)(2,1)S(1)} async-done(((bf16[128,32,128]{2,1,0:T(8,128)(2,1)}), bf16[128,32,128]{2,1,0:T(8,128)(2,1)S(1)}, u32[]{:S(2)}, u32[]{:S(2)}) %all-to-all-start.1) | async-done | bytes 1048608 | tf_op jit(solution)/shard_map/all_to_all | solution.py:538
  198.2 7.4 %blend.1 = bf16[512,1280]{1,0:T(8,128)(2,1)} custom-call(bf16[512,1280]{1,0:T(8,128)(2,1)} %bitcast.10, bf16[512,1280]{1,0:T(8,128)(2,1)} %bitcast.17, f32[512,128]{1,0:T(8,128)} %get-tuple-element.49.mask_hbm, bf16[16,8,32,128]{3,2,1,0:T(8,128)(2,1)} %bitcast.12, f32[512,1024]{1,0:T(8,128)} %get-tuple-element.51.sum_hbm, ...), custom_call_target="tpu_custom_call" | custom-call | flops 1879048192 | bytes 6553600 | tf_op jit(solution)/shard_map/blend/pallas_call | solution.py:515
  (30 shorter events, 4.8 us)
Async XLA Ops:
  0.0 7.2 %copy-start = (bf16[32,16,1280]{2,1,0:T(8,128)(2,1)S(1)}, bf16[32,16,1280]{2,1,0:T(8,128)(2,1)}, u32[]{:S(2)}) copy-start(bf16[32,16,1280]{2,1,0:T(8,128)(2,1)} %mid_hbm.1) | copy-start | bytes 3932164
  1.5 12.4 %copy-start.5 = (s32[32,16]{0,1:T(8,128)S(1)}, s32[32,16]{0,1:T(8,128)}, u32[]{:S(2)}) copy-start(s32[32,16]{0,1:T(8,128)} %param.10) | copy-start | bytes 6148
  1.5 22.8 %collective-permute-start.1 = (bf16[32,8,1280]{2,1,0:T(8,128)(2,1)S(1)}, bf16[32,8,1280]{2,1,0:T(8,128)(2,1)S(1)}, u32[]{:S(2)}, u32[]{:S(2)}) collective-permute-start(bf16[32,8,1280]{2,1,0:T(8,128)(2,1)S(1)} %get-tuple-element.55), channel_id=1, source_target_pairs={{0,1},{1,2},{2,3},{3,4},{4,5},{5,6},{6,7},{7,8},{8,9},{9,10},{10,1... | collective-permute-start | bytes 1966088 | tf_op jit(solution)/shard_map/ppermute | solution.py:558
  5.9 18.4 %collective-permute-start = (bf16[32,8,1280]{2,1,0:T(8,128)(2,1)S(1)}, bf16[32,8,1280]{2,1,0:T(8,128)(2,1)S(1)}, u32[]{:S(2)}, u32[]{:S(2)}) collective-permute-start(bf16[32,8,1280]{2,1,0:T(8,128)(2,1)S(1)} %get-tuple-element.56), channel_id=1, source_target_pairs={{1,0},{2,1},{3,2},{4,3},{5,4},{6,5},{7,6},{8,7},{9,8},{10,9},{11,1... | collective-permute-start | bytes 1966088 | tf_op jit(solution)/shard_map/ppermute | solution.py:557
  8.0 35.5 %collective-permute-start.3 = (bf16[8,16,1280]{2,1,0:T(8,128)(2,1)}, bf16[8,16,1280]{2,1,0:T(8,128)(2,1)}, u32[]{:S(2)}, u32[]{:S(2)}) collective-permute-start(bf16[8,16,1280]{2,1,0:T(8,128)(2,1)} %get-tuple-element.53), channel_id=1, source_target_pairs={{16,0},{32,16},{48,32},{64,48},{80,64},{96,80},{112,96},{17,1},{33... | collective-permute-start | bytes 983048 | tf_op jit(solution)/shard_map/ppermute | solution.py:560
  10.9 32.6 %collective-permute-start.2 = (bf16[8,16,1280]{2,1,0:T(8,128)(2,1)S(1)}, bf16[8,16,1280]{2,1,0:T(8,128)(2,1)}, u32[]{:S(2)}, u32[]{:S(2)}) collective-permute-start(bf16[8,16,1280]{2,1,0:T(8,128)(2,1)S(1)} %get-tuple-element.54), channel_id=1, source_target_pairs={{0,16},{16,32},{32,48},{48,64},{64,80},{80,96},{96,112},{1,17},{17... | collective-permute-start | bytes 983048 | tf_op jit(solution)/shard_map/ppermute | solution.py:559
  24.3 5.5 %copy-start.3 = (bf16[32,8,1280]{2,1,0:T(8,128)(2,1)}, bf16[32,8,1280]{2,1,0:T(8,128)(2,1)S(1)}, u32[]{:S(2)}) copy-start(bf16[32,8,1280]{2,1,0:T(8,128)(2,1)S(1)} %collective-permute-done.1.left_ref) | copy-start | bytes 1966084
  24.3 5.5 %copy-start.4 = (bf16[32,8,1280]{2,1,0:T(8,128)(2,1)}, bf16[32,8,1280]{2,1,0:T(8,128)(2,1)S(1)}, u32[]{:S(2)}) copy-start(bf16[32,8,1280]{2,1,0:T(8,128)(2,1)S(1)} %collective-permute-done.right_ref) | copy-start | bytes 1966084
  25.2 18.2 %collective-permute-start.4 = (bf16[8,16,1280]{2,1,0:T(8,128)(2,1)}, bf16[8,16,1280]{2,1,0:T(8,128)(2,1)}, u32[]{:S(2)}, u32[]{:S(2)}) collective-permute-start(bf16[8,16,1280]{2,1,0:T(8,128)(2,1)} %pad_maximum_fusion.1), channel_id=1, source_target_pairs={{0,16},{16,32},{32,48},{48,64},{64,80},{80,96},{96,112},{1,17},{17... | collective-permute-start | bytes 983048 | tf_op jit(solution)/shard_map/ppermute | solution.py:569
  29.8 13.0 %copy-start.6 = (s32[1,1,6,2]{2,3,1,0:T(2,128)S(1)}, s32[1,1,6,2]{2,3,1,0:T(2,128)}, u32[]{:S(2)}) copy-start(s32[1,1,6,2]{2,3,1,0:T(2,128)} %param.14) | copy-start | bytes 148
  29.8 13.7 %collective-permute-start.5 = (bf16[8,16,1280]{2,1,0:T(8,128)(2,1)}, bf16[8,16,1280]{2,1,0:T(8,128)(2,1)}, u32[]{:S(2)}, u32[]{:S(2)}) collective-permute-start(bf16[8,16,1280]{2,1,0:T(8,128)(2,1)} %pad_maximum_fusion.2), channel_id=1, source_target_pairs={{16,0},{32,16},{48,32},{64,48},{80,64},{96,80},{112,96},{17,1},{33... | collective-permute-start | bytes 983048 | tf_op jit(solution)/shard_map/ppermute | solution.py:570
  31.8 51.8 %all-to-all-start = ((bf16[128,32,384]{2,1,0:T(8,128)(2,1)}), bf16[128,32,384]{2,1,0:T(8,128)(2,1)S(1)}, u32[]{:S(2)}, u32[]{:S(2)}) async-start(bf16[128,32,384]{2,1,0:T(8,128)(2,1)} %bitcast.11), calls=%async_computation | async-start | bytes 6291456 | tf_op jit(solution)/shard_map/all_to_all | solution.py:538
  57.8 66.0 %collective-permute-start.6 = (bf16[8,32,1152]{2,1,0:T(8,128)(2,1)}, bf16[8,32,1152]{2,1,0:T(8,128)(2,1)}, u32[]{:S(2)}, u32[]{:S(2)}) collective-permute-start(bf16[8,32,1152]{2,1,0:T(8,128)(2,1)} %get-tuple-element.33), channel_id=1, source_target_pairs={{0,16},{16,32},{32,48},{48,64},{64,80},{80,96},{96,112},{1,17},{17... | collective-permute-start | bytes 1769480 | tf_op jit(solution)/shard_map/ppermute | solution.py:587
  59.8 64.0 %collective-permute-start.7 = (bf16[8,32,1152]{2,1,0:T(8,128)(2,1)}, bf16[8,32,1152]{2,1,0:T(8,128)(2,1)}, u32[]{:S(2)}, u32[]{:S(2)}) collective-permute-start(bf16[8,32,1152]{2,1,0:T(8,128)(2,1)} %get-tuple-element.34), channel_id=1, source_target_pairs={{16,0},{32,16},{48,32},{64,48},{80,64},{96,80},{112,96},{17,1},{33... | collective-permute-start | bytes 1769480 | tf_op jit(solution)/shard_map/ppermute | solution.py:588
  83.6 1.6 copy-start.2
  126.5 42.7 %collective-permute-start.8 = (bf16[32,8,1152]{2,1,0:T(8,128)(2,1)}, bf16[32,8,1152]{2,1,0:T(8,128)(2,1)S(1)}, u32[]{:S(2)}, u32[]{:S(2)}) collective-permute-start(bf16[32,8,1152]{2,1,0:T(8,128)(2,1)} %get-tuple-element.44), channel_id=1, source_target_pairs={{0,1},{1,2},{2,3},{3,4},{4,5},{5,6},{6,7},{7,8},{8,9},{9,10},{10,1... | collective-permute-start | bytes 1769480 | tf_op jit(solution)/shard_map/ppermute | solution.py:593
  128.6 40.6 %collective-permute-start.9 = (bf16[32,8,1152]{2,1,0:T(8,128)(2,1)}, bf16[32,8,1152]{2,1,0:T(8,128)(2,1)S(1)}, u32[]{:S(2)}, u32[]{:S(2)}) collective-permute-start(bf16[32,8,1152]{2,1,0:T(8,128)(2,1)} %get-tuple-element.45), channel_id=1, source_target_pairs={{1,0},{2,1},{3,2},{4,3},{5,4},{6,5},{7,6},{8,7},{9,8},{10,9},{11,1... | collective-permute-start | bytes 1769480 | tf_op jit(solution)/shard_map/ppermute | solution.py:594
  169.2 28.0 %all-to-all-start.1 = ((bf16[128,32,128]{2,1,0:T(8,128)(2,1)}), bf16[128,32,128]{2,1,0:T(8,128)(2,1)S(1)}, u32[]{:S(2)}, u32[]{:S(2)}) async-start(bf16[128,32,128]{2,1,0:T(8,128)(2,1)} %bitcast.18), calls=%async_computation.1 | async-start | bytes 2097152 | tf_op jit(solution)/shard_map/all_to_all | solution.py:538
  197.2 1.0 copy-start.1

commit v4 on v3

--- a/solution.py
+++ b/solution.py
@@ -37,7 +37,8 @@
     return pl.BlockSpec(shape, lambda *_: (0,) * len(shape), pipeline_mode=pl.Buffered(1))
 
 
-PARAMS = pltpu.CompilerParams(vmem_limit_bytes=60 * 2**20)
+def params(mebibytes=63):
+    return pltpu.CompilerParams(vmem_limit_bytes=mebibytes * 2**20)
 
 
 def lattice_order(count, by_row):
@@ -52,54 +53,82 @@
     return jnp.where(cell == row * tile_cols + col, 1.0, 0.0).astype(BF16)
 
 
-def project_kernel(x_ref, wq_ref, wk_ref, wv_ref, out_ref, ordered):
-    count = x_ref.shape[0]
-
-    @pl.when(pl.program_id(0) == 0)
-    def _():
-        ordered[...] = dot(lattice_order(count, True), x_ref[...]).astype(BF16)
-
-    x = ordered[...]
-    q, k, v = (dot(x, w_ref[...]) for w_ref in (wq_ref, wk_ref, wv_ref))
-    for g in range(2):
-        at = g * LANES
-        parts = [
-            jnp.concatenate([q[:, at : at + HD], k[:, at : at + HD]], 1),
-            v[:, at : at + LANES],
-            jnp.concatenate([q[:, at + HD : at + LANES], k[:, at + HD : at + LANES]], 1),
-        ]
-        for j, part in enumerate(parts):
-            out_ref[:, g, :, j * LANES : (j + 1) * LANES] = part.astype(BF16).reshape(
-                SUBS, count // SUBS, LANES
-            )
+def project_kernel(
+    x_hbm, wq_hbm, wkv_hbm, out_hbm, x_ref, wq_ref, wkv_ref, ordered, queries, out_ref, sems,
+    out_sems,
+):
+    count, channels = x_ref.shape
+    inner = wq_ref.shape[1]
+    width = 2 * LANES
+    x_copy = pltpu.make_async_copy(x_hbm, x_ref, sems.at[0])
+    x_copy.start()
+    weight_copies = [
+        pltpu.make_async_copy(source, target, sems.at[1 + i])
+        for i, (source, target) in enumerate(((wq_hbm, wq_ref), (wkv_hbm, wkv_ref)))
+    ]
+    for copy in weight_copies:
+        copy.start()
+    order = lattice_order(count, True)
+    x_copy.wait()
+    ordered[...] = dot(order, x_ref[...]).astype(BF16)
+    weight_copies[0].wait()
+    for c in range(0, inner, width):
+        queries[:, c : c + width] = dot(ordered[...], wq_ref[:, c : c + width])
+    weight_copies[1].wait()
+    leaving = []
+    for i, c in enumerate(range(0, inner, width)):
+        q = queries[:, c : c + width]
+        k = dot(ordered[...], wkv_ref[:, c : c + width])
+        v = dot(ordered[...], wkv_ref[:, inner + c : inner + c + width])
+        for g in range(2):
+            at = g * LANES
+            parts = [
+                jnp.concatenate([q[:, at : at + HD], k[:, at : at + HD]], 1),
+                v[:, at : at + LANES],
+                jnp.concatenate([q[:, at + HD : at + LANES], k[:, at + HD : at + LANES]], 1),
+            ]
+            for j, part in enumerate(parts):
+                out_ref[:, 2 * i + g, :, j * LANES : (j + 1) * LANES] = part.astype(BF16).reshape(
+                    SUBS, count // SUBS, LANES
+                )
+        groups = slice(2 * i, 2 * i + 2)
+        leaving.append(
+            pltpu.make_async_copy(out_ref.at[:, groups], out_hbm.at[:, groups], out_sems.at[i])
+        )
+        leaving[-1].start()
+    for copy in leaving:
+        copy.wait()
 
 
 def project(x, w_query, w_keyval):
     count, channels = x.shape
     inner = w_query.shape[1]
     groups = inner // LANES
-    steps = groups // 2
-    per_sub = count // SUBS
+    shape = (SUBS, groups, count // SUBS, 3 * LANES)
+    free = pl.BlockSpec(memory_space=pl.ANY)
     return pl.pallas_call(
         project_kernel,
-        grid=(steps,),
-        in_specs=[
-            whole(x.shape),
-            pl.BlockSpec((channels, 2 * LANES), lambda g: (0, g)),
-            pl.BlockSpec((channels, 2 * LANES), lambda g: (0, g)),
-            pl.BlockSpec((channels, 2 * LANES), lambda g: (0, g + steps)),
+        in_specs=[free] * 3,
+        out_specs=free,
+        out_shape=jax.ShapeDtypeStruct(shape, BF16),
+        scratch_shapes=[
+            pltpu.VMEM(x.shape, BF16),
+            pltpu.VMEM(w_query.shape, BF16),
+            pltpu.VMEM(w_keyval.shape, BF16),
+            pltpu.VMEM(x.shape, BF16),
+            pltpu.VMEM((count, inner), F32),
+            pltpu.VMEM(shape, BF16),
+            pltpu.SemaphoreType.DMA((3,)),
+            pltpu.SemaphoreType.DMA((groups // 2,)),
         ],
-        out_specs=pl.BlockSpec((SUBS, 2, per_sub, 3 * LANES), lambda g: (0, g, 0, 0)),
-        out_shape=jax.ShapeDtypeStruct((SUBS, groups, per_sub, 3 * LANES), BF16),
-        scratch_shapes=[pltpu.VMEM((count, channels), BF16)],
-        compiler_params=PARAMS,
+        compiler_params=params(61),
         cost_estimate=pl.CostEstimate(
             flops=2 * count * channels * 3 * inner,
             bytes_accessed=2 * (3 * channels * inner + count * channels + 3 * count * inner),
             transcendentals=0,
         ),
         name="project",
-    )(x, w_query, w_keyval, w_keyval)
+    )(x, w_query, w_keyval)
 
 
 def lattice_kernel(head, qk_ref, v_ref, *refs):
@@ -113,16 +142,18 @@
 
     @pl.when(step == 0)
     def _():
-        both = qk_ref[...].astype(F32)
-        q_t = both.T[:HD]
-        lane = lax.broadcasted_iota(jnp.int32, both.shape, 1)
-        k_norms = jnp.sum(jnp.where(lane < HD, 0.0, both * both), axis=1)
-        bound = jnp.max(jnp.sum(q_t * q_t, axis=0)) * jnp.max(k_norms)
+        row = lax.broadcasted_iota(jnp.int32, (LANES, LANES), 0)
+        lane = lax.broadcasted_iota(jnp.int32, (LANES, LANES), 1)
+        to_keys = jnp.where(row == lane + HD, 1.0, 0.0).astype(BF16)
+        queries_t[...] = dot_nt(to_keys, qk_ref[...]).astype(BF16)
+        own = (row[:HD] + head * HD == lane[:HD]).astype(F32).astype(BF16)
+        values_t[0:HD] = dot_nt(own, v_ref[...]).astype(BF16)
+        squares = qk_ref[...].astype(F32)
+        squares = (squares * squares).astype(BF16)
+        halves = ((row[:VROWS - HD] < 8) == (lane[:VROWS - HD] < HD)).astype(F32).astype(BF16)
+        norms = dot_nt(halves, squares)
+        bound = jnp.max(norms[:8]) * jnp.max(norms[8:]) * 1.02
         free[0] = (bound * (SCALE * SCALE) <= FREE_RANGE * FREE_RANGE).astype(jnp.int32)
-        queries_t[0:HD] = jnp.zeros((HD, count), BF16)
-        queries_t[HD:LANES] = q_t.astype(BF16)
-        v_t = v_ref[...].astype(F32).T
-        values_t[0:HD] = v_t[head * HD : (head + 1) * HD].astype(BF16)
         values_t[HD:VROWS] = jnp.ones((VROWS - HD, count), BF16)
 
     cols = pl.ds(pl.multiple_of(step * block, block), block)
@@ -205,7 +236,7 @@
             pltpu.VMEM((VROWS, count), BF16),
             pltpu.SMEM((1,), jnp.int32),
         ],
-        compiler_params=PARAMS,
+        compiler_params=params(63 if head else 61),
         cost_estimate=pl.CostEstimate(
             flops=4 * 4 * count * count * HD,
             bytes_accessed=6 * count * LANES,
@@ -216,7 +247,7 @@
 
 
 def windows_kernel(
-    anchor, weight, mid_hbm, before_hbm, after_hbm, side_before_hbm, side_after_hbm, right_ref, left_ref,
+    anchor, weight, mid_hbm, before_hbm, after_hbm, right_ref, left_ref,
     wq_hbm, wkv_hbm, top_out, bottom_out, mid_out, right_out, left_out, held, wq_ref, wkv_ref, mid_sum, side_sum, results_t, sems,
 ):
     channels, inner = wq_ref.shape
@@ -230,10 +261,8 @@
         for i, (source, target) in enumerate(
             (
                 (mid_hbm, held.at[HALO:end, 0:WIN]),
-                (before_hbm, held.at[0:HALO, 0:WIN]),
-                (after_hbm, held.at[end : end + HALO, 0:WIN]),
-                (side_before_hbm, held.at[0:HALO, WIN : 2 * WIN]),
-                (side_after_hbm, held.at[end : end + HALO, WIN : 2 * WIN]),
+                (before_hbm, held.at[0:HALO]),
+                (after_hbm, held.at[end : end + HALO]),
             )
         )
     ]
@@ -251,7 +280,6 @@
         copy.start()
     mid_sum[...] = jnp.zeros(mid_sum.shape, F32)
     side_sum[...] = jnp.zeros(side_sum.shape, F32)
-    results_t[inner:wide] = jnp.ones((LANES, cells), BF16)
     for row in range(0, tile_rows, HALO):
         rows = slice(row, row + HALO)
         pair = (right_ref[rows].astype(F32), left_ref[rows].astype(F32))
@@ -263,28 +291,20 @@
     first = lax.broadcasted_iota(jnp.int32, (cells, LANES), 1) < HD
     ones = jnp.ones((VROWS - HD, cells), BF16)
 
-    def one_hot(window_dim, left):
-        shape = (cells, 2 * cells) if window_dim == 0 else (2 * cells, cells)
-        window = lax.broadcasted_iota(jnp.int32, shape, window_dim)
-        source = lax.broadcasted_iota(jnp.int32, shape, 1 - window_dim)
-        place = ((window & (WIN - 1)) + left) & (2 * WIN - 1)
-        held = (source & (WIN - 1)) + ((source >> 8) << 4)
-        same = (((window ^ source) & (cells - WIN)) == 0) & (place == held)
-        return jnp.where(same, 1.0, 0.0)
+    column = lax.broadcasted_iota(jnp.int32, (1, WIN, 1), 1)
+    across = lax.broadcasted_iota(jnp.int32, (cells, cells), 0)
+    along = lax.broadcasted_iota(jnp.int32, (cells, cells), 1)
+    diagonal = jnp.where(across == along, 1.0, 0.0)
 
     def one_window(slot, arriving):
-        top = anchor[slot, 0] + HALO
-        left = anchor[slot, 1]
+        top = anchor[0, slot] + HALO
+        left = anchor[1, slot]
         factor = weight[slot].astype(F32)
         rows = pl.ds(top, WIN)
-        source = jnp.concatenate(
-            [
-                held[rows, 0:WIN].reshape(cells, channels),
-                held[rows, WIN : 2 * WIN].reshape(cells, channels),
-            ],
-            0,
-        )
-        x = dot(one_hot(0, left).astype(BF16), source).astype(BF16)
+        in_mid = ((column >= left) & (column < left + WIN)).astype(F32)
+        own = in_mid.astype(BF16)
+        x = held[rows, 0:WIN] * own + held[rows, WIN : 2 * WIN] * (1 - own)
+        x = x.reshape(cells, channels)
 
         def project(g):
             for copy in arriving.get(g, ()):
@@ -313,9 +333,12 @@
                 later = project(g + 2 * LANES)
             for j in range(4):
                 mix(now[j], v_t, g, j)
-        placed = dot_nt((one_hot(1, left) * factor).astype(BF16), results_t[...])
-        mid_sum[rows] += placed[:cells].reshape(WIN, WIN, wide)
-        side_sum[rows] += placed[cells:].reshape(WIN, WIN, wide)
+        placed = dot_nt((diagonal * factor).astype(BF16), results_t[...]).reshape(WIN, WIN, inner)
+        mid_sum[rows, :, 0:inner] += placed * in_mid
+        side_sum[rows, :, 0:inner] += placed * (1.0 - in_mid)
+        cover = jnp.broadcast_to(in_mid * factor, (WIN, WIN, LANES))
+        mid_sum[rows, :, inner:wide] += cover
+        side_sum[rows, :, inner:wide] += factor - cover
 
     def later_window(slot, carry):
         one_window(slot, {})
@@ -333,7 +356,7 @@
 
 
 def windows(
-    mid, before, after, side_before, side_after, from_right, from_left, w_query, w_keyval, anchor, weight
+    mid, before, after, from_right, from_left, w_query, w_keyval, anchor, weight
 ):
     tile_rows, _, channels = mid.shape
     high = tile_rows + 2 * HALO
@@ -349,7 +372,7 @@
     cells = WIN * WIN
     return pl.pallas_call(
         windows_kernel,
-        in_specs=[smem, smem] + [free] * 5 + [vmem] * 2 + [free] * 2,
+        in_specs=[smem, smem] + [free] * 3 + [vmem] * 2 + [free] * 2,
         out_specs=[vmem] * 5,
         out_shape=[rim, rim, inside, edge, edge],
         scratch_shapes=[
@@ -358,10 +381,10 @@
             pltpu.VMEM(w_keyval.shape, BF16),
             pltpu.VMEM((high, WIN, wide), F32),
             pltpu.VMEM((high, WIN, wide), F32),
-            pltpu.VMEM((wide, cells), BF16),
-            pltpu.SemaphoreType.DMA((5 + 3 * (inner // (2 * LANES)),)),
+            pltpu.VMEM((inner, cells), BF16),
+            pltpu.SemaphoreType.DMA((3 + 3 * (inner // (2 * LANES)),)),
         ],
-        compiler_params=PARAMS,
+        compiler_params=params(61),
         cost_estimate=pl.CostEstimate(
             flops=8 * slots * 2 * cells * 3 * inner * (channels + 2 * cells),
             bytes_accessed=6 * channels * inner + 4 * high * WIN * channels,
@@ -369,30 +392,58 @@
         ),
         name="windows",
     )(
-        anchor, weight, mid, before, after, side_before, side_after, from_right, from_left,
+        anchor, weight, mid, before, after, from_right, from_left,
         w_query, w_keyval,
     )
 
 
-def fold_kernel(right_ref, left_ref, above_ref, below_ref, right_out, left_out):
-    tile_rows = right_ref.shape[0]
-    sides = [ref[:, WIN : 2 * WIN].astype(F32) for ref in (above_ref, below_ref)]
-    for j, (source, target) in enumerate(((right_ref, right_out), (left_ref, left_out))):
-        upper, lower = [side[:, j * HALO : (j + 1) * HALO] for side in sides]
-        target[0:HALO] = (source[0:HALO].astype(F32) + upper).astype(BF16)
-        target[HALO : tile_rows - HALO] = source[HALO : tile_rows - HALO]
-        last = slice(tile_rows - HALO, tile_rows)
-        target[last] = (source[last].astype(F32) + lower).astype(BF16)
+def fold_kernel(
+    right_hbm, left_hbm, above_hbm, below_hbm, right_out, left_out, edges, sides, sems, out_sems
+):
+    tile_rows = right_hbm.shape[0]
+    ends = (slice(0, HALO), slice(tile_rows - HALO, tile_rows))
+    targets = [out.at[end] for end in ends for out in (right_out, left_out)]
+    copies = [
+        pltpu.make_async_copy(source, target, sems.at[i])
+        for i, (source, target) in enumerate(
+            [(source.at[end], edges.at[2 * i + j])
+             for i, end in enumerate(ends) for j, source in enumerate((right_hbm, left_hbm))]
+            + [(source.at[:, WIN : 2 * WIN], sides.at[i])
+               for i, source in enumerate((above_hbm, below_hbm))]
+        )
+    ]
+    for copy in copies:
+        copy.start()
+    for copy in copies:
+        copy.wait()
+    leaving = []
+    for i in range(2):
+        side = sides[i].astype(F32)
+        for j in range(2):
+            at = 2 * i + j
+            edges[at] = (edges[at].astype(F32) + side[:, j * HALO : (j + 1) * HALO]).astype(BF16)
+            leaving.append(pltpu.make_async_copy(edges.at[at], targets[at], out_sems.at[at]))
+            leaving[-1].start()
+    for copy in leaving:
+        copy.wait()
 
 
 def fold(on_right, on_left, above, below):
-    vmem = pl.BlockSpec(memory_space=pltpu.VMEM)
+    wide = on_right.shape[-1]
+    free = pl.BlockSpec(memory_space=pl.ANY)
     return pl.pallas_call(
         fold_kernel,
-        in_specs=[vmem] * 4,
-        out_specs=[vmem] * 2,
+        in_specs=[free] * 4,
+        out_specs=[free] * 2,
         out_shape=[jax.ShapeDtypeStruct(a.shape, a.dtype) for a in (on_right, on_left)],
-        compiler_params=PARAMS,
+        input_output_aliases={0: 0, 1: 1},
+        scratch_shapes=[
+            pltpu.VMEM((4, HALO, HALO, wide), BF16),
+            pltpu.VMEM((2, HALO, WIN, wide), BF16),
+            pltpu.SemaphoreType.DMA((6,)),
+            pltpu.SemaphoreType.DMA((4,)),
+        ],
+        compiler_params=params(61),
         cost_estimate=pl.CostEstimate(
             flops=on_right.size, bytes_accessed=12 * on_right.size, transcendentals=0
         ),
@@ -401,18 +452,17 @@
 
 
 def settle_kernel(
-    mid_ref, above_ref, below_ref, beside_ref, mask_ref, sum_ref, share_ref, wide_mask_ref
+    mid_ref, above_ref, below_ref, beside_ref, mask_ref, x_ref, known_ref, w_ref, base_ref, share_ref, own
 ):
-    count, inner = sum_ref.shape
-    tile_rows, tile_cols = mask_ref.shape
+    count, inner = own.shape
+    tile_cols, tile_rows = mask_ref.shape
     cell = lax.broadcasted_iota(jnp.int32, (count, tile_rows), 0)
     row = lax.broadcasted_iota(jnp.int32, (count, tile_rows), 1)
     pick_row = jnp.where(cell // tile_cols == row, 1.0, 0.0).astype(BF16)
-    in_row = dot(pick_row, mask_ref[...].astype(BF16))
+    in_row = dot_nt(pick_row, mask_ref[...].astype(F32).astype(BF16))
     cell = lax.broadcasted_iota(jnp.int32, (count, tile_cols), 0)
     col = lax.broadcasted_iota(jnp.int32, (count, tile_cols), 1)
-    own = jnp.sum(jnp.where(cell % tile_cols == col, in_row, 0.0), axis=1, keepdims=True)
-    wide_mask_ref[...] = jnp.broadcast_to(own, wide_mask_ref.shape)
+    known_cell = jnp.sum(jnp.where(cell % tile_cols == col, in_row, 0.0), axis=1, keepdims=True) == 1
 
     def total(lanes):
         upper = above_ref[:, 0:WIN, lanes].astype(F32)
@@ -426,78 +476,67 @@
         return jnp.concatenate(parts, 0).reshape(count, LANES)
 
     share = 1.0 / (1.0 + total(slice(inner, inner + LANES)))
-    share_ref[...] = share
+    share_ref[...] = jnp.where(known_cell, 0.0, share)
     for g in range(0, inner, LANES):
         lanes = slice(g, g + LANES)
-        sum_ref[:, lanes] = total(lanes) * share
-
-
-def settle(mid, above, below, beside, mask):
+        own[:, lanes] = (total(lanes) * share).astype(BF16)
+    width = 2 * LANES
+    for c in range(0, base_ref.shape[1], width):
+        cols = slice(c, c + width)
+        y = x_ref[:, cols].astype(F32) + dot(own[...], w_ref[:, cols])
+        base_ref[:, cols] = jnp.where(known_cell, known_ref[:, cols].astype(F32), y)
+
+
+def settle(mid, above, below, beside, mask, x, known, w_out):
     tile_rows, tile_cols, wide = mid.shape
-    count = tile_rows * tile_cols
+    count, channels = x.shape
     vmem = pl.BlockSpec(memory_space=pltpu.VMEM)
     return pl.pallas_call(
         settle_kernel,
-        in_specs=[vmem] * 5,
-        out_specs=[vmem] * 3,
+        in_specs=[vmem] * 8,
+        out_specs=[vmem] * 2,
         out_shape=[
-            jax.ShapeDtypeStruct((count, wide - LANES), F32),
-            jax.ShapeDtypeStruct((count, LANES), F32),
+            jax.ShapeDtypeStruct((count, channels), F32),
             jax.ShapeDtypeStruct((count, LANES), F32),
         ],
-        compiler_params=PARAMS,
+        scratch_shapes=[pltpu.VMEM((count, wide - LANES), BF16)],
+        compiler_params=params(),
         cost_estimate=pl.CostEstimate(
             flops=2**17 * count * wide, bytes_accessed=12 * count * wide, transcendentals=0
         ),
         name="settle",
-    )(mid, above, below, beside, mask)
+    )(mid, above, below, beside, mask, x, known, w_out)
 
 
 def blend_kernel(
-    x_hbm, known_hbm, mask_hbm, mixed_hbm, sum_hbm, share_hbm, w_hbm, out_hbm,
-    x_ref, known_ref, mask_ref, mixed_ref, sum_ref, share_ref, w_ref, out_ref, blended, sems, out_sems,
+    mixed_hbm, share_hbm, base_hbm, w_hbm, out_hbm, mixed_ref, share_ref, base_ref, w_ref, out_ref,
+    blended, sems, out_sems,
 ):
-    count, channels = x_ref.shape
+    count, channels = base_ref.shape
     groups = mixed_ref.shape[1]
     width = 2 * LANES
-    blocks = [slice(c, c + width) for c in range(0, channels, width)]
-    whole_copies = [
+    copies = [
         pltpu.make_async_copy(source, target, sems.at[i])
         for i, (source, target) in enumerate(
-            (
-                (mixed_hbm, mixed_ref),
-                (share_hbm, share_ref),
-                (sum_hbm, sum_ref),
-                (mask_hbm, mask_ref),
-            )
+            ((mixed_hbm, mixed_ref), (share_hbm, share_ref), (w_hbm, w_ref), (base_hbm, base_ref))
         )
     ]
-    block_copies = [
-        [
-            pltpu.make_async_copy(source.at[:, cols], target.at[:, cols], sems.at[4 + 3 * i + j])
-            for j, (source, target) in enumerate(
-                ((w_hbm, w_ref), (x_hbm, x_ref), (known_hbm, known_ref))
-            )
-        ]
-        for i, cols in enumerate(blocks)
-    ]
-    for copy in whole_copies + sum(block_copies, []):
+    for copy in copies:
         copy.start()
     back = lattice_order(count, False)
-    for copy in whole_copies:
+    for copy in copies[:2]:
         copy.wait()
     share = jnp.concatenate([share_ref[...]] * 2, 1)
     for g in range(0, groups, 2):
         lanes = slice(g * LANES, (g + 2) * LANES)
         mixed = jnp.concatenate([mixed_ref[:, g + j].reshape(count, LANES) for j in range(2)], 1)
-        blended[:, lanes] = (dot(back, mixed) * share + sum_ref[:, lanes]).astype(BF16)
-    known_cell = jnp.concatenate([mask_ref[...]] * 2, 1) == 1
+        blended[:, lanes] = (dot(back, mixed) * share).astype(BF16)
+    for copy in copies[2:]:
+        copy.wait()
     outs = []
-    for i, cols in enumerate(blocks):
-        for copy in block_copies[i]:
-            copy.wait()
-        y = (x_ref[:, cols].astype(F32) + dot(blended[...], w_ref[:, cols])).astype(BF16)
-        out_ref[:, cols] = jnp.where(known_cell, known_ref[:, cols], y)
+    for i, c in enumerate(range(0, channels, width)):
+        cols = slice(c, c + width)
+        out_ref[:, cols] = (base_ref[:, cols] + dot(blended[...], w_ref[:, cols])).astype(BF16)
         outs.append(
             pltpu.make_async_copy(out_ref.at[:, cols], out_hbm.at[:, cols], out_sems.at[i])
         )
@@ -506,12 +545,11 @@
         copy.wait()
 
 
-def blend(x, known, mask, mixed, windowed, share, w_out):
-    count, channels = x.shape
+def blend(mixed, share, base, w_out):
+    count, channels = base.shape
     inner = w_out.shape[0]
-    arrays = (x, known, mask, mixed, windowed, share, w_out)
+    arrays = (mixed, share, base, w_out)
     free = pl.BlockSpec(memory_space=pl.ANY)
-    blocks = channels // (2 * LANES)
     return pl.pallas_call(
         blend_kernel,
         in_specs=[free] * len(arrays),
@@ -521,10 +559,10 @@
         + [
             pltpu.VMEM((count, channels), BF16),
             pltpu.VMEM((count, inner), BF16),
-            pltpu.SemaphoreType.DMA((4 + 3 * blocks,)),
-            pltpu.SemaphoreType.DMA((blocks,)),
+            pltpu.SemaphoreType.DMA((len(arrays),)),
+            pltpu.SemaphoreType.DMA((channels // (2 * LANES),)),
         ],
-        compiler_params=PARAMS,
+        compiler_params=params(),
         cost_estimate=pl.CostEstimate(
             flops=2 * count * inner * (channels + count),
             bytes_accessed=2 * inner * channels + 6 * count * channels,
@@ -556,18 +594,14 @@
 
     from_right = lax.ppermute(features[:, :HALO], "col", left)
     from_left = lax.ppermute(features[:, tile_cols - HALO :], "col", right)
-    before = lax.ppermute(features[tile_rows - HALO :], "row", down)
-    after = lax.ppermute(features[:HALO], "row", up)
     pieces = project(x, w_query, w_keyval).reshape(devices, per_sub, 3 * LANES)
-    from_right, from_left, mask, anchors, _ = lax.optimization_barrier(
-        (from_right, from_left, known_mask.astype(F32), win_anchor.reshape(-1, 2), pieces)
-    )
-
-    def corners(rows):
-        return jnp.concatenate([from_right[rows], from_left[rows]], 1)
-
-    side_before = lax.ppermute(corners(slice(tile_rows - HALO, None)), "row", down)
-    side_after = lax.ppermute(corners(slice(0, HALO)), "row", up)
+    from_right, from_left, _ = lax.optimization_barrier((from_right, from_left, pieces))
+
+    def rows_of_halo(rows):
+        return jnp.concatenate([features[rows], from_right[rows], from_left[rows]], 1)
+
+    before = lax.ppermute(rows_of_halo(slice(tile_rows - HALO, None)), "row", down)
+    after = lax.ppermute(rows_of_halo(slice(0, HALO)), "row", up)
 
     gathered = exchange(pieces).reshape(devices * per_sub, 3 * LANES)
 
@@ -575,13 +609,11 @@
         features,
         before,
         after,
-        side_before,
-        side_after,
         from_right,
         from_left,
         w_query,
         w_keyval,
-        anchors,
+        win_anchor.reshape(-1, 2).T,
         win_weight.reshape(-1),
     )
     above = lax.ppermute(bottom, "row", down)
@@ -596,9 +628,11 @@
     mixed, on_first, on_last = lax.optimization_barrier((mixed, on_first, on_last))
     returned = exchange(mixed.reshape(devices, per_sub, LANES))
     arrived = jnp.concatenate([on_first, on_last], 1)
-    windowed, share, mask = settle(inside, above, below, arrived, mask)
+    base, share = settle(
+        inside, above, below, arrived, known_mask.T, x, known.reshape(count, channels), w_out
+    )
     returned = returned.reshape(SUBS, devices // SUBS, per_sub, LANES)
-    out = blend(x, known.reshape(count, channels), mask, returned, windowed, share, w_out)
+    out = blend(returned, share, base, w_out)
     return out.reshape(tile_rows, tile_cols, channels)
 
 

time: 207 us -> 202 us (0.976)
  Pallas kernels: 116 us -> 110 us
  starting transfers between devices: 46.1 us -> 49.7 us
    ppermute x1, starting transfers between devices: 1.92 us -> 10.8 us  [on_device(): above = lax.ppermute(bottom, 'row', down)]
    all_to_all x2, waiting for transfers between devices: 34.1 us -> 26.1 us  [exchange(): lax.all_to_all(pieces, ('row', 'col'), split_axis=0, concat_axis=0, tiled...]
    ppermute x4 -> x2, starting transfers between devices: 11.7 us -> 6.79 us  [the longest x1 4.87 us: on_device(): lax.ppermute(rows_of_halo(slice(tile_rows - HALO, None)), 'row', down)]
    ppermute x1, waiting for transfers between devices: 0.01 us -> 4.72 us  [on_device(): from_right = lax.ppermute(features[:, :HALO], 'col', left)]
    pallas_call x4, Pallas kernels: 31.1 us -> 27.3 us  [the longest x1 9.99 us: windows(): pl.pallas_call(windows_kernel, in_specs=[smem, smem] + [free] * 3 + [vmem...]
    ppermute x1, waiting for transfers between devices: 0.01 us -> 3.14 us  [on_device(): from_left = lax.ppermute(features[:, tile_cols - HALO:], 'col', right)]
  transfers between devices with their start and end apart: 12 -> 10, of which waited for: 2 -> 4; matrix products, arithmetic and copies ran while one was open for 2% -> 1% of each run, Pallas kernels for 52% -> 51%
where the time goes in v4:
time: 202 us; the launch traced here: 201 us
  Pallas kernels  110 us (54%)
  starting transfers between devices  49.7 us (25%)
  waiting for transfers between devices  33.9 us (17%)
  local copies, waits for them, and re-layouts  4.75 us (2%)
  other arithmetic  2.26 us (1%)
    pallas_call x2, Pallas kernels, lattice_attend(): pl.pallas_call(functools.partial(lattice_kernel, head), grid=(count // QB...  77.5 us
    all_to_all x2, waiting for transfers between devices, exchange(): lax.all_to_all(pieces, ('row', 'col'), split_axis=0, concat_axis=0, tiled...  26.1 us
    all_to_all x2, starting transfers between devices, exchange(): lax.all_to_all(pieces, ('row', 'col'), split_axis=0, concat_axis=0, tiled...  20.2 us
    ppermute x1, starting transfers between devices, on_device(): above = lax.ppermute(bottom, 'row', down)  10.8 us
    pallas_call x1, Pallas kernels, windows(): pl.pallas_call(windows_kernel, in_specs=[smem, smem] + [free] * 3 + [vmem...  9.99 us
    pallas_call x1, Pallas kernels, project(): pl.pallas_call(project_kernel, in_specs=[free] * 3, out_specs=free, out_s...  8.04 us
    pallas_call x1, Pallas kernels, settle(): pl.pallas_call(settle_kernel, in_specs=[vmem] * 8, out_specs=[vmem] * 2,...  7 us
    pallas_call x1, Pallas kernels, blend(): pl.pallas_call(blend_kernel, in_specs=[free] * len(arrays), out_specs=fre...  5.5 us
  transfers between devices with their start and end apart: 10, of which 4 were waited for; matrix products, arithmetic and copies ran while one was open for 1% of the time, Pallas kernels for 51%

profile of v4, /device:TPU:1, one launch (start us, length us, event | category | flops | bytes accessed | tf_op | source)
XLA Modules:
  0.0 201.4 jit_solution(16943412438357943693)
XLA Ops:
  0.0 1.4 fusion.1
  1.4 5.2 %collective-permute-start.1 = (bf16[32,8,1280]{2,1,0:T(8,128)(2,1)S(1)}, bf16[32,8,1280]{2,1,0:T(8,128)(2,1)}, u32[]{:S(2)}, u32[]{:S(2)}) collective-permute-start(bf16[32,8,1280]{2,1,0:T(8,128)(2,1)S(1)} %get-tuple-element.49), channel_id=1, source_target_pairs={{0,1},{1,2},{2,3},{3,4},{4,5},{5,6},{6,7},{7,8},{8,9},{9,10},{10,1... | collective-permute-start | bytes 1966088 | tf_op jit(solution)/shard_map/ppermute | solution.py:596
  6.6 1.3 collective-permute-start
  7.9 8.0 %project.1 = bf16[16,8,32,384]{3,2,1,0:T(8,128)(2,1)} custom-call(bf16[512,1280]{1,0:T(8,128)(2,1)} %bitcast.12, bf16[1280,1024]{1,0:T(8,128)(2,1)} %wq_hbm.3, bf16[1280,2048]{1,0:T(8,128)(2,1)} %wkv_hbm.3), custom_call_target="tpu_custom_call" | custom-call | flops 4026531840 | bytes 12320768 | tf_op jit(solution)/shard_map/project/pallas_call | solution.py:109
  16.0 3.1 %collective-permute-done.1.left_ref = bf16[32,8,1280]{2,1,0:T(8,128)(2,1)} collective-permute-done((bf16[32,8,1280]{2,1,0:T(8,128)(2,1)S(1)}, bf16[32,8,1280]{2,1,0:T(8,128)(2,1)}, u32[]{:S(2)}, u32[]{:S(2)}) %collective-permute-start.1) | collective-permute-done | bytes 655392 | tf_op jit(solution)/shard_map/ppermute | solution.py:596
  19.1 4.7 %collective-permute-done.right_ref = bf16[32,8,1280]{2,1,0:T(8,128)(2,1)} collective-permute-done((bf16[32,8,1280]{2,1,0:T(8,128)(2,1)S(1)}, bf16[32,8,1280]{2,1,0:T(8,128)(2,1)}, u32[]{:S(2)}, u32[]{:S(2)}) %collective-permute-start) | collective-permute-done | bytes 655392 | tf_op jit(solution)/shard_map/ppermute | solution.py:595
  23.9 1.2 fusion.2
  25.1 4.9 %collective-permute-start.2 = (bf16[8,32,1280]{2,1,0:T(8,128)(2,1)S(1)}, bf16[8,32,1280]{2,1,0:T(8,128)(2,1)S(1)}, u32[]{:S(2)}, u32[]{:S(2)}) collective-permute-start(bf16[8,32,1280]{2,1,0:T(8,128)(2,1)S(1)} %pad_maximum_fusion.1), channel_id=1, source_target_pairs={{0,16},{16,32},{32,48},{48,64},{64,80},{80,96},{96,112},{1,17},{17... | collective-permute-start | bytes 1966088 | tf_op jit(solution)/shard_map/ppermute | solution.py:603
  30.0 1.9 collective-permute-start.3
  32.0 10.7 %all-to-all-start = ((bf16[128,32,384]{2,1,0:T(8,128)(2,1)}), bf16[128,32,384]{2,1,0:T(8,128)(2,1)}, u32[]{:S(2)}, u32[]{:S(2)}) async-start(bf16[128,32,384]{2,1,0:T(8,128)(2,1)} %bitcast.1), calls=%async_computation | async-start | bytes 6291456 | tf_op jit(solution)/shard_map/all_to_all | solution.py:576
  43.8 10.0 %windows.1 = (bf16[8,32,1152]{2,1,0:T(8,128)(2,1)}, bf16[8,32,1152]{2,1,0:T(8,128)(2,1)}, bf16[32,16,1152]{2,1,0:T(8,128)(2,1)}, bf16[32,8,1152]{2,1,0:T(8,128)(2,1)}, bf16[32,8,1152]{2,1,0:T(8,128)(2,1)}) custom-call(s32[2,6]{1,0:T(2,128)} %bitcast.17, s32[6]{0:T(128)} %bitcast.18, bf16[32,16,1280]{2,1,0:T(8,128)(2,1)} %mid_hbm.1, ...), custom_call_target="tpu_custom_call" | custom-call | flops 135291469824 | bytes 11796480 | tf_op jit(solution)/shard_map/windows/pallas_call | solution.py:373
  53.8 10.8 %collective-permute-start.4 = (bf16[8,32,1152]{2,1,0:T(8,128)(2,1)}, bf16[8,32,1152]{2,1,0:T(8,128)(2,1)S(1)}, u32[]{:S(2)}, u32[]{:S(2)}) collective-permute-start(bf16[8,32,1152]{2,1,0:T(8,128)(2,1)} %get-tuple-element.28), channel_id=1, source_target_pairs={{0,16},{16,32},{32,48},{48,64},{64,80},{80,96},{96,112},{1,17},{17... | collective-permute-start | bytes 1769480 | tf_op jit(solution)/shard_map/ppermute | solution.py:619
  64.6 1.9 collective-permute-start.5
  66.6 16.7 %all-to-all-done = bf16[128,32,384]{2,1,0:T(8,128)(2,1)} async-done(((bf16[128,32,384]{2,1,0:T(8,128)(2,1)}), bf16[128,32,384]{2,1,0:T(8,128)(2,1)}, u32[]{:S(2)}, u32[]{:S(2)}) %all-to-all-start) | async-done | bytes 3145760 | tf_op jit(solution)/shard_map/all_to_all | solution.py:576
  83.3 38.5 %lattice_attend_0.1.refs_0_ = bf16[64,4096]{1,0:T(8,128)(2,1)} custom-call(bf16[4096,384]{1,0:T(8,128)(2,1)} %bitcast.2.qk_ref.v_ref, bf16[4096,384]{1,0:T(8,128)(2,1)} %bitcast.2.qk_ref.v_ref), custom_call_target="tpu_custom_call" | custom-call | flops 17179869184 | bytes 3145728 | tf_op jit(solution)/shard_map/lattice_attend_0/pallas_call | solution.py:228
  122.8 2.3 %fold.1 = (bf16[32,8,1152]{2,1,0:T(8,128)(2,1)}, bf16[32,8,1152]{2,1,0:T(8,128)(2,1)}) custom-call(bf16[32,8,1152]{2,1,0:T(8,128)(2,1)} %get-tuple-element.31.right_hbm, bf16[32,8,1152]{2,1,0:T(8,128)(2,1)} %get-tuple-element.32.left_hbm, bf16[8,32,1152]{2,1,0:T(8,128)(2,1)} %copy-done.1, ...), custom_call_target="tpu_custom_call", output_to_operand_aliasing={{0}: (0, {}), {1}: (1, {})} | custom-call | flops 294912 | bytes 3538944 | tf_op jit(solution)/shard_map/fold/pallas_call | solution.py:434
  125.1 2.0 collective-permute-start.6
  127.1 1.5 collective-permute-start.7
  128.6 39.0 %lattice_attend_1.1 = bf16[4096,128]{1,0:T(8,128)(2,1)} custom-call(bf16[4096,384]{1,0:T(8,128)(2,1)} %bitcast.2.qk_ref.v_ref, bf16[4096,384]{1,0:T(8,128)(2,1)} %bitcast.2.qk_ref.v_ref, bf16[64,4096]{1,0:T(8,128)(2,1)} %lattice_attend_0.1.refs_0_), custom_call_target="tpu_custom_call" | custom-call | flops 17179869184 | bytes 3145728 | tf_op jit(solution)/shard_map/lattice_attend_1/pallas_call | solution.py:228
  167.7 9.5 %all-to-all-start.1 = ((bf16[128,32,128]{2,1,0:T(8,128)(2,1)}), bf16[128,32,128]{2,1,0:T(8,128)(2,1)}, u32[]{:S(2)}, u32[]{:S(2)}) async-start(bf16[128,32,128]{2,1,0:T(8,128)(2,1)} %bitcast.14), calls=%async_computation.1 | async-start | bytes 2097152 | tf_op jit(solution)/shard_map/all_to_all | solution.py:576
  177.2 2.2 %pad_maximum_fusion.beside_ref = bf16[32,16,1152]{2,1,0:T(8,128)(2,1)} fusion(bf16[32,8,1152]{2,1,0:T(8,128)(2,1)} %collective-permute-done.7, bf16[32,8,1152]{2,1,0:T(8,128)(2,1)S(1)} %collective-permute-done.6), kind=kLoop, calls=%fused_computation | loop fusion | flops 2359296 | bytes 2359296 | tf_op jit(solution)/shard_map/concatenate | solution.py:630
  179.4 7.0 %settle.1 = (f32[512,1280]{1,0:T(8,128)}, f32[512,128]{1,0:T(8,128)}) custom-call(bf16[32,16,1152]{2,1,0:T(8,128)(2,1)} %get-tuple-element.42.mid_ref, bf16[8,32,1152]{2,1,0:T(8,128)(2,1)} %copy-done.1, bf16[8,32,1152]{2,1,0:T(8,128)(2,1)} %copy-done.2, bf16[32,16,1152]{2,1,0:T(8,128)(2,1)} %pad_maximum_fusion.beside_ref, s32[16,32]{1,0:T(8,128)} %bitcast.16, ...), custom_call_target="tpu_custom_call" | custom-call | flops 77309411328 | bytes 7077888 | tf_op jit(solution)/shard_map/settle/pallas_call | solution.py:494
  186.4 9.4 %all-to-all-done.1 = bf16[128,32,128]{2,1,0:T(8,128)(2,1)} async-done(((bf16[128,32,128]{2,1,0:T(8,128)(2,1)}), bf16[128,32,128]{2,1,0:T(8,128)(2,1)}, u32[]{:S(2)}, u32[]{:S(2)}) %all-to-all-start.1) | async-done | bytes 1048608 | tf_op jit(solution)/shard_map/all_to_all | solution.py:576
  195.7 5.5 %blend.1 = bf16[512,1280]{1,0:T(8,128)(2,1)} custom-call(bf16[16,8,32,128]{3,2,1,0:T(8,128)(2,1)} %bitcast.7.mixed_hbm, f32[512,128]{1,0:T(8,128)} %get-tuple-element.45.share_hbm, f32[512,1280]{1,0:T(8,128)} %get-tuple-element.46.base_hbm, bf16[1024,1280]{1,0:T(8,128)(2,1)} %w_hbm.1), custom_call_target="tpu_custom_call" | custom-call | flops 1879048192 | bytes 6553600 | tf_op jit(solution)/shard_map/blend/pallas_call | solution.py:553
  (19 shorter events, 2.3 us)
Async XLA Ops:
  1.4 17.8 %collective-permute-start.1 = (bf16[32,8,1280]{2,1,0:T(8,128)(2,1)S(1)}, bf16[32,8,1280]{2,1,0:T(8,128)(2,1)}, u32[]{:S(2)}, u32[]{:S(2)}) collective-permute-start(bf16[32,8,1280]{2,1,0:T(8,128)(2,1)S(1)} %get-tuple-element.49), channel_id=1, source_target_pairs={{0,1},{1,2},{2,3},{3,4},{4,5},{5,6},{6,7},{7,8},{8,9},{9,10},{10,1... | collective-permute-start | bytes 1966088 | tf_op jit(solution)/shard_map/ppermute | solution.py:596
  6.6 17.3 %collective-permute-start = (bf16[32,8,1280]{2,1,0:T(8,128)(2,1)S(1)}, bf16[32,8,1280]{2,1,0:T(8,128)(2,1)}, u32[]{:S(2)}, u32[]{:S(2)}) collective-permute-start(bf16[32,8,1280]{2,1,0:T(8,128)(2,1)S(1)} %get-tuple-element.50), channel_id=1, source_target_pairs={{1,0},{2,1},{3,2},{4,3},{5,4},{6,5},{7,6},{8,7},{9,8},{10,9},{11,1... | collective-permute-start | bytes 1966088 | tf_op jit(solution)/shard_map/ppermute | solution.py:595
  7.9 8.1 %copy-start = (bf16[32,16,1280]{2,1,0:T(8,128)(2,1)S(1)}, bf16[32,16,1280]{2,1,0:T(8,128)(2,1)}, u32[]{:S(2)}) copy-start(bf16[32,16,1280]{2,1,0:T(8,128)(2,1)} %mid_hbm.1) | copy-start | bytes 3932164
  25.1 17.6 %collective-permute-start.2 = (bf16[8,32,1280]{2,1,0:T(8,128)(2,1)S(1)}, bf16[8,32,1280]{2,1,0:T(8,128)(2,1)S(1)}, u32[]{:S(2)}, u32[]{:S(2)}) collective-permute-start(bf16[8,32,1280]{2,1,0:T(8,128)(2,1)S(1)} %pad_maximum_fusion.1), channel_id=1, source_target_pairs={{0,16},{16,32},{32,48},{48,64},{64,80},{80,96},{96,112},{1,17},{17... | collective-permute-start | bytes 1966088 | tf_op jit(solution)/shard_map/ppermute | solution.py:603
  30.0 12.7 %collective-permute-start.3 = (bf16[8,32,1280]{2,1,0:T(8,128)(2,1)S(1)}, bf16[8,32,1280]{2,1,0:T(8,128)(2,1)S(1)}, u32[]{:S(2)}, u32[]{:S(2)}) collective-permute-start(bf16[8,32,1280]{2,1,0:T(8,128)(2,1)S(1)} %pad_maximum_fusion.2), channel_id=1, source_target_pairs={{16,0},{32,16},{48,32},{64,48},{80,64},{96,80},{112,96},{17,1},{33... | collective-permute-start | bytes 1966088 | tf_op jit(solution)/shard_map/ppermute | solution.py:604
  32.0 51.3 %all-to-all-start = ((bf16[128,32,384]{2,1,0:T(8,128)(2,1)}), bf16[128,32,384]{2,1,0:T(8,128)(2,1)}, u32[]{:S(2)}, u32[]{:S(2)}) async-start(bf16[128,32,384]{2,1,0:T(8,128)(2,1)} %bitcast.1), calls=%async_computation | async-start | bytes 6291456 | tf_op jit(solution)/shard_map/all_to_all | solution.py:576
  42.7 0.9 copy-start.3
  42.7 1.1 copy-start.4
  53.8 67.9 %collective-permute-start.4 = (bf16[8,32,1152]{2,1,0:T(8,128)(2,1)}, bf16[8,32,1152]{2,1,0:T(8,128)(2,1)S(1)}, u32[]{:S(2)}, u32[]{:S(2)}) collective-permute-start(bf16[8,32,1152]{2,1,0:T(8,128)(2,1)} %get-tuple-element.28), channel_id=1, source_target_pairs={{0,16},{16,32},{32,48},{48,64},{64,80},{80,96},{96,112},{1,17},{17... | collective-permute-start | bytes 1769480 | tf_op jit(solution)/shard_map/ppermute | solution.py:619
  64.6 57.1 %collective-permute-start.5 = (bf16[8,32,1152]{2,1,0:T(8,128)(2,1)}, bf16[8,32,1152]{2,1,0:T(8,128)(2,1)S(1)}, u32[]{:S(2)}, u32[]{:S(2)}) collective-permute-start(bf16[8,32,1152]{2,1,0:T(8,128)(2,1)} %get-tuple-element.29), channel_id=1, source_target_pairs={{16,0},{32,16},{48,32},{64,48},{80,64},{96,80},{112,96},{17,1},{33... | collective-permute-start | bytes 1769480 | tf_op jit(solution)/shard_map/ppermute | solution.py:620
  121.8 0.8 copy-start.1
  121.8 1.0 copy-start.2
  125.1 42.5 %collective-permute-start.6 = (bf16[32,8,1152]{2,1,0:T(8,128)(2,1)}, bf16[32,8,1152]{2,1,0:T(8,128)(2,1)S(1)}, u32[]{:S(2)}, u32[]{:S(2)}) collective-permute-start(bf16[32,8,1152]{2,1,0:T(8,128)(2,1)} %get-tuple-element.39), channel_id=1, source_target_pairs={{0,1},{1,2},{2,3},{3,4},{4,5},{5,6},{6,7},{7,8},{8,9},{9,10},{10,1... | collective-permute-start | bytes 1769480 | tf_op jit(solution)/shard_map/ppermute | solution.py:625
  127.1 40.6 %collective-permute-start.7 = (bf16[32,8,1152]{2,1,0:T(8,128)(2,1)}, bf16[32,8,1152]{2,1,0:T(8,128)(2,1)}, u32[]{:S(2)}, u32[]{:S(2)}) collective-permute-start(bf16[32,8,1152]{2,1,0:T(8,128)(2,1)} %get-tuple-element.40), channel_id=1, source_target_pairs={{1,0},{2,1},{3,2},{4,3},{5,4},{6,5},{7,6},{8,7},{9,8},{10,9},{11,1... | collective-permute-start | bytes 1769480 | tf_op jit(solution)/shard_map/ppermute | solution.py:626
  167.7 28.1 %all-to-all-start.1 = ((bf16[128,32,128]{2,1,0:T(8,128)(2,1)}), bf16[128,32,128]{2,1,0:T(8,128)(2,1)}, u32[]{:S(2)}, u32[]{:S(2)}) async-start(bf16[128,32,128]{2,1,0:T(8,128)(2,1)} %bitcast.14), calls=%async_computation.1 | async-start | bytes 2097152 | tf_op jit(solution)/shard_map/all_to_all | solution.py:576

commit v5 on v4

--- a/solution.py
+++ b/solution.py
@@ -247,8 +247,9 @@
 
 
 def windows_kernel(
-    anchor, weight, mid_hbm, before_hbm, after_hbm, right_ref, left_ref,
-    wq_hbm, wkv_hbm, top_out, bottom_out, mid_out, right_out, left_out, held, wq_ref, wkv_ref, mid_sum, side_sum, results_t, sems,
+    even, anchor, weight, mid_hbm, rows_1_hbm, rows_2_hbm, cols_1_ref, cols_2_ref,
+    wq_hbm, wkv_hbm, rim_1_out, rim_2_out, mid_out, ends_1_out, ends_2_out,
+    middle_1_out, middle_2_out, held, wq_ref, wkv_ref, mid_sum, side_sum, results_t, sems,
 ):
     channels, inner = wq_ref.shape
     cells = WIN * WIN
@@ -256,13 +257,16 @@
     tile_rows = mid_hbm.shape[0]
     end = tile_rows + HALO
     pair_lanes = 2 * LANES
+    row_even, col_even = even[0] == 1, even[1] == 1
+    rows_1 = pl.ds(jnp.where(row_even, end, 0), HALO)
+    rows_2 = pl.ds(jnp.where(row_even, 0, end), HALO)
     copies = [
         pltpu.make_async_copy(source, target, sems.at[i])
         for i, (source, target) in enumerate(
             (
                 (mid_hbm, held.at[HALO:end, 0:WIN]),
-                (before_hbm, held.at[0:HALO]),
-                (after_hbm, held.at[end : end + HALO]),
+                (rows_1_hbm, held.at[rows_1]),
+                (rows_2_hbm, held.at[rows_2]),
             )
         )
     ]
@@ -282,7 +286,8 @@
     side_sum[...] = jnp.zeros(side_sum.shape, F32)
     for row in range(0, tile_rows, HALO):
         rows = slice(row, row + HALO)
-        pair = (right_ref[rows].astype(F32), left_ref[rows].astype(F32))
+        pair = (cols_1_ref[rows].astype(F32), cols_2_ref[rows].astype(F32))
+        pair = (jnp.where(col_even, *pair), jnp.where(col_even, *pair[::-1]))
         held[HALO + row : 2 * HALO + row, WIN : 2 * WIN] = jnp.concatenate(pair, 1).astype(BF16)
     for copy in copies:
         copy.wait()
@@ -346,17 +351,22 @@
 
     one_window(0, weight_copies)
     lax.fori_loop(1, live, later_window, 0)
-    top_out[:, 0:WIN] = mid_sum[0:HALO].astype(BF16)
-    top_out[:, WIN : 2 * WIN] = side_sum[0:HALO].astype(BF16)
-    bottom_out[:, 0:WIN] = mid_sum[end : end + HALO].astype(BF16)
-    bottom_out[:, WIN : 2 * WIN] = side_sum[end : end + HALO].astype(BF16)
+    for out, rows in ((rim_1_out, rows_1), (rim_2_out, rows_2)):
+        out[:, 0:WIN] = mid_sum[rows].astype(BF16)
+        out[:, WIN : 2 * WIN] = side_sum[rows].astype(BF16)
     mid_out[...] = mid_sum[HALO:end].astype(BF16)
-    right_out[...] = side_sum[HALO:end, 0:HALO].astype(BF16)
-    left_out[...] = side_sum[HALO:end, HALO : 2 * HALO].astype(BF16)
+
+    def edges(rows):
+        right, left = side_sum[rows, 0:HALO], side_sum[rows, HALO : 2 * HALO]
+        return jnp.where(col_even, right, left).astype(BF16), jnp.where(col_even, left, right).astype(BF16)
+
+    ends_1_out[0:HALO], ends_2_out[0:HALO] = edges(slice(HALO, 2 * HALO))
+    ends_1_out[HALO : 2 * HALO], ends_2_out[HALO : 2 * HALO] = edges(slice(end - HALO, end))
+    middle_1_out[...], middle_2_out[...] = edges(slice(2 * HALO, end - HALO))
 
 
 def windows(
-    mid, before, after, from_right, from_left, w_query, w_keyval, anchor, weight
+    even, mid, rows_1, rows_2, cols_1, cols_2, w_query, w_keyval, anchor, weight
 ):
     tile_rows, _, channels = mid.shape
     high = tile_rows + 2 * HALO
@@ -367,14 +377,15 @@
     free = pl.BlockSpec(memory_space=pl.ANY)
     rim = jax.ShapeDtypeStruct((HALO, 2 * WIN, wide), BF16)
     inside = jax.ShapeDtypeStruct((tile_rows, WIN, wide), BF16)
-    edge = jax.ShapeDtypeStruct((tile_rows, HALO, wide), BF16)
+    ends = jax.ShapeDtypeStruct((2 * HALO, HALO, wide), BF16)
+    middle = jax.ShapeDtypeStruct((tile_rows - 2 * HALO, HALO, wide), BF16)
     slots = weight.shape[0]
     cells = WIN * WIN
     return pl.pallas_call(
         windows_kernel,
-        in_specs=[smem, smem] + [free] * 3 + [vmem] * 2 + [free] * 2,
-        out_specs=[vmem] * 5,
-        out_shape=[rim, rim, inside, edge, edge],
+        in_specs=[smem] * 3 + [free] * 3 + [vmem] * 2 + [free] * 2,
+        out_specs=[vmem] * 7,
+        out_shape=[rim, rim, inside, ends, ends, middle, middle],
         scratch_shapes=[
             pltpu.VMEM((high, 2 * WIN, channels), BF16),
             pltpu.VMEM(w_query.shape, BF16),
@@ -392,67 +403,13 @@
         ),
         name="windows",
     )(
-        anchor, weight, mid, before, after, from_right, from_left,
+        even, anchor, weight, mid, rows_1, rows_2, cols_1, cols_2,
         w_query, w_keyval,
     )
 
 
-def fold_kernel(
-    right_hbm, left_hbm, above_hbm, below_hbm, right_out, left_out, edges, sides, sems, out_sems
-):
-    tile_rows = right_hbm.shape[0]
-    ends = (slice(0, HALO), slice(tile_rows - HALO, tile_rows))
-    targets = [out.at[end] for end in ends for out in (right_out, left_out)]
-    copies = [
-        pltpu.make_async_copy(source, target, sems.at[i])
-        for i, (source, target) in enumerate(
-            [(source.at[end], edges.at[2 * i + j])
-             for i, end in enumerate(ends) for j, source in enumerate((right_hbm, left_hbm))]
-            + [(source.at[:, WIN : 2 * WIN], sides.at[i])
-               for i, source in enumerate((above_hbm, below_hbm))]
-        )
-    ]
-    for copy in copies:
-        copy.start()
-    for copy in copies:
-        copy.wait()
-    leaving = []
-    for i in range(2):
-        side = sides[i].astype(F32)
-        for j in range(2):
-            at = 2 * i + j
-            edges[at] = (edges[at].astype(F32) + side[:, j * HALO : (j + 1) * HALO]).astype(BF16)
-            leaving.append(pltpu.make_async_copy(edges.at[at], targets[at], out_sems.at[at]))
-            leaving[-1].start()
-    for copy in leaving:
-        copy.wait()
-
-
-def fold(on_right, on_left, above, below):
-    wide = on_right.shape[-1]
-    free = pl.BlockSpec(memory_space=pl.ANY)
-    return pl.pallas_call(
-        fold_kernel,
-        in_specs=[free] * 4,
-        out_specs=[free] * 2,
-        out_shape=[jax.ShapeDtypeStruct(a.shape, a.dtype) for a in (on_right, on_left)],
-        input_output_aliases={0: 0, 1: 1},
-        scratch_shapes=[
-            pltpu.VMEM((4, HALO, HALO, wide), BF16),
-            pltpu.VMEM((2, HALO, WIN, wide), BF16),
-            pltpu.SemaphoreType.DMA((6,)),
-            pltpu.SemaphoreType.DMA((4,)),
-        ],
-        compiler_params=params(61),
-        cost_estimate=pl.CostEstimate(
-            flops=on_right.size, bytes_accessed=12 * on_right.size, transcendentals=0
-        ),
-        name="fold",
-    )(on_right, on_left, above, below)
-
-
 def settle_kernel(
-    mid_ref, above_ref, below_ref, beside_ref, mask_ref, x_ref, known_ref, w_ref, base_ref, share_ref, own
+    even, mid_ref, rim_1_ref, rim_2_ref, beside_ref, mask_ref, x_ref, known_ref, w_ref, base_ref, share_ref, own
 ):
     count, inner = own.shape
     tile_cols, tile_rows = mask_ref.shape
@@ -465,8 +422,8 @@
     known_cell = jnp.sum(jnp.where(cell % tile_cols == col, in_row, 0.0), axis=1, keepdims=True) == 1
 
     def total(lanes):
-        upper = above_ref[:, 0:WIN, lanes].astype(F32)
-        lower = below_ref[:, 0:WIN, lanes].astype(F32)
+        rims = [ref[:, 0:WIN, lanes].astype(F32) for ref in (rim_1_ref, rim_2_ref)]
+        lower, upper = jnp.where(even[0] == 1, *rims), jnp.where(even[0] == 1, *rims[::-1])
         middle = mid_ref[:, :, lanes].astype(F32) + beside_ref[:, :, lanes].astype(F32)
         parts = [
             middle[:HALO] + upper,
@@ -487,13 +444,13 @@
         base_ref[:, cols] = jnp.where(known_cell, known_ref[:, cols].astype(F32), y)
 
 
-def settle(mid, above, below, beside, mask, x, known, w_out):
+def settle(even, mid, rim_1, rim_2, beside, mask, x, known, w_out):
     tile_rows, tile_cols, wide = mid.shape
     count, channels = x.shape
     vmem = pl.BlockSpec(memory_space=pltpu.VMEM)
     return pl.pallas_call(
         settle_kernel,
-        in_specs=[vmem] * 8,
+        in_specs=[pl.BlockSpec(memory_space=pltpu.SMEM)] + [vmem] * 8,
         out_specs=[vmem] * 2,
         out_shape=[
             jax.ShapeDtypeStruct((count, channels), F32),
@@ -505,7 +462,7 @@
             flops=2**17 * count * wide, bytes_accessed=12 * count * wide, transcendentals=0
         ),
         name="settle",
-    )(mid, above, below, beside, mask, x, known, w_out)
+    )(even, mid, rim_1, rim_2, beside, mask, x, known, w_out)
 
 
 def blend_kernel(
@@ -576,10 +533,13 @@
     return lax.all_to_all(pieces, ("row", "col"), split_axis=0, concat_axis=0, tiled=True)
 
 
-def neighbours(axis):
+def meet(axis, first, second):
     peers = lax.axis_size(axis)
-    onward = [(i, i + 1) for i in range(peers - 1)]
-    return onward, [(j, i) for i, j in onward]
+    met = []
+    for start, array in ((0, first), (1, second)):
+        pairs = [(i, i + 1) for i in range(start, peers - 1, 2)]
+        met.append(lax.ppermute(array, axis, pairs + [(j, i) for i, j in pairs]))
+    return met
 
 
 def on_device(features, known, known_mask, w_query, w_keyval, w_out, win_anchor, win_weight):
@@ -588,48 +548,64 @@
     per_sub = count // SUBS
     inner = w_query.shape[1]
     devices = lax.axis_size("row") * lax.axis_size("col")
-    down, up = neighbours("row")
-    right, left = neighbours("col")
+    row_even, col_even = (lax.axis_index(axis) % 2 == 0 for axis in ("row", "col"))
+    even = jnp.stack([row_even, col_even]).astype(jnp.int32)
+
+    def swap(flag, lower, higher):
+        return jnp.where(flag, higher, lower), jnp.where(flag, lower, higher)
+
     x = features.reshape(count, channels)
 
-    from_right = lax.ppermute(features[:, :HALO], "col", left)
-    from_left = lax.ppermute(features[:, tile_cols - HALO :], "col", right)
+    cols = meet("col", *swap(col_even, features[:, :HALO], features[:, tile_cols - HALO :]))
     pieces = project(x, w_query, w_keyval).reshape(devices, per_sub, 3 * LANES)
-    from_right, from_left, _ = lax.optimization_barrier((from_right, from_left, pieces))
+    cols_1, cols_2, _ = lax.optimization_barrier((*cols, pieces))
+    from_right, from_left = swap(col_even, cols_2, cols_1)
 
     def rows_of_halo(rows):
         return jnp.concatenate([features[rows], from_right[rows], from_left[rows]], 1)
 
-    before = lax.ppermute(rows_of_halo(slice(tile_rows - HALO, None)), "row", down)
-    after = lax.ppermute(rows_of_halo(slice(0, HALO)), "row", up)
+    first_rows, last_rows = rows_of_halo(slice(0, HALO)), rows_of_halo(slice(tile_rows - HALO, None))
+    rows_1, rows_2 = meet("row", *swap(row_even, first_rows, last_rows))
 
     gathered = exchange(pieces).reshape(devices * per_sub, 3 * LANES)
 
-    top, bottom, inside, on_right, on_left = windows(
+    rim_1, rim_2, inside, ends_1, ends_2, middle_1, middle_2 = windows(
+        even,
         features,
-        before,
-        after,
-        from_right,
-        from_left,
+        rows_1,
+        rows_2,
+        cols_1,
+        cols_2,
         w_query,
         w_keyval,
         win_anchor.reshape(-1, 2).T,
         win_weight.reshape(-1),
     )
-    above = lax.ppermute(bottom, "row", down)
-    below = lax.ppermute(top, "row", up)
+    rim_1, rim_2 = meet("row", rim_1, rim_2)
+    middle_1, middle_2 = meet("col", middle_1, middle_2)
     half = lattice_attend(0, gathered)
-    half, above, below = lax.optimization_barrier((half, above, below))
-    on_right, on_left = fold(on_right, on_left, above, below)
-    gathered, half, on_right, on_left = lax.optimization_barrier((gathered, half, on_right, on_left))
-    on_first = lax.ppermute(on_right, "col", right)
-    on_last = lax.ppermute(on_left, "col", left)
+    half, rim_1, rim_2, middle_1, middle_2 = lax.optimization_barrier(
+        (half, rim_1, rim_2, middle_1, middle_2)
+    )
+    below, above = swap(row_even, rim_2, rim_1)
+
+    def with_rims(ends, cols):
+        rims = jnp.concatenate([above[:, cols], below[:, cols]], 0)
+        return ends.astype(F32) + rims.astype(F32)
+
+    right, left = slice(WIN, WIN + HALO), slice(WIN + HALO, 2 * WIN)
+    ends_1 = jnp.where(col_even, with_rims(ends_1, right), with_rims(ends_1, left)).astype(BF16)
+    ends_2 = jnp.where(col_even, with_rims(ends_2, left), with_rims(ends_2, right)).astype(BF16)
+    gathered, half, ends_1, ends_2 = lax.optimization_barrier((gathered, half, ends_1, ends_2))
+    ends_1, ends_2 = meet("col", ends_1, ends_2)
     mixed = lattice_attend(1, gathered, half)
-    mixed, on_first, on_last = lax.optimization_barrier((mixed, on_first, on_last))
+    mixed, ends_1, ends_2 = lax.optimization_barrier((mixed, ends_1, ends_2))
     returned = exchange(mixed.reshape(devices, per_sub, LANES))
-    arrived = jnp.concatenate([on_first, on_last], 1)
+    ends = jnp.concatenate(swap(col_even, ends_1, ends_2), 1)
+    middle = jnp.concatenate(swap(col_even, middle_1, middle_2), 1)
+    arrived = jnp.concatenate([ends[:HALO], middle, ends[HALO:]], 0)
     base, share = settle(
-        inside, above, below, arrived, known_mask.T, x, known.reshape(count, channels), w_out
+        even, inside, rim_1, rim_2, arrived, known_mask.T, x, known.reshape(count, channels), w_out
     )
     returned = returned.reshape(SUBS, devices // SUBS, per_sub, LANES)
     out = blend(returned, share, base, w_out)

time: 202 us -> 210 us (1.040); the launches traced: 201 us -> 205 us
  waiting for transfers between devices: 33.9 us -> 15.3 us
  Pallas kernels: 110 us -> 121 us
  starting transfers between devices: 49.7 us -> 58.2 us
  other arithmetic: 2.26 us -> 6.98 us
    all_to_all x2, waiting for transfers between devices: 26.1 us -> 9.11 us  [exchange(): lax.all_to_all(pieces, ('row', 'col'), split_axis=0, concat_axis=0, tiled...]
    pallas_call x3 -> x2, Pallas kernels: 19.3 us -> 30 us  [the longest x1 23 us: windows(): pl.pallas_call(windows_kernel, in_specs=[smem] * 3 + [free] * 3 + [vmem]...]
    ppermute x8 -> x10, starting transfers between devices: 29.5 us -> 36.3 us  [meet(): met.append(lax.ppermute(array, axis, pairs + [(j, i) for i, j in pairs]))]
    select_n x0 -> x6, other arithmetic: none -> 4.23 us  [swap(): return (jnp.where(flag, higher, lower), jnp.where(flag, lower, higher))]
    ppermute x8 -> x10, waiting for transfers between devices: 7.87 us -> 6.22 us  [meet(): met.append(lax.ppermute(array, axis, pairs + [(j, i) for i, j in pairs]))]
  transfers between devices with their start and end apart: 10 -> 12, of which waited for: 4 -> 2; matrix products, arithmetic and copies ran while one was open for 1% -> 1% of each run, Pallas kernels for 51% -> 56%
where the time goes in v5:
time: 210 us; the launch traced here: 205 us
  Pallas kernels  121 us (58%)
  starting transfers between devices  58.2 us (28%)
  waiting for transfers between devices  15.3 us (7%)
  other arithmetic  6.98 us (3%)
  local copies, waits for them, and re-layouts  3.15 us (2%)
    pallas_call x2, Pallas kernels, lattice_attend(): pl.pallas_call(functools.partial(lattice_kernel, head), grid=(count // QB...  77.5 us
    ppermute x10, starting transfers between devices, meet(): met.append(lax.ppermute(array, axis, pairs + [(j, i) for i, j in pairs]))  36.3 us
    pallas_call x1, Pallas kernels, windows(): pl.pallas_call(windows_kernel, in_specs=[smem] * 3 + [free] * 3 + [vmem]...  23 us
    all_to_all x2, starting transfers between devices, exchange(): lax.all_to_all(pieces, ('row', 'col'), split_axis=0, concat_axis=0, tiled...  22 us
    all_to_all x2, waiting for transfers between devices, exchange(): lax.all_to_all(pieces, ('row', 'col'), split_axis=0, concat_axis=0, tiled...  9.11 us
    pallas_call x1, Pallas kernels, project(): pl.pallas_call(project_kernel, in_specs=[free] * 3, out_specs=free, out_s...  8.05 us
    pallas_call x1, Pallas kernels, settle(): pl.pallas_call(settle_kernel, in_specs=[pl.BlockSpec(memory_space=pltpu.S...  7.07 us
    ppermute x10, waiting for transfers between devices, meet(): met.append(lax.ppermute(array, axis, pairs + [(j, i) for i, j in pairs]))  6.22 us
  transfers between devices with their start and end apart: 12, of which 2 were waited for; matrix products, arithmetic and copies ran while one was open for 1% of the time, Pallas kernels for 56%

profile of v5, /device:TPU:1, one launch (start us, length us, event | category | flops | bytes accessed | tf_op | source)
XLA Modules:
  0.0 205.5 jit_solution(13121031248093011501)
XLA Ops:
  0.0 2.4 %broadcast_select_fusion.2 = (bf16[32,8,1280]{2,1,0:T(8,128)(2,1)}, bf16[32,8,1280]{2,1,0:T(8,128)(2,1)}) fusion(pred[]{:T(512)} %eq.10, bf16[32,16,1280]{2,1,0:T(8,128)(2,1)} %mid_hbm.1), kind=kLoop, calls=%fused_computation.13 | loop fusion | flops 655360 | bytes 2621441 | tf_op jit(solution)/shard_map/jit(_where)/select_n | solution.py:555
  2.4 0.7 collective-permute-start.1
  3.1 5.4 %collective-permute-start = (bf16[32,8,1280]{2,1,0:T(8,128)(2,1)}, bf16[32,8,1280]{2,1,0:T(8,128)(2,1)S(1)}, u32[]{:S(2)}, u32[]{:S(2)}) collective-permute-start(bf16[32,8,1280]{2,1,0:T(8,128)(2,1)} %get-tuple-element.58), channel_id=1, source_target_pairs={{0,1},{2,3},{4,5},{6,7},{8,9},{10,11},{12,13},{14,15},{1,0},{3,2},... | collective-permute-start | bytes 1966088 | tf_op jit(solution)/shard_map/ppermute | solution.py:541
  8.5 8.1 %project.1 = bf16[16,8,32,384]{3,2,1,0:T(8,128)(2,1)} custom-call(bf16[512,1280]{1,0:T(8,128)(2,1)} %bitcast.14, bf16[1280,1024]{1,0:T(8,128)(2,1)} %wq_hbm.3, bf16[1280,2048]{1,0:T(8,128)(2,1)} %wkv_hbm.3), custom_call_target="tpu_custom_call" | custom-call | flops 4026531840 | bytes 12320768 | tf_op jit(solution)/shard_map/project/pallas_call | solution.py:109
  16.7 6.2 %collective-permute-done.cols_1_ref = bf16[32,8,1280]{2,1,0:T(8,128)(2,1)S(1)} collective-permute-done((bf16[32,8,1280]{2,1,0:T(8,128)(2,1)}, bf16[32,8,1280]{2,1,0:T(8,128)(2,1)S(1)}, u32[]{:S(2)}, u32[]{:S(2)}) %collective-permute-start) | collective-permute-done | bytes 655392 | tf_op jit(solution)/shard_map/ppermute | solution.py:541
  23.0 0.7 copy-done.2
  24.3 4.6 %collective-permute-start.3 = (bf16[8,32,1280]{2,1,0:T(8,128)(2,1)S(1)}, bf16[8,32,1280]{2,1,0:T(8,128)(2,1)S(1)}, u32[]{:S(2)}, u32[]{:S(2)}) collective-permute-start(bf16[8,32,1280]{2,1,0:T(8,128)(2,1)S(1)} %get-tuple-element.51), channel_id=1, source_target_pairs={{16,32},{48,64},{80,96},{32,16},{64,48},{96,80},{17,33},{49,65},{8... | collective-permute-start | bytes 1966088 | tf_op jit(solution)/shard_map/ppermute | solution.py:541
  28.9 11.0 %all-to-all-start = ((bf16[128,32,384]{2,1,0:T(8,128)(2,1)}), bf16[128,32,384]{2,1,0:T(8,128)(2,1)}, u32[]{:S(2)}, u32[]{:S(2)}) async-start(bf16[128,32,384]{2,1,0:T(8,128)(2,1)} %bitcast.1), calls=%async_computation | async-start | bytes 6291456 | tf_op jit(solution)/shard_map/all_to_all | solution.py:533
  40.5 0.9 copy-done.9
  41.6 23.0 %windows.1 = (bf16[8,32,1152]{2,1,0:T(8,128)(2,1)}, bf16[8,32,1152]{2,1,0:T(8,128)(2,1)}, bf16[32,16,1152]{2,1,0:T(8,128)(2,1)}, bf16[16,8,1152]{2,1,0:T(8,128)(...) custom-call(s32[2]{0:T(128)} %add_convert_fusion.even, ...), custom_call_target="tpu_custom_call" | custom-call | flops 135291469824 | bytes 11796480 | tf_op jit(solution)/shard_map/windows/pallas_call | solution.py:384
  64.6 5.2 %collective-permute-start.6 = (bf16[16,8,1152]{2,1,0:T(8,128)(2,1)}, bf16[16,8,1152]{2,1,0:T(8,128)(2,1)S(1)}, u32[]{:S(2)}, u32[]{:S(2)}) collective-permute-start(bf16[16,8,1152]{2,1,0:T(8,128)(2,1)} %get-tuple-element.32), channel_id=1, source_target_pairs={{0,1},{2,3},{4,5},{6,7},{8,9},{10,11},{12,13},{14,15},{1,0},{3,2},... | collective-permute-start | bytes 884744 | tf_op jit(solution)/shard_map/ppermute | solution.py:541
  69.8 0.7 collective-permute-start.7
  70.6 13.1 %collective-permute-start.5 = (bf16[8,32,1152]{2,1,0:T(8,128)(2,1)}, bf16[8,32,1152]{2,1,0:T(8,128)(2,1)S(1)}, u32[]{:S(2)}, u32[]{:S(2)}) collective-permute-start(bf16[8,32,1152]{2,1,0:T(8,128)(2,1)} %get-tuple-element.31), channel_id=1, source_target_pairs={{16,32},{48,64},{80,96},{32,16},{64,48},{96,80},{17,33},{49,65},{8... | collective-permute-start | bytes 1769480 | tf_op jit(solution)/shard_map/ppermute | solution.py:541
  83.7 38.5 %lattice_attend_0.1.refs_0_ = bf16[64,4096]{1,0:T(8,128)(2,1)} custom-call(bf16[4096,384]{1,0:T(8,128)(2,1)} %bitcast.2.qk_ref.v_ref, bf16[4096,384]{1,0:T(8,128)(2,1)} %bitcast.2.qk_ref.v_ref), custom_call_target="tpu_custom_call" | custom-call | flops 17179869184 | bytes 3145728 | tf_op jit(solution)/shard_map/lattice_attend_0/pallas_call | solution.py:228
  123.6 1.0 fusion.7
  124.6 5.1 %collective-permute-start.8 = (bf16[16,8,1152]{2,1,0:T(8,128)(2,1)}, bf16[16,8,1152]{2,1,0:T(8,128)(2,1)S(1)}, u32[]{:S(2)}, u32[]{:S(2)}) collective-permute-start(bf16[16,8,1152]{2,1,0:T(8,128)(2,1)} %get-tuple-element.41), channel_id=1, source_target_pairs={{0,1},{2,3},{4,5},{6,7},{8,9},{10,11},{12,13},{14,15},{1,0},{3,2},... | collective-permute-start | bytes 884744 | tf_op jit(solution)/shard_map/ppermute | solution.py:541
  129.8 1.4 collective-permute-start.9
  131.1 39.0 %lattice_attend_1.1 = bf16[4096,128]{1,0:T(8,128)(2,1)} custom-call(bf16[4096,384]{1,0:T(8,128)(2,1)} %bitcast.2.qk_ref.v_ref, bf16[4096,384]{1,0:T(8,128)(2,1)} %bitcast.2.qk_ref.v_ref, bf16[64,4096]{1,0:T(8,128)(2,1)} %lattice_attend_0.1.refs_0_), custom_call_target="tpu_custom_call" | custom-call | flops 17179869184 | bytes 3145728 | tf_op jit(solution)/shard_map/lattice_attend_1/pallas_call | solution.py:228
  170.2 11.0 %all-to-all-start.1 = ((bf16[128,32,128]{2,1,0:T(8,128)(2,1)}), bf16[128,32,128]{2,1,0:T(8,128)(2,1)}, u32[]{:S(2)}, u32[]{:S(2)}) async-start(bf16[128,32,128]{2,1,0:T(8,128)(2,1)} %bitcast.16), calls=%async_computation.1 | async-start | bytes 2097152 | tf_op jit(solution)/shard_map/all_to_all | solution.py:533
  181.2 1.0 broadcast_select_fusion.11
  182.2 1.1 fusion.3.beside_ref
  183.3 7.1 %settle.1 = (f32[512,1280]{1,0:T(8,128)}, f32[512,128]{1,0:T(8,128)}) custom-call(s32[2]{0:T(128)} %add_convert_fusion.even, bf16[32,16,1152]{2,1,0:T(8,128)(2,1)} %get-tuple-element.44.mid_ref, bf16[8,32,1152]{2,1,0:T(8,128)(2,1)} %copy-done.3, bf16[8,32,1152]{2,1,0:T(8,128)(2,1)} %copy-done.4, bf16[32,16,1152]{2,1,0:T(8,128)(2,1)} %fusion.3.beside_ref, ...), custom_call_target="tpu_custom_call" | custom-call | flops 77309411328 | bytes 7077888 | tf_op jit(solution)/shard_map/settle/pallas_call | solution.py:451
  190.4 9.1 %all-to-all-done.1 = bf16[128,32,128]{2,1,0:T(8,128)(2,1)} async-done(((bf16[128,32,128]{2,1,0:T(8,128)(2,1)}), bf16[128,32,128]{2,1,0:T(8,128)(2,1)}, u32[]{:S(2)}, u32[]{:S(2)}) %all-to-all-start.1) | async-done | bytes 1048608 | tf_op jit(solution)/shard_map/all_to_all | solution.py:533
  199.5 5.5 %blend.1 = bf16[512,1280]{1,0:T(8,128)(2,1)} custom-call(bf16[16,8,32,128]{3,2,1,0:T(8,128)(2,1)} %bitcast.9.mixed_hbm, f32[512,128]{1,0:T(8,128)} %get-tuple-element.49.share_hbm, f32[512,1280]{1,0:T(8,128)} %get-tuple-element.50.base_hbm, bf16[1024,1280]{1,0:T(8,128)(2,1)} %w_hbm.1), custom_call_target="tpu_custom_call" | custom-call | flops 1879048192 | bytes 6553600 | tf_op jit(solution)/shard_map/blend/pallas_call | solution.py:510
  (42 shorter events, 3.1 us)
Async XLA Ops:
  2.4 14.2 %collective-permute-start.1 = (bf16[32,8,1280]{2,1,0:T(8,128)(2,1)}, bf16[32,8,1280]{2,1,0:T(8,128)(2,1)S(1)}, u32[]{:S(2)}, u32[]{:S(2)}) collective-permute-start(bf16[32,8,1280]{2,1,0:T(8,128)(2,1)} %get-tuple-element.57), channel_id=1, source_target_pairs={{1,2},{3,4},{5,6},{7,8},{9,10},{11,12},{13,14},{2,1},{4,3},{6,5},{... | collective-permute-start | bytes 1966088 | tf_op jit(solution)/shard_map/ppermute | solution.py:541
  3.1 19.7 %collective-permute-start = (bf16[32,8,1280]{2,1,0:T(8,128)(2,1)}, bf16[32,8,1280]{2,1,0:T(8,128)(2,1)S(1)}, u32[]{:S(2)}, u32[]{:S(2)}) collective-permute-start(bf16[32,8,1280]{2,1,0:T(8,128)(2,1)} %get-tuple-element.58), channel_id=1, source_target_pairs={{0,1},{2,3},{4,5},{6,7},{8,9},{10,11},{12,13},{14,15},{1,0},{3,2},... | collective-permute-start | bytes 1966088 | tf_op jit(solution)/shard_map/ppermute | solution.py:541
  8.5 8.1 %copy-start = (bf16[32,16,1280]{2,1,0:T(8,128)(2,1)S(1)}, bf16[32,16,1280]{2,1,0:T(8,128)(2,1)}, u32[]{:S(2)}) copy-start(bf16[32,16,1280]{2,1,0:T(8,128)(2,1)} %mid_hbm.1) | copy-start | bytes 3932164
  16.7 6.3 %copy-start.1 = (bf16[32,8,1280]{2,1,0:T(8,128)(2,1)}, bf16[32,8,1280]{2,1,0:T(8,128)(2,1)S(1)}, u32[]{:S(2)}) copy-start(bf16[32,8,1280]{2,1,0:T(8,128)(2,1)S(1)} %collective-permute-done.1.cols_2_ref) | copy-start | bytes 1966084
  22.9 0.9 copy-start.2
  24.3 16.2 %collective-permute-start.3 = (bf16[8,32,1280]{2,1,0:T(8,128)(2,1)S(1)}, bf16[8,32,1280]{2,1,0:T(8,128)(2,1)S(1)}, u32[]{:S(2)}, u32[]{:S(2)}) collective-permute-start(bf16[8,32,1280]{2,1,0:T(8,128)(2,1)S(1)} %get-tuple-element.51), channel_id=1, source_target_pairs={{16,32},{48,64},{80,96},{32,16},{64,48},{96,80},{17,33},{49,65},{8... | collective-permute-start | bytes 1966088 | tf_op jit(solution)/shard_map/ppermute | solution.py:541
  28.8 11.7 %collective-permute-start.2 = (bf16[8,32,1280]{2,1,0:T(8,128)(2,1)S(1)}, bf16[8,32,1280]{2,1,0:T(8,128)(2,1)S(1)}, u32[]{:S(2)}, u32[]{:S(2)}) collective-permute-start(bf16[8,32,1280]{2,1,0:T(8,128)(2,1)S(1)} %get-tuple-element.52), channel_id=1, source_target_pairs={{0,16},{32,48},{64,80},{96,112},{16,0},{48,32},{80,64},{112,96},{1... | collective-permute-start | bytes 1966088 | tf_op jit(solution)/shard_map/ppermute | solution.py:541
  28.9 54.8 %all-to-all-start = ((bf16[128,32,384]{2,1,0:T(8,128)(2,1)}), bf16[128,32,384]{2,1,0:T(8,128)(2,1)}, u32[]{:S(2)}, u32[]{:S(2)}) async-start(bf16[128,32,384]{2,1,0:T(8,128)(2,1)} %bitcast.1), calls=%async_computation | async-start | bytes 6291456 | tf_op jit(solution)/shard_map/all_to_all | solution.py:533
  40.5 0.9 copy-start.9
  40.5 1.1 copy-start.10
  64.6 57.6 %collective-permute-start.6 = (bf16[16,8,1152]{2,1,0:T(8,128)(2,1)}, bf16[16,8,1152]{2,1,0:T(8,128)(2,1)S(1)}, u32[]{:S(2)}, u32[]{:S(2)}) collective-permute-start(bf16[16,8,1152]{2,1,0:T(8,128)(2,1)} %get-tuple-element.32), channel_id=1, source_target_pairs={{0,1},{2,3},{4,5},{6,7},{8,9},{10,11},{12,13},{14,15},{1,0},{3,2},... | collective-permute-start | bytes 884744 | tf_op jit(solution)/shard_map/ppermute | solution.py:541
  69.8 52.4 %collective-permute-start.7 = (bf16[16,8,1152]{2,1,0:T(8,128)(2,1)}, bf16[16,8,1152]{2,1,0:T(8,128)(2,1)S(1)}, u32[]{:S(2)}, u32[]{:S(2)}) collective-permute-start(bf16[16,8,1152]{2,1,0:T(8,128)(2,1)} %get-tuple-element.33), channel_id=1, source_target_pairs={{1,2},{3,4},{5,6},{7,8},{9,10},{11,12},{13,14},{2,1},{4,3},{6,5},{... | collective-permute-start | bytes 884744 | tf_op jit(solution)/shard_map/ppermute | solution.py:541
  70.5 51.7 %collective-permute-start.4 = (bf16[8,32,1152]{2,1,0:T(8,128)(2,1)}, bf16[8,32,1152]{2,1,0:T(8,128)(2,1)S(1)}, u32[]{:S(2)}, u32[]{:S(2)}) collective-permute-start(bf16[8,32,1152]{2,1,0:T(8,128)(2,1)} %get-tuple-element.30), channel_id=1, source_target_pairs={{0,16},{32,48},{64,80},{96,112},{16,0},{48,32},{80,64},{112,96},{1... | collective-permute-start | bytes 1769480 | tf_op jit(solution)/shard_map/ppermute | solution.py:541
  70.6 51.7 %collective-permute-start.5 = (bf16[8,32,1152]{2,1,0:T(8,128)(2,1)}, bf16[8,32,1152]{2,1,0:T(8,128)(2,1)S(1)}, u32[]{:S(2)}, u32[]{:S(2)}) collective-permute-start(bf16[8,32,1152]{2,1,0:T(8,128)(2,1)} %get-tuple-element.31), channel_id=1, source_target_pairs={{16,32},{48,64},{80,96},{32,16},{64,48},{96,80},{17,33},{49,65},{8... | collective-permute-start | bytes 1769480 | tf_op jit(solution)/shard_map/ppermute | solution.py:541
  122.2 1.2 copy-start.7
  122.2 1.4 copy-start.8
  122.2 0.7 copy-start.5
  122.2 0.9 copy-start.3
  122.3 1.1 copy-start.4
  124.6 45.5 %copy-start.6 = (bf16[16,8,1152]{2,1,0:T(8,128)(2,1)S(1)}, bf16[16,8,1152]{2,1,0:T(8,128)(2,1)}, u32[]{:S(2)}) copy-start(bf16[16,8,1152]{2,1,0:T(8,128)(2,1)} %copy-done.5) | copy-start | bytes 884740
  124.6 45.5 %collective-permute-start.8 = (bf16[16,8,1152]{2,1,0:T(8,128)(2,1)}, bf16[16,8,1152]{2,1,0:T(8,128)(2,1)S(1)}, u32[]{:S(2)}, u32[]{:S(2)}) collective-permute-start(bf16[16,8,1152]{2,1,0:T(8,128)(2,1)} %get-tuple-element.41), channel_id=1, source_target_pairs={{0,1},{2,3},{4,5},{6,7},{8,9},{10,11},{12,13},{14,15},{1,0},{3,2},... | collective-permute-start | bytes 884744 | tf_op jit(solution)/shard_map/ppermute | solution.py:541
  129.8 40.4 %collective-permute-start.9 = (bf16[16,8,1152]{2,1,0:T(8,128)(2,1)}, bf16[16,8,1152]{2,1,0:T(8,128)(2,1)}, u32[]{:S(2)}, u32[]{:S(2)}) collective-permute-start(bf16[16,8,1152]{2,1,0:T(8,128)(2,1)} %get-tuple-element.42), channel_id=1, source_target_pairs={{1,2},{3,4},{5,6},{7,8},{9,10},{11,12},{13,14},{2,1},{4,3},{6,5},{... | collective-permute-start | bytes 884744 | tf_op jit(solution)/shard_map/ppermute | solution.py:541
  170.2 29.3 %all-to-all-start.1 = ((bf16[128,32,128]{2,1,0:T(8,128)(2,1)}), bf16[128,32,128]{2,1,0:T(8,128)(2,1)}, u32[]{:S(2)}, u32[]{:S(2)}) async-start(bf16[128,32,128]{2,1,0:T(8,128)(2,1)} %bitcast.16), calls=%async_computation.1 | async-start | bytes 2097152 | tf_op jit(solution)/shard_map/all_to_all | solution.py:533

commit v6 on v5

--- a/solution.py
+++ b/solution.py
@@ -301,7 +301,7 @@
     along = lax.broadcasted_iota(jnp.int32, (cells, cells), 1)
     diagonal = jnp.where(across == along, 1.0, 0.0)
 
-    def one_window(slot, arriving):
+    def one_window(slot, carry):
         top = anchor[0, slot] + HALO
         left = anchor[1, slot]
         factor = weight[slot].astype(F32)
@@ -312,8 +312,6 @@
         x = x.reshape(cells, channels)
 
         def project(g):
-            for copy in arriving.get(g, ()):
-                copy.wait()
             q = dot(x, wq_ref[:, g : g + 2 * LANES]).astype(BF16)
             k = dot(x, wkv_ref[:, g : g + 2 * LANES]).astype(BF16)
             v = dot(x, wkv_ref[:, inner + g : inner + g + 2 * LANES])
@@ -344,13 +342,11 @@
         cover = jnp.broadcast_to(in_mid * factor, (WIN, WIN, LANES))
         mid_sum[rows, :, inner:wide] += cover
         side_sum[rows, :, inner:wide] += factor - cover
-
-    def later_window(slot, carry):
-        one_window(slot, {})
         return carry
 
-    one_window(0, weight_copies)
-    lax.fori_loop(1, live, later_window, 0)
+    for copy in sum(weight_copies.values(), []):
+        copy.wait()
+    lax.fori_loop(0, live, one_window, 0)
     for out, rows in ((rim_1_out, rows_1), (rim_2_out, rows_2)):
         out[:, 0:WIN] = mid_sum[rows].astype(BF16)
         out[:, WIN : 2 * WIN] = side_sum[rows].astype(BF16)

time: 210 us -> 197 us (0.938); the launches traced: 205 us -> 197 us
  Pallas kernels: 121 us -> 113 us
  waiting for transfers between devices: 15.3 us -> 20.7 us
  starting transfers between devices: 58.2 us -> 53.5 us
    pallas_call x1, Pallas kernels: 23 us -> 14.6 us  [windows(): pl.pallas_call(windows_kernel, in_specs=[smem] * 3 + [free] * 3 + [vmem]...]
    all_to_all x2, waiting for transfers between devices: 9.11 us -> 14.5 us  [exchange(): lax.all_to_all(pieces, ('row', 'col'), split_axis=0, concat_axis=0, tiled...]
    ppermute x10, starting transfers between devices: 36.3 us -> 31.3 us  [meet(): met.append(lax.ppermute(array, axis, pairs + [(j, i) for i, j in pairs]))]
  transfers between devices with their start and end apart: 12 -> 12, of which waited for: 2 -> 3; matrix products, arithmetic and copies ran while one was open for 1% -> 1% of each run, Pallas kernels for 56% -> 54%
where the time goes in v6:
time: 197 us
  Pallas kernels  113 us (57%)
  starting transfers between devices  53.5 us (27%)
  waiting for transfers between devices  20.7 us (11%)
  other arithmetic  6.98 us (4%)
  local copies, waits for them, and re-layouts  3.15 us (2%)
    pallas_call x2, Pallas kernels, lattice_attend(): pl.pallas_call(functools.partial(lattice_kernel, head), grid=(count // QB...  77.4 us
    ppermute x10, starting transfers between devices, meet(): met.append(lax.ppermute(array, axis, pairs + [(j, i) for i, j in pairs]))  31.3 us
    all_to_all x2, starting transfers between devices, exchange(): lax.all_to_all(pieces, ('row', 'col'), split_axis=0, concat_axis=0, tiled...  22.2 us
    pallas_call x1, Pallas kernels, windows(): pl.pallas_call(windows_kernel, in_specs=[smem] * 3 + [free] * 3 + [vmem]...  14.6 us
    all_to_all x2, waiting for transfers between devices, exchange(): lax.all_to_all(pieces, ('row', 'col'), split_axis=0, concat_axis=0, tiled...  14.5 us
    pallas_call x1, Pallas kernels, project(): pl.pallas_call(project_kernel, in_specs=[free] * 3, out_specs=free, out_s...  8.05 us
    pallas_call x1, Pallas kernels, settle(): pl.pallas_call(settle_kernel, in_specs=[pl.BlockSpec(memory_space=pltpu.S...  7.07 us
    ppermute x10, waiting for transfers between devices, meet(): met.append(lax.ppermute(array, axis, pairs + [(j, i) for i, j in pairs]))  6.21 us
  transfers between devices with their start and end apart: 12, of which 3 were waited for; matrix products, arithmetic and copies ran while one was open for 1% of the time, Pallas kernels for 54%

profile of v6, /device:TPU:1, one launch (start us, length us, event | category | flops | bytes accessed | tf_op | source)
XLA Modules:
  0.0 197.5 jit_solution(3565564727190703067)
XLA Ops:
  0.0 2.4 %broadcast_select_fusion.2 = (bf16[32,8,1280]{2,1,0:T(8,128)(2,1)}, bf16[32,8,1280]{2,1,0:T(8,128)(2,1)}) fusion(pred[]{:T(512)} %eq.10, bf16[32,16,1280]{2,1,0:T(8,128)(2,1)} %mid_hbm.1), kind=kLoop, calls=%fused_computation.13 | loop fusion | flops 655360 | bytes 2621441 | tf_op jit(solution)/shard_map/jit(_where)/select_n | solution.py:551
  2.4 0.7 collective-permute-start.1
  3.1 5.4 %collective-permute-start = (bf16[32,8,1280]{2,1,0:T(8,128)(2,1)}, bf16[32,8,1280]{2,1,0:T(8,128)(2,1)S(1)}, u32[]{:S(2)}, u32[]{:S(2)}) collective-permute-start(bf16[32,8,1280]{2,1,0:T(8,128)(2,1)} %get-tuple-element.58), channel_id=1, source_target_pairs={{0,1},{2,3},{4,5},{6,7},{8,9},{10,11},{12,13},{14,15},{1,0},{3,2},... | collective-permute-start | bytes 1966088 | tf_op jit(solution)/shard_map/ppermute | solution.py:537
  8.5 8.1 %project.1 = bf16[16,8,32,384]{3,2,1,0:T(8,128)(2,1)} custom-call(bf16[512,1280]{1,0:T(8,128)(2,1)} %bitcast.14, bf16[1280,1024]{1,0:T(8,128)(2,1)} %wq_hbm.3, bf16[1280,2048]{1,0:T(8,128)(2,1)} %wkv_hbm.3), custom_call_target="tpu_custom_call" | custom-call | flops 4026531840 | bytes 12320768 | tf_op jit(solution)/shard_map/project/pallas_call | solution.py:109
  16.7 6.2 %collective-permute-done.cols_1_ref = bf16[32,8,1280]{2,1,0:T(8,128)(2,1)S(1)} collective-permute-done((bf16[32,8,1280]{2,1,0:T(8,128)(2,1)}, bf16[32,8,1280]{2,1,0:T(8,128)(2,1)S(1)}, u32[]{:S(2)}, u32[]{:S(2)}) %collective-permute-start) | collective-permute-done | bytes 655392 | tf_op jit(solution)/shard_map/ppermute | solution.py:537
  23.0 0.7 copy-done.2
  24.3 4.6 %collective-permute-start.3 = (bf16[8,32,1280]{2,1,0:T(8,128)(2,1)S(1)}, bf16[8,32,1280]{2,1,0:T(8,128)(2,1)S(1)}, u32[]{:S(2)}, u32[]{:S(2)}) collective-permute-start(bf16[8,32,1280]{2,1,0:T(8,128)(2,1)S(1)} %get-tuple-element.51), channel_id=1, source_target_pairs={{16,32},{48,64},{80,96},{32,16},{64,48},{96,80},{17,33},{49,65},{8... | collective-permute-start | bytes 1966088 | tf_op jit(solution)/shard_map/ppermute | solution.py:537
  28.9 11.0 %all-to-all-start = ((bf16[128,32,384]{2,1,0:T(8,128)(2,1)}), bf16[128,32,384]{2,1,0:T(8,128)(2,1)}, u32[]{:S(2)}, u32[]{:S(2)}) async-start(bf16[128,32,384]{2,1,0:T(8,128)(2,1)} %bitcast.1), calls=%async_computation | async-start | bytes 6291456 | tf_op jit(solution)/shard_map/all_to_all | solution.py:529
  40.5 0.9 copy-done.9
  41.6 14.6 %windows.1 = (bf16[8,32,1152]{2,1,0:T(8,128)(2,1)}, bf16[8,32,1152]{2,1,0:T(8,128)(2,1)}, bf16[32,16,1152]{2,1,0:T(8,128)(2,1)}, bf16[16,8,1152]{2,1,0:T(8,128)(...) custom-call(s32[2]{0:T(128)} %add_convert_fusion.even, ...), custom_call_target="tpu_custom_call" | custom-call | flops 135291469824 | bytes 11796480 | tf_op jit(solution)/shard_map/windows/pallas_call | solution.py:380
  56.2 5.2 %collective-permute-start.6 = (bf16[16,8,1152]{2,1,0:T(8,128)(2,1)}, bf16[16,8,1152]{2,1,0:T(8,128)(2,1)S(1)}, u32[]{:S(2)}, u32[]{:S(2)}) collective-permute-start(bf16[16,8,1152]{2,1,0:T(8,128)(2,1)} %get-tuple-element.32), channel_id=1, source_target_pairs={{0,1},{2,3},{4,5},{6,7},{8,9},{10,11},{12,13},{14,15},{1,0},{3,2},... | collective-permute-start | bytes 884744 | tf_op jit(solution)/shard_map/ppermute | solution.py:537
  61.5 0.7 collective-permute-start.7
  62.4 12.9 %collective-permute-start.5 = (bf16[8,32,1152]{2,1,0:T(8,128)(2,1)}, bf16[8,32,1152]{2,1,0:T(8,128)(2,1)S(1)}, u32[]{:S(2)}, u32[]{:S(2)}) collective-permute-start(bf16[8,32,1152]{2,1,0:T(8,128)(2,1)} %get-tuple-element.31), channel_id=1, source_target_pairs={{16,32},{48,64},{80,96},{32,16},{64,48},{96,80},{17,33},{49,65},{8... | collective-permute-start | bytes 1769480 | tf_op jit(solution)/shard_map/ppermute | solution.py:537
  75.3 5.2 %all-to-all-done = bf16[128,32,384]{2,1,0:T(8,128)(2,1)} async-done(((bf16[128,32,384]{2,1,0:T(8,128)(2,1)}), bf16[128,32,384]{2,1,0:T(8,128)(2,1)}, u32[]{:S(2)}, u32[]{:S(2)}) %all-to-all-start) | async-done | bytes 3145760 | tf_op jit(solution)/shard_map/all_to_all | solution.py:529
  80.6 38.5 %lattice_attend_0.1.refs_0_ = bf16[64,4096]{1,0:T(8,128)(2,1)} custom-call(bf16[4096,384]{1,0:T(8,128)(2,1)} %bitcast.2.qk_ref.v_ref, bf16[4096,384]{1,0:T(8,128)(2,1)} %bitcast.2.qk_ref.v_ref), custom_call_target="tpu_custom_call" | custom-call | flops 17179869184 | bytes 3145728 | tf_op jit(solution)/shard_map/lattice_attend_0/pallas_call | solution.py:228
  120.4 1.0 fusion.7
  121.5 1.5 collective-permute-start.9
  123.0 39.0 %lattice_attend_1.1 = bf16[4096,128]{1,0:T(8,128)(2,1)} custom-call(bf16[4096,384]{1,0:T(8,128)(2,1)} %bitcast.2.qk_ref.v_ref, bf16[4096,384]{1,0:T(8,128)(2,1)} %bitcast.2.qk_ref.v_ref, bf16[64,4096]{1,0:T(8,128)(2,1)} %lattice_attend_0.1.refs_0_), custom_call_target="tpu_custom_call" | custom-call | flops 17179869184 | bytes 3145728 | tf_op jit(solution)/shard_map/lattice_attend_1/pallas_call | solution.py:228
  162.0 11.2 %all-to-all-start.1 = ((bf16[128,32,128]{2,1,0:T(8,128)(2,1)}), bf16[128,32,128]{2,1,0:T(8,128)(2,1)}, u32[]{:S(2)}, u32[]{:S(2)}) async-start(bf16[128,32,128]{2,1,0:T(8,128)(2,1)} %bitcast.16), calls=%async_computation.1 | async-start | bytes 2097152 | tf_op jit(solution)/shard_map/all_to_all | solution.py:529
  173.2 1.0 broadcast_select_fusion.11
  174.3 1.1 fusion.3.beside_ref
  175.4 7.1 %settle.1 = (f32[512,1280]{1,0:T(8,128)}, f32[512,128]{1,0:T(8,128)}) custom-call(s32[2]{0:T(128)} %add_convert_fusion.even, bf16[32,16,1152]{2,1,0:T(8,128)(2,1)} %get-tuple-element.44.mid_ref, bf16[8,32,1152]{2,1,0:T(8,128)(2,1)} %copy-done.3, bf16[8,32,1152]{2,1,0:T(8,128)(2,1)} %copy-done.4, bf16[32,16,1152]{2,1,0:T(8,128)(2,1)} %fusion.3.beside_ref, ...), custom_call_target="tpu_custom_call" | custom-call | flops 77309411328 | bytes 7077888 | tf_op jit(solution)/shard_map/settle/pallas_call | solution.py:447
  182.5 9.3 %all-to-all-done.1 = bf16[128,32,128]{2,1,0:T(8,128)(2,1)} async-done(((bf16[128,32,128]{2,1,0:T(8,128)(2,1)}), bf16[128,32,128]{2,1,0:T(8,128)(2,1)}, u32[]{:S(2)}, u32[]{:S(2)}) %all-to-all-start.1) | async-done | bytes 1048608 | tf_op jit(solution)/shard_map/all_to_all | solution.py:529
  191.8 5.5 %blend.1 = bf16[512,1280]{1,0:T(8,128)(2,1)} custom-call(bf16[16,8,32,128]{3,2,1,0:T(8,128)(2,1)} %bitcast.9.mixed_hbm, f32[512,128]{1,0:T(8,128)} %get-tuple-element.49.share_hbm, f32[512,1280]{1,0:T(8,128)} %get-tuple-element.50.base_hbm, bf16[1024,1280]{1,0:T(8,128)(2,1)} %w_hbm.1), custom_call_target="tpu_custom_call" | custom-call | flops 1879048192 | bytes 6553600 | tf_op jit(solution)/shard_map/blend/pallas_call | solution.py:506
  (42 shorter events, 3.3 us)
Async XLA Ops:
  2.4 14.2 %collective-permute-start.1 = (bf16[32,8,1280]{2,1,0:T(8,128)(2,1)}, bf16[32,8,1280]{2,1,0:T(8,128)(2,1)S(1)}, u32[]{:S(2)}, u32[]{:S(2)}) collective-permute-start(bf16[32,8,1280]{2,1,0:T(8,128)(2,1)} %get-tuple-element.57), channel_id=1, source_target_pairs={{1,2},{3,4},{5,6},{7,8},{9,10},{11,12},{13,14},{2,1},{4,3},{6,5},{... | collective-permute-start | bytes 1966088 | tf_op jit(solution)/shard_map/ppermute | solution.py:537
  3.1 19.7 %collective-permute-start = (bf16[32,8,1280]{2,1,0:T(8,128)(2,1)}, bf16[32,8,1280]{2,1,0:T(8,128)(2,1)S(1)}, u32[]{:S(2)}, u32[]{:S(2)}) collective-permute-start(bf16[32,8,1280]{2,1,0:T(8,128)(2,1)} %get-tuple-element.58), channel_id=1, source_target_pairs={{0,1},{2,3},{4,5},{6,7},{8,9},{10,11},{12,13},{14,15},{1,0},{3,2},... | collective-permute-start | bytes 1966088 | tf_op jit(solution)/shard_map/ppermute | solution.py:537
  8.5 8.1 %copy-start = (bf16[32,16,1280]{2,1,0:T(8,128)(2,1)S(1)}, bf16[32,16,1280]{2,1,0:T(8,128)(2,1)}, u32[]{:S(2)}) copy-start(bf16[32,16,1280]{2,1,0:T(8,128)(2,1)} %mid_hbm.1) | copy-start | bytes 3932164
  16.7 6.3 %copy-start.1 = (bf16[32,8,1280]{2,1,0:T(8,128)(2,1)}, bf16[32,8,1280]{2,1,0:T(8,128)(2,1)S(1)}, u32[]{:S(2)}) copy-start(bf16[32,8,1280]{2,1,0:T(8,128)(2,1)S(1)} %collective-permute-done.1.cols_2_ref) | copy-start | bytes 1966084
  22.9 0.9 copy-start.2
  24.3 16.2 %collective-permute-start.3 = (bf16[8,32,1280]{2,1,0:T(8,128)(2,1)S(1)}, bf16[8,32,1280]{2,1,0:T(8,128)(2,1)S(1)}, u32[]{:S(2)}, u32[]{:S(2)}) collective-permute-start(bf16[8,32,1280]{2,1,0:T(8,128)(2,1)S(1)} %get-tuple-element.51), channel_id=1, source_target_pairs={{16,32},{48,64},{80,96},{32,16},{64,48},{96,80},{17,33},{49,65},{8... | collective-permute-start | bytes 1966088 | tf_op jit(solution)/shard_map/ppermute | solution.py:537
  28.8 11.7 %collective-permute-start.2 = (bf16[8,32,1280]{2,1,0:T(8,128)(2,1)S(1)}, bf16[8,32,1280]{2,1,0:T(8,128)(2,1)S(1)}, u32[]{:S(2)}, u32[]{:S(2)}) collective-permute-start(bf16[8,32,1280]{2,1,0:T(8,128)(2,1)S(1)} %get-tuple-element.52), channel_id=1, source_target_pairs={{0,16},{32,48},{64,80},{96,112},{16,0},{48,32},{80,64},{112,96},{1... | collective-permute-start | bytes 1966088 | tf_op jit(solution)/shard_map/ppermute | solution.py:537
  28.9 51.6 %all-to-all-start = ((bf16[128,32,384]{2,1,0:T(8,128)(2,1)}), bf16[128,32,384]{2,1,0:T(8,128)(2,1)}, u32[]{:S(2)}, u32[]{:S(2)}) async-start(bf16[128,32,384]{2,1,0:T(8,128)(2,1)} %bitcast.1), calls=%async_computation | async-start | bytes 6291456 | tf_op jit(solution)/shard_map/all_to_all | solution.py:529
  40.5 0.9 copy-start.9
  40.5 1.1 copy-start.10
  56.2 62.8 %collective-permute-start.6 = (bf16[16,8,1152]{2,1,0:T(8,128)(2,1)}, bf16[16,8,1152]{2,1,0:T(8,128)(2,1)S(1)}, u32[]{:S(2)}, u32[]{:S(2)}) collective-permute-start(bf16[16,8,1152]{2,1,0:T(8,128)(2,1)} %get-tuple-element.32), channel_id=1, source_target_pairs={{0,1},{2,3},{4,5},{6,7},{8,9},{10,11},{12,13},{14,15},{1,0},{3,2},... | collective-permute-start | bytes 884744 | tf_op jit(solution)/shard_map/ppermute | solution.py:537
  61.5 57.6 %collective-permute-start.7 = (bf16[16,8,1152]{2,1,0:T(8,128)(2,1)}, bf16[16,8,1152]{2,1,0:T(8,128)(2,1)S(1)}, u32[]{:S(2)}, u32[]{:S(2)}) collective-permute-start(bf16[16,8,1152]{2,1,0:T(8,128)(2,1)} %get-tuple-element.33), channel_id=1, source_target_pairs={{1,2},{3,4},{5,6},{7,8},{9,10},{11,12},{13,14},{2,1},{4,3},{6,5},{... | collective-permute-start | bytes 884744 | tf_op jit(solution)/shard_map/ppermute | solution.py:537
  62.1 56.9 %collective-permute-start.4 = (bf16[8,32,1152]{2,1,0:T(8,128)(2,1)}, bf16[8,32,1152]{2,1,0:T(8,128)(2,1)S(1)}, u32[]{:S(2)}, u32[]{:S(2)}) collective-permute-start(bf16[8,32,1152]{2,1,0:T(8,128)(2,1)} %get-tuple-element.30), channel_id=1, source_target_pairs={{0,16},{32,48},{64,80},{96,112},{16,0},{48,32},{80,64},{112,96},{1... | collective-permute-start | bytes 1769480 | tf_op jit(solution)/shard_map/ppermute | solution.py:537
  62.4 56.7 %collective-permute-start.5 = (bf16[8,32,1152]{2,1,0:T(8,128)(2,1)}, bf16[8,32,1152]{2,1,0:T(8,128)(2,1)S(1)}, u32[]{:S(2)}, u32[]{:S(2)}) collective-permute-start(bf16[8,32,1152]{2,1,0:T(8,128)(2,1)} %get-tuple-element.31), channel_id=1, source_target_pairs={{16,32},{48,64},{80,96},{32,16},{64,48},{96,80},{17,33},{49,65},{8... | collective-permute-start | bytes 1769480 | tf_op jit(solution)/shard_map/ppermute | solution.py:537
  119.0 1.2 copy-start.7
  119.0 1.4 copy-start.8
  119.0 0.7 copy-start.5
  119.1 0.9 copy-start.3
  119.1 1.1 copy-start.4
  121.5 40.5 %copy-start.6 = (bf16[16,8,1152]{2,1,0:T(8,128)(2,1)S(1)}, bf16[16,8,1152]{2,1,0:T(8,128)(2,1)}, u32[]{:S(2)}) copy-start(bf16[16,8,1152]{2,1,0:T(8,128)(2,1)} %copy-done.5) | copy-start | bytes 884740
  121.5 40.6 %collective-permute-start.8 = (bf16[16,8,1152]{2,1,0:T(8,128)(2,1)}, bf16[16,8,1152]{2,1,0:T(8,128)(2,1)S(1)}, u32[]{:S(2)}, u32[]{:S(2)}) collective-permute-start(bf16[16,8,1152]{2,1,0:T(8,128)(2,1)} %get-tuple-element.41), channel_id=1, source_target_pairs={{0,1},{2,3},{4,5},{6,7},{8,9},{10,11},{12,13},{14,15},{1,0},{3,2},... | collective-permute-start | bytes 884744 | tf_op jit(solution)/shard_map/ppermute | solution.py:537
  121.5 40.6 %collective-permute-start.9 = (bf16[16,8,1152]{2,1,0:T(8,128)(2,1)}, bf16[16,8,1152]{2,1,0:T(8,128)(2,1)}, u32[]{:S(2)}, u32[]{:S(2)}) collective-permute-start(bf16[16,8,1152]{2,1,0:T(8,128)(2,1)} %get-tuple-element.42), channel_id=1, source_target_pairs={{1,2},{3,4},{5,6},{7,8},{9,10},{11,12},{13,14},{2,1},{4,3},{6,5},{... | collective-permute-start | bytes 884744 | tf_op jit(solution)/shard_map/ppermute | solution.py:537
  162.0 29.8 %all-to-all-start.1 = ((bf16[128,32,128]{2,1,0:T(8,128)(2,1)}), bf16[128,32,128]{2,1,0:T(8,128)(2,1)}, u32[]{:S(2)}, u32[]{:S(2)}) async-start(bf16[128,32,128]{2,1,0:T(8,128)(2,1)} %bitcast.16), calls=%async_computation.1 | async-start | bytes 2097152 | tf_op jit(solution)/shard_map/all_to_all | solution.py:529

commit v7 on v6

--- a/solution.py
+++ b/solution.py
@@ -178,16 +178,19 @@
             c, j = items[i]
             return dot(qk_ref[c : c + KBLOCK, :], queries[j])
 
-        totals = [None] * parts
+        totals, sums = [None] * parts, [None] * parts
         ahead = [score(i) for i in range(AHEAD)]
         for i, (c, j) in enumerate(items):
             now = ahead.pop(0)
             if i + AHEAD < len(items):
                 ahead.append(score(i + AHEAD))
-            weights = jnp.exp2(now * SCALE).astype(BF16)
-            part = dot(values_t[:, c : c + KBLOCK], weights)
+            weights = jnp.exp2(now * SCALE)
+            part = dot(values_t[0:HD, c : c + KBLOCK], weights.astype(BF16))
+            total = jnp.sum(weights.reshape(KBLOCK // 8, 8, QPART), axis=0)
             totals[j] = part if totals[j] is None else totals[j] + part
-        finish(jnp.concatenate(totals, 1))
+            sums[j] = total if sums[j] is None else sums[j] + total
+        sums = jnp.sum(jnp.concatenate(sums, 1), axis=0, keepdims=True)
+        finish(jnp.concatenate([jnp.concatenate(totals, 1), jnp.broadcast_to(sums, (VROWS - HD, block))], 0))
 
     @pl.when(free[0] == 0)
     def _():
@@ -236,7 +239,7 @@
             pltpu.VMEM((VROWS, count), BF16),
             pltpu.SMEM((1,), jnp.int32),
         ],
-        compiler_params=params(63 if head else 61),
+        compiler_params=params(61),
         cost_estimate=pl.CostEstimate(
             flops=4 * 4 * count * count * HD,
             bytes_accessed=6 * count * LANES,
@@ -552,9 +555,16 @@
 
     x = features.reshape(count, channels)
 
-    cols = meet("col", *swap(col_even, features[:, :HALO], features[:, tile_cols - HALO :]))
+    high = tile_cols - HALO
+    cols = meet(
+        "col",
+        *(
+            lax.dynamic_slice_in_dim(features, jnp.where(flag, high, 0), HALO, axis=1)
+            for flag in (col_even, ~col_even)
+        ),
+    )
     pieces = project(x, w_query, w_keyval).reshape(devices, per_sub, 3 * LANES)
-    cols_1, cols_2, _ = lax.optimization_barrier((*cols, pieces))
+    cols_1, cols_2, even, _ = lax.optimization_barrier((*cols, even, pieces))
     from_right, from_left = swap(col_even, cols_2, cols_1)
 
     def rows_of_halo(rows):

time: 197 us -> 196 us (level)
  starting transfers between devices: 53.5 us -> 36.9 us
  Pallas kernels: 113 us -> 127 us
  other arithmetic: 6.98 us -> 2.78 us
  waiting for transfers between devices: 20.7 us -> 23.3 us
  local copies, waits for them, and re-layouts: 3.15 us -> 5.51 us
    ppermute x10, starting transfers between devices: 31.3 us -> 14.7 us  [meet(): met.append(lax.ppermute(array, axis, pairs + [(j, i) for i, j in pairs]))]
    pallas_call x1, Pallas kernels: 14.6 us -> 29.1 us  [windows(): pl.pallas_call(windows_kernel, in_specs=[smem] * 3 + [free] * 3 + [vmem]...]
    select_n x6 -> x5, other arithmetic: 4.23 us -> 0.83 us  [swap(): return (jnp.where(flag, higher, lower), jnp.where(flag, lower, higher))]
    all_to_all x2, waiting for transfers between devices: 14.5 us -> 17.6 us  [exchange(): lax.all_to_all(pieces, ('row', 'col'), split_axis=0, concat_axis=0, tiled...]
    dynamic_slice x0 -> x1, local copies, waits for them, and re-layouts: none -> 2.42 us  [on_device(): lax.dynamic_slice_in_dim(features, jnp.where(flag, high, 0), HALO, axis=1)]
  transfers between devices with their start and end apart: 12 -> 12, of which waited for: 3 -> 3; matrix products, arithmetic and copies ran while one was open for 1% -> 1% of each run, Pallas kernels for 54% -> 62%
where the time goes in v7:
time: 196 us
  Pallas kernels  127 us (65%)
  starting transfers between devices  36.9 us (19%)
  waiting for transfers between devices  23.3 us (12%)
  local copies, waits for them, and re-layouts  5.51 us (3%)
  other arithmetic  2.78 us (1%)
    pallas_call x2, Pallas kernels, lattice_attend(): pl.pallas_call(functools.partial(lattice_kernel, head), grid=(count // QB...  77.5 us
    pallas_call x1, Pallas kernels, windows(): pl.pallas_call(windows_kernel, in_specs=[smem] * 3 + [free] * 3 + [vmem]...  29.1 us
    all_to_all x2, starting transfers between devices, exchange(): lax.all_to_all(pieces, ('row', 'col'), split_axis=0, concat_axis=0, tiled...  22.2 us
    all_to_all x2, waiting for transfers between devices, exchange(): lax.all_to_all(pieces, ('row', 'col'), split_axis=0, concat_axis=0, tiled...  17.6 us
    ppermute x10, starting transfers between devices, meet(): met.append(lax.ppermute(array, axis, pairs + [(j, i) for i, j in pairs]))  14.7 us
    pallas_call x1, Pallas kernels, project(): pl.pallas_call(project_kernel, in_specs=[free] * 3, out_specs=free, out_s...  8.09 us
    pallas_call x1, Pallas kernels, settle(): pl.pallas_call(settle_kernel, in_specs=[pl.BlockSpec(memory_space=pltpu.S...  7.06 us
    ppermute x10, waiting for transfers between devices, meet(): met.append(lax.ppermute(array, axis, pairs + [(j, i) for i, j in pairs]))  5.61 us
  transfers between devices with their start and end apart: 12, of which 3 were waited for; matrix products, arithmetic and copies ran while one was open for 1% of the time, Pallas kernels for 62%

profile of v7, /device:TPU:1, one launch (start us, length us, event | category | flops | bytes accessed | tf_op | source)
XLA Modules:
  0.0 196.1 jit_solution(9302152496939358487)
XLA Ops:
  0.0 2.4 %constant_dynamic-slice_fusion = (bf16[32,8,1280]{2,1,0:T(8,128)(2,1)}, bf16[32,8,1280]{2,1,0:T(8,128)(2,1)}) fusion(bf16[32,16,1280]{2,1,0:T(8,128)(2,1)} %mid_hbm.1, s32[]{:T(128)S(6)} %select_n.88, s32[]{:T(128)S(6)} %select_n.87), kind=kLoop, calls=%fused_computation.31 | loop fusion | bytes 2621448 | tf_op jit(solution)/shard_map/dynamic_slice | solution.py:562
  2.4 0.7 collective-permute-start.1
  3.1 5.4 %collective-permute-start = (bf16[32,8,1280]{2,1,0:T(8,128)(2,1)}, bf16[32,8,1280]{2,1,0:T(8,128)(2,1)S(1)}, u32[]{:S(2)}, u32[]{:S(2)}) collective-permute-start(bf16[32,8,1280]{2,1,0:T(8,128)(2,1)} %get-tuple-element.60), channel_id=1, source_target_pairs={{0,1},{2,3},{4,5},{6,7},{8,9},{10,11},{12,13},{14,15},{1,0},{3,2},... | collective-permute-start | bytes 1966088 | tf_op jit(solution)/shard_map/ppermute | solution.py:540
  8.5 8.1 %project.1 = bf16[16,8,32,384]{3,2,1,0:T(8,128)(2,1)} custom-call(bf16[512,1280]{1,0:T(8,128)(2,1)} %bitcast.14, bf16[1280,1024]{1,0:T(8,128)(2,1)} %wq_hbm.3, bf16[1280,2048]{1,0:T(8,128)(2,1)} %wkv_hbm.3), custom_call_target="tpu_custom_call" | custom-call | flops 4026531840 | bytes 12320768 | tf_op jit(solution)/shard_map/project/pallas_call | solution.py:109
  16.6 0.6 add_convert_fusion.even
  17.3 5.6 %collective-permute-done.cols_1_ref = bf16[32,8,1280]{2,1,0:T(8,128)(2,1)S(1)} collective-permute-done((bf16[32,8,1280]{2,1,0:T(8,128)(2,1)}, bf16[32,8,1280]{2,1,0:T(8,128)(2,1)S(1)}, u32[]{:S(2)}, u32[]{:S(2)}) %collective-permute-start) | collective-permute-done | bytes 655392 | tf_op jit(solution)/shard_map/ppermute | solution.py:540
  23.0 0.7 copy-done.2
  23.8 0.5 broadcast_select_fusion.2
  24.3 4.6 %collective-permute-start.3 = (bf16[8,32,1280]{2,1,0:T(8,128)(2,1)S(1)}, bf16[8,32,1280]{2,1,0:T(8,128)(2,1)S(1)}, u32[]{:S(2)}, u32[]{:S(2)}) collective-permute-start(bf16[8,32,1280]{2,1,0:T(8,128)(2,1)S(1)} %get-tuple-element.53), channel_id=1, source_target_pairs={{16,32},{48,64},{80,96},{32,16},{64,48},{96,80},{17,33},{49,65},{8... | collective-permute-start | bytes 1966088 | tf_op jit(solution)/shard_map/ppermute | solution.py:540
  28.9 11.0 %all-to-all-start = ((bf16[128,32,384]{2,1,0:T(8,128)(2,1)}), bf16[128,32,384]{2,1,0:T(8,128)(2,1)}, u32[]{:S(2)}, u32[]{:S(2)}) async-start(bf16[128,32,384]{2,1,0:T(8,128)(2,1)} %bitcast.1), calls=%async_computation | async-start | bytes 6291456 | tf_op jit(solution)/shard_map/all_to_all | solution.py:532
  40.0 0.9 copy-done.7
  41.1 29.1 %windows.1 = (bf16[8,32,1152]{2,1,0:T(8,128)(2,1)}, bf16[8,32,1152]{2,1,0:T(8,128)(2,1)}, bf16[32,16,1152]{2,1,0:T(8,128)(2,1)}, bf16[16,8,1152]{2,1,0:T(8,128)(...) custom-call(s32[2]{0:T(128)} %add_convert_fusion.even, ...), custom_call_target="tpu_custom_call" | custom-call | flops 135291469824 | bytes 11796480 | tf_op jit(solution)/shard_map/windows/pallas_call | solution.py:383
  70.3 0.7 collective-permute-start.7
  71.2 1.9 collective-permute-start.5
  73.1 7.4 %all-to-all-done = bf16[128,32,384]{2,1,0:T(8,128)(2,1)} async-done(((bf16[128,32,384]{2,1,0:T(8,128)(2,1)}), bf16[128,32,384]{2,1,0:T(8,128)(2,1)}, u32[]{:S(2)}, u32[]{:S(2)}) %all-to-all-start) | async-done | bytes 3145760 | tf_op jit(solution)/shard_map/all_to_all | solution.py:532
  80.6 38.5 %lattice_attend_0.1.refs_0_ = bf16[64,4096]{1,0:T(8,128)(2,1)} custom-call(bf16[4096,384]{1,0:T(8,128)(2,1)} %bitcast.2.qk_ref.v_ref, bf16[4096,384]{1,0:T(8,128)(2,1)} %bitcast.2.qk_ref.v_ref), custom_call_target="tpu_custom_call" | custom-call | flops 17179869184 | bytes 3145728 | tf_op jit(solution)/shard_map/lattice_attend_0/pallas_call | solution.py:231
  119.2 0.7 copy-done.3
  120.7 0.9 collective-permute-start.9
  121.6 39.0 %lattice_attend_1.1 = bf16[4096,128]{1,0:T(8,128)(2,1)} custom-call(bf16[4096,384]{1,0:T(8,128)(2,1)} %bitcast.2.qk_ref.v_ref, bf16[4096,384]{1,0:T(8,128)(2,1)} %bitcast.2.qk_ref.v_ref, bf16[64,4096]{1,0:T(8,128)(2,1)} %lattice_attend_0.1.refs_0_), custom_call_target="tpu_custom_call" | custom-call | flops 17179869184 | bytes 3145728 | tf_op jit(solution)/shard_map/lattice_attend_1/pallas_call | solution.py:231
  160.7 11.2 %all-to-all-start.1 = ((bf16[128,32,128]{2,1,0:T(8,128)(2,1)}), bf16[128,32,128]{2,1,0:T(8,128)(2,1)}, u32[]{:S(2)}, u32[]{:S(2)}) async-start(bf16[128,32,128]{2,1,0:T(8,128)(2,1)} %bitcast.16), calls=%async_computation.1 | async-start | bytes 2097152 | tf_op jit(solution)/shard_map/all_to_all | solution.py:532
  172.0 1.1 fusion.3.beside_ref
  173.1 7.1 %settle.1 = (f32[512,1280]{1,0:T(8,128)}, f32[512,128]{1,0:T(8,128)}) custom-call(s32[2]{0:T(128)} %add_convert_fusion.even, bf16[32,16,1152]{2,1,0:T(8,128)(2,1)} %get-tuple-element.46.mid_ref, bf16[8,32,1152]{2,1,0:T(8,128)(2,1)} %copy-done.3, bf16[8,32,1152]{2,1,0:T(8,128)(2,1)} %copy-done.4, bf16[32,16,1152]{2,1,0:T(8,128)(2,1)} %fusion.3.beside_ref, ...), custom_call_target="tpu_custom_call" | custom-call | flops 77309411328 | bytes 7077888 | tf_op jit(solution)/shard_map/settle/pallas_call | solution.py:450
  180.2 10.2 %all-to-all-done.1 = bf16[128,32,128]{2,1,0:T(8,128)(2,1)} async-done(((bf16[128,32,128]{2,1,0:T(8,128)(2,1)}), bf16[128,32,128]{2,1,0:T(8,128)(2,1)}, u32[]{:S(2)}, u32[]{:S(2)}) %all-to-all-start.1) | async-done | bytes 1048608 | tf_op jit(solution)/shard_map/all_to_all | solution.py:532
  190.4 5.5 %blend.1 = bf16[512,1280]{1,0:T(8,128)(2,1)} custom-call(bf16[16,8,32,128]{3,2,1,0:T(8,128)(2,1)} %bitcast.9.mixed_hbm, f32[512,128]{1,0:T(8,128)} %get-tuple-element.51.share_hbm, f32[512,1280]{1,0:T(8,128)} %get-tuple-element.52.base_hbm, bf16[1024,1280]{1,0:T(8,128)(2,1)} %w_hbm.1), custom_call_target="tpu_custom_call" | custom-call | flops 1879048192 | bytes 6553600 | tf_op jit(solution)/shard_map/blend/pallas_call | solution.py:509
  (38 shorter events, 1.9 us)
Async XLA Ops:
  2.4 14.8 %collective-permute-start.1 = (bf16[32,8,1280]{2,1,0:T(8,128)(2,1)}, bf16[32,8,1280]{2,1,0:T(8,128)(2,1)S(1)}, u32[]{:S(2)}, u32[]{:S(2)}) collective-permute-start(bf16[32,8,1280]{2,1,0:T(8,128)(2,1)} %get-tuple-element.59), channel_id=1, source_target_pairs={{1,2},{3,4},{5,6},{7,8},{9,10},{11,12},{13,14},{2,1},{4,3},{6,5},{... | collective-permute-start | bytes 1966088 | tf_op jit(solution)/shard_map/ppermute | solution.py:540
  3.1 19.7 %collective-permute-start = (bf16[32,8,1280]{2,1,0:T(8,128)(2,1)}, bf16[32,8,1280]{2,1,0:T(8,128)(2,1)S(1)}, u32[]{:S(2)}, u32[]{:S(2)}) collective-permute-start(bf16[32,8,1280]{2,1,0:T(8,128)(2,1)} %get-tuple-element.60), channel_id=1, source_target_pairs={{0,1},{2,3},{4,5},{6,7},{8,9},{10,11},{12,13},{14,15},{1,0},{3,2},... | collective-permute-start | bytes 1966088 | tf_op jit(solution)/shard_map/ppermute | solution.py:540
  8.5 8.7 %copy-start = (bf16[32,16,1280]{2,1,0:T(8,128)(2,1)S(1)}, bf16[32,16,1280]{2,1,0:T(8,128)(2,1)}, u32[]{:S(2)}) copy-start(bf16[32,16,1280]{2,1,0:T(8,128)(2,1)} %mid_hbm.1) | copy-start | bytes 3932164
  17.3 5.7 %copy-start.1 = (bf16[32,8,1280]{2,1,0:T(8,128)(2,1)}, bf16[32,8,1280]{2,1,0:T(8,128)(2,1)S(1)}, u32[]{:S(2)}) copy-start(bf16[32,8,1280]{2,1,0:T(8,128)(2,1)S(1)} %collective-permute-done.1.cols_2_ref) | copy-start | bytes 1966084
  22.9 0.8 copy-start.2
  24.3 15.7 %collective-permute-start.3 = (bf16[8,32,1280]{2,1,0:T(8,128)(2,1)S(1)}, bf16[8,32,1280]{2,1,0:T(8,128)(2,1)S(1)}, u32[]{:S(2)}, u32[]{:S(2)}) collective-permute-start(bf16[8,32,1280]{2,1,0:T(8,128)(2,1)S(1)} %get-tuple-element.53), channel_id=1, source_target_pairs={{16,32},{48,64},{80,96},{32,16},{64,48},{96,80},{17,33},{49,65},{8... | collective-permute-start | bytes 1966088 | tf_op jit(solution)/shard_map/ppermute | solution.py:540
  28.8 11.1 %collective-permute-start.2 = (bf16[8,32,1280]{2,1,0:T(8,128)(2,1)S(1)}, bf16[8,32,1280]{2,1,0:T(8,128)(2,1)S(1)}, u32[]{:S(2)}, u32[]{:S(2)}) collective-permute-start(bf16[8,32,1280]{2,1,0:T(8,128)(2,1)S(1)} %get-tuple-element.54), channel_id=1, source_target_pairs={{0,16},{32,48},{64,80},{96,112},{16,0},{48,32},{80,64},{112,96},{1... | collective-permute-start | bytes 1966088 | tf_op jit(solution)/shard_map/ppermute | solution.py:540
  28.9 51.6 %all-to-all-start = ((bf16[128,32,384]{2,1,0:T(8,128)(2,1)}), bf16[128,32,384]{2,1,0:T(8,128)(2,1)}, u32[]{:S(2)}, u32[]{:S(2)}) async-start(bf16[128,32,384]{2,1,0:T(8,128)(2,1)} %bitcast.1), calls=%async_computation | async-start | bytes 6291456 | tf_op jit(solution)/shard_map/all_to_all | solution.py:532
  40.0 0.9 copy-start.7
  40.0 1.1 copy-start.8
  70.2 48.9 %collective-permute-start.6 = (bf16[16,8,1152]{2,1,0:T(8,128)(2,1)}, bf16[16,8,1152]{2,1,0:T(8,128)(2,1)S(1)}, u32[]{:S(2)}, u32[]{:S(2)}) collective-permute-start(bf16[16,8,1152]{2,1,0:T(8,128)(2,1)} %get-tuple-element.34), channel_id=1, source_target_pairs={{0,1},{2,3},{4,5},{6,7},{8,9},{10,11},{12,13},{14,15},{1,0},{3,2},... | collective-permute-start | bytes 884744 | tf_op jit(solution)/shard_map/ppermute | solution.py:540
  70.3 48.8 %collective-permute-start.7 = (bf16[16,8,1152]{2,1,0:T(8,128)(2,1)}, bf16[16,8,1152]{2,1,0:T(8,128)(2,1)S(1)}, u32[]{:S(2)}, u32[]{:S(2)}) collective-permute-start(bf16[16,8,1152]{2,1,0:T(8,128)(2,1)} %get-tuple-element.35), channel_id=1, source_target_pairs={{1,2},{3,4},{5,6},{7,8},{9,10},{11,12},{13,14},{2,1},{4,3},{6,5},{... | collective-permute-start | bytes 884744 | tf_op jit(solution)/shard_map/ppermute | solution.py:540
  70.9 48.1 %collective-permute-start.4 = (bf16[8,32,1152]{2,1,0:T(8,128)(2,1)}, bf16[8,32,1152]{2,1,0:T(8,128)(2,1)S(1)}, u32[]{:S(2)}, u32[]{:S(2)}) collective-permute-start(bf16[8,32,1152]{2,1,0:T(8,128)(2,1)} %get-tuple-element.32), channel_id=1, source_target_pairs={{0,16},{32,48},{64,80},{96,112},{16,0},{48,32},{80,64},{112,96},{1... | collective-permute-start | bytes 1769480 | tf_op jit(solution)/shard_map/ppermute | solution.py:540
  71.2 47.8 %collective-permute-start.5 = (bf16[8,32,1152]{2,1,0:T(8,128)(2,1)}, bf16[8,32,1152]{2,1,0:T(8,128)(2,1)S(1)}, u32[]{:S(2)}, u32[]{:S(2)}) collective-permute-start(bf16[8,32,1152]{2,1,0:T(8,128)(2,1)} %get-tuple-element.33), channel_id=1, source_target_pairs={{16,32},{48,64},{80,96},{32,16},{64,48},{96,80},{17,33},{49,65},{8... | collective-permute-start | bytes 1769480 | tf_op jit(solution)/shard_map/ppermute | solution.py:540
  119.0 1.1 copy-start.5
  119.0 1.4 copy-start.6
  119.0 0.8 copy-start.3
  119.1 1.0 copy-start.4
  120.6 40.1 %collective-permute-start.8 = (bf16[16,8,1152]{2,1,0:T(8,128)(2,1)S(1)}, bf16[16,8,1152]{2,1,0:T(8,128)(2,1)S(1)}, u32[]{:S(2)}, u32[]{:S(2)}) collective-permute-start(bf16[16,8,1152]{2,1,0:T(8,128)(2,1)S(1)} %get-tuple-element.43), channel_id=1, source_target_pairs={{0,1},{2,3},{4,5},{6,7},{8,9},{10,11},{12,13},{14,15},{1,0},{3,2},... | collective-permute-start | bytes 884744 | tf_op jit(solution)/shard_map/ppermute | solution.py:540
  120.7 40.0 %collective-permute-start.9 = (bf16[16,8,1152]{2,1,0:T(8,128)(2,1)S(1)}, bf16[16,8,1152]{2,1,0:T(8,128)(2,1)S(1)}, u32[]{:S(2)}, u32[]{:S(2)}) collective-permute-start(bf16[16,8,1152]{2,1,0:T(8,128)(2,1)S(1)} %get-tuple-element.44), channel_id=1, source_target_pairs={{1,2},{3,4},{5,6},{7,8},{9,10},{11,12},{13,14},{2,1},{4,3},{6,5},{... | collective-permute-start | bytes 884744 | tf_op jit(solution)/shard_map/ppermute | solution.py:540
  160.7 29.8 %all-to-all-start.1 = ((bf16[128,32,128]{2,1,0:T(8,128)(2,1)}), bf16[128,32,128]{2,1,0:T(8,128)(2,1)}, u32[]{:S(2)}, u32[]{:S(2)}) async-start(bf16[128,32,128]{2,1,0:T(8,128)(2,1)} %bitcast.16), calls=%async_computation.1 | async-start | bytes 2097152 | tf_op jit(solution)/shard_map/all_to_all | solution.py:532

commit v8 on v7

--- a/solution.py
+++ b/solution.py
@@ -44,12 +44,17 @@
 def lattice_order(count, by_row):
     lattice = lax.broadcasted_iota(jnp.int32, (count, count), 0 if by_row else 1)
     cell = lax.broadcasted_iota(jnp.int32, (count, count), 1 if by_row else 0)
-    per_sub = count // SUBS
-    tile_cols = 16
-    sub, place = lattice // per_sub, lattice % per_sub
+    per_sub, tile_cols = count // SUBS, 16
     across = tile_cols // STRIDE
-    row = (place // across) * STRIDE + sub // STRIDE
-    col = (place % across) * STRIDE + sub % STRIDE
+
+    def split(index, size):
+        return index >> (size.bit_length() - 1), index & (size - 1)
+
+    sub, place = split(lattice, per_sub)
+    sub_row, sub_col = split(sub, STRIDE)
+    place_row, place_col = split(place, across)
+    row = place_row * STRIDE + sub_row
+    col = place_col * STRIDE + sub_col
     return jnp.where(cell == row * tile_cols + col, 1.0, 0.0).astype(BF16)
 
 
@@ -414,11 +419,11 @@
     tile_cols, tile_rows = mask_ref.shape
     cell = lax.broadcasted_iota(jnp.int32, (count, tile_rows), 0)
     row = lax.broadcasted_iota(jnp.int32, (count, tile_rows), 1)
-    pick_row = jnp.where(cell // tile_cols == row, 1.0, 0.0).astype(BF16)
+    pick_row = jnp.where(cell >> (tile_cols.bit_length() - 1) == row, 1.0, 0.0).astype(BF16)
     in_row = dot_nt(pick_row, mask_ref[...].astype(F32).astype(BF16))
     cell = lax.broadcasted_iota(jnp.int32, (count, tile_cols), 0)
     col = lax.broadcasted_iota(jnp.int32, (count, tile_cols), 1)
-    known_cell = jnp.sum(jnp.where(cell % tile_cols == col, in_row, 0.0), axis=1, keepdims=True) == 1
+    known_cell = jnp.sum(jnp.where(cell & (tile_cols - 1) == col, in_row, 0.0), axis=1, keepdims=True) == 1
 
     def total(lanes):
         rims = [ref[:, 0:WIN, lanes].astype(F32) for ref in (rim_1_ref, rim_2_ref)]
@@ -487,12 +492,14 @@
         lanes = slice(g * LANES, (g + 2) * LANES)
         mixed = jnp.concatenate([mixed_ref[:, g + j].reshape(count, LANES) for j in range(2)], 1)
         blended[:, lanes] = (dot(back, mixed) * share).astype(BF16)
-    for copy in copies[2:]:
-        copy.wait()
+    copies[2].wait()
     outs = []
     for i, c in enumerate(range(0, channels, width)):
         cols = slice(c, c + width)
-        out_ref[:, cols] = (base_ref[:, cols] + dot(blended[...], w_ref[:, cols])).astype(BF16)
+        part = dot(blended[...], w_ref[:, cols])
+        if i == 0:
+            copies[3].wait()
+        out_ref[:, cols] = (base_ref[:, cols] + part).astype(BF16)
         outs.append(
             pltpu.make_async_copy(out_ref.at[:, cols], out_hbm.at[:, cols], out_sems.at[i])
         )

time: 196 us -> 196 us (level)
  waiting for transfers between devices: 23.3 us -> 20.1 us
  starting transfers between devices: 36.9 us -> 39.2 us
    all_to_all x2, waiting for transfers between devices: 17.6 us -> 14.4 us  [exchange(): lax.all_to_all(pieces, ('row', 'col'), split_axis=0, concat_axis=0, tiled...]
    ppermute x10, starting transfers between devices: 14.7 us -> 17.9 us  [meet(): met.append(lax.ppermute(array, axis, pairs + [(j, i) for i, j in pairs]))]
where the time goes in v8:
time: 196 us; the launch traced here: 195 us
  Pallas kernels  127 us (65%)
  starting transfers between devices  39.2 us (20%)
  waiting for transfers between devices  20.1 us (10%)
  local copies, waits for them, and re-layouts  5.51 us (3%)
  other arithmetic  2.78 us (1%)
    pallas_call x2, Pallas kernels, lattice_attend(): pl.pallas_call(functools.partial(lattice_kernel, head), grid=(count // QB...  77.5 us
    pallas_call x1, Pallas kernels, windows(): pl.pallas_call(windows_kernel, in_specs=[smem] * 3 + [free] * 3 + [vmem]...  29.1 us
    all_to_all x2, starting transfers between devices, exchange(): lax.all_to_all(pieces, ('row', 'col'), split_axis=0, concat_axis=0, tiled...  21.3 us
    ppermute x10, starting transfers between devices, meet(): met.append(lax.ppermute(array, axis, pairs + [(j, i) for i, j in pairs]))  17.9 us
    all_to_all x2, waiting for transfers between devices, exchange(): lax.all_to_all(pieces, ('row', 'col'), split_axis=0, concat_axis=0, tiled...  14.4 us
    pallas_call x1, Pallas kernels, project(): pl.pallas_call(project_kernel, in_specs=[free] * 3, out_specs=free, out_s...  8.09 us
    pallas_call x1, Pallas kernels, settle(): pl.pallas_call(settle_kernel, in_specs=[pl.BlockSpec(memory_space=pltpu.S...  7.08 us
    ppermute x10, waiting for transfers between devices, meet(): met.append(lax.ppermute(array, axis, pairs + [(j, i) for i, j in pairs]))  5.62 us
  transfers between devices with their start and end apart: 12, of which 3 were waited for; matrix products, arithmetic and copies ran while one was open for 1% of the time, Pallas kernels for 62%

profile of v8, /device:TPU:1, one launch (start us, length us, event | category | flops | bytes accessed | tf_op | source)
XLA Modules:
  0.0 194.8 jit_solution(12408896168534744571)
XLA Ops:
  0.0 2.4 %constant_dynamic-slice_fusion = (bf16[32,8,1280]{2,1,0:T(8,128)(2,1)}, bf16[32,8,1280]{2,1,0:T(8,128)(2,1)}) fusion(bf16[32,16,1280]{2,1,0:T(8,128)(2,1)} %mid_hbm.1, s32[]{:T(128)S(6)} %select_n.88, s32[]{:T(128)S(6)} %select_n.87), kind=kLoop, calls=%fused_computation.31 | loop fusion | bytes 2621448 | tf_op jit(solution)/shard_map/dynamic_slice | solution.py:569
  2.4 0.7 collective-permute-start.1
  3.1 5.4 %collective-permute-start = (bf16[32,8,1280]{2,1,0:T(8,128)(2,1)}, bf16[32,8,1280]{2,1,0:T(8,128)(2,1)S(1)}, u32[]{:S(2)}, u32[]{:S(2)}) collective-permute-start(bf16[32,8,1280]{2,1,0:T(8,128)(2,1)} %get-tuple-element.60), channel_id=1, source_target_pairs={{0,1},{2,3},{4,5},{6,7},{8,9},{10,11},{12,13},{14,15},{1,0},{3,2},... | collective-permute-start | bytes 1966088 | tf_op jit(solution)/shard_map/ppermute | solution.py:547
  8.5 8.1 %project.1 = bf16[16,8,32,384]{3,2,1,0:T(8,128)(2,1)} custom-call(bf16[512,1280]{1,0:T(8,128)(2,1)} %bitcast.14, bf16[1280,1024]{1,0:T(8,128)(2,1)} %wq_hbm.3, bf16[1280,2048]{1,0:T(8,128)(2,1)} %wkv_hbm.3), custom_call_target="tpu_custom_call" | custom-call | flops 4026531840 | bytes 12320768 | tf_op jit(solution)/shard_map/project/pallas_call | solution.py:114
  16.6 0.6 add_convert_fusion.even
  17.3 5.6 %collective-permute-done.cols_1_ref = bf16[32,8,1280]{2,1,0:T(8,128)(2,1)S(1)} collective-permute-done((bf16[32,8,1280]{2,1,0:T(8,128)(2,1)}, bf16[32,8,1280]{2,1,0:T(8,128)(2,1)S(1)}, u32[]{:S(2)}, u32[]{:S(2)}) %collective-permute-start) | collective-permute-done | bytes 655392 | tf_op jit(solution)/shard_map/ppermute | solution.py:547
  23.0 0.7 copy-done.2
  23.8 0.5 broadcast_select_fusion.2
  24.3 4.6 %collective-permute-start.3 = (bf16[8,32,1280]{2,1,0:T(8,128)(2,1)S(1)}, bf16[8,32,1280]{2,1,0:T(8,128)(2,1)S(1)}, u32[]{:S(2)}, u32[]{:S(2)}) collective-permute-start(bf16[8,32,1280]{2,1,0:T(8,128)(2,1)S(1)} %get-tuple-element.53), channel_id=1, source_target_pairs={{16,32},{48,64},{80,96},{32,16},{64,48},{96,80},{17,33},{49,65},{8... | collective-permute-start | bytes 1966088 | tf_op jit(solution)/shard_map/ppermute | solution.py:547
  28.9 11.0 %all-to-all-start = ((bf16[128,32,384]{2,1,0:T(8,128)(2,1)}), bf16[128,32,384]{2,1,0:T(8,128)(2,1)}, u32[]{:S(2)}, u32[]{:S(2)}) async-start(bf16[128,32,384]{2,1,0:T(8,128)(2,1)} %bitcast.1), calls=%async_computation | async-start | bytes 6291456 | tf_op jit(solution)/shard_map/all_to_all | solution.py:539
  40.0 0.9 copy-done.7
  41.1 29.1 %windows.1 = (bf16[8,32,1152]{2,1,0:T(8,128)(2,1)}, bf16[8,32,1152]{2,1,0:T(8,128)(2,1)}, bf16[32,16,1152]{2,1,0:T(8,128)(2,1)}, bf16[16,8,1152]{2,1,0:T(8,128)(...) custom-call(s32[2]{0:T(128)} %add_convert_fusion.even, ...), custom_call_target="tpu_custom_call" | custom-call | flops 135291469824 | bytes 11796480 | tf_op jit(solution)/shard_map/windows/pallas_call | solution.py:388
  70.3 0.7 collective-permute-start.7
  71.0 5.3 %collective-permute-start.5 = (bf16[8,32,1152]{2,1,0:T(8,128)(2,1)}, bf16[8,32,1152]{2,1,0:T(8,128)(2,1)S(1)}, u32[]{:S(2)}, u32[]{:S(2)}) collective-permute-start(bf16[8,32,1152]{2,1,0:T(8,128)(2,1)} %get-tuple-element.33), channel_id=1, source_target_pairs={{16,32},{48,64},{80,96},{32,16},{64,48},{96,80},{17,33},{49,65},{8... | collective-permute-start | bytes 1769480 | tf_op jit(solution)/shard_map/ppermute | solution.py:547
  76.3 4.2 %all-to-all-done = bf16[128,32,384]{2,1,0:T(8,128)(2,1)} async-done(((bf16[128,32,384]{2,1,0:T(8,128)(2,1)}), bf16[128,32,384]{2,1,0:T(8,128)(2,1)}, u32[]{:S(2)}, u32[]{:S(2)}) %all-to-all-start) | async-done | bytes 3145760 | tf_op jit(solution)/shard_map/all_to_all | solution.py:539
  80.6 38.5 %lattice_attend_0.1.refs_0_ = bf16[64,4096]{1,0:T(8,128)(2,1)} custom-call(bf16[4096,384]{1,0:T(8,128)(2,1)} %bitcast.2.qk_ref.v_ref, bf16[4096,384]{1,0:T(8,128)(2,1)} %bitcast.2.qk_ref.v_ref), custom_call_target="tpu_custom_call" | custom-call | flops 17179869184 | bytes 3145728 | tf_op jit(solution)/shard_map/lattice_attend_0/pallas_call | solution.py:236
  119.2 0.7 copy-done.3
  120.7 0.9 collective-permute-start.9
  121.6 39.0 %lattice_attend_1.1 = bf16[4096,128]{1,0:T(8,128)(2,1)} custom-call(bf16[4096,384]{1,0:T(8,128)(2,1)} %bitcast.2.qk_ref.v_ref, bf16[4096,384]{1,0:T(8,128)(2,1)} %bitcast.2.qk_ref.v_ref, bf16[64,4096]{1,0:T(8,128)(2,1)} %lattice_attend_0.1.refs_0_), custom_call_target="tpu_custom_call" | custom-call | flops 17179869184 | bytes 3145728 | tf_op jit(solution)/shard_map/lattice_attend_1/pallas_call | solution.py:236
  160.7 10.3 %all-to-all-start.1 = ((bf16[128,32,128]{2,1,0:T(8,128)(2,1)}), bf16[128,32,128]{2,1,0:T(8,128)(2,1)}, u32[]{:S(2)}, u32[]{:S(2)}) async-start(bf16[128,32,128]{2,1,0:T(8,128)(2,1)} %bitcast.16), calls=%async_computation.1 | async-start | bytes 2097152 | tf_op jit(solution)/shard_map/all_to_all | solution.py:539
  171.1 1.1 fusion.3.beside_ref
  172.2 7.1 %settle.1 = (f32[512,1280]{1,0:T(8,128)}, f32[512,128]{1,0:T(8,128)}) custom-call(s32[2]{0:T(128)} %add_convert_fusion.even, bf16[32,16,1152]{2,1,0:T(8,128)(2,1)} %get-tuple-element.46.mid_ref, bf16[8,32,1152]{2,1,0:T(8,128)(2,1)} %copy-done.3, bf16[8,32,1152]{2,1,0:T(8,128)(2,1)} %copy-done.4, bf16[32,16,1152]{2,1,0:T(8,128)(2,1)} %fusion.3.beside_ref, ...), custom_call_target="tpu_custom_call" | custom-call | flops 77309411328 | bytes 7077888 | tf_op jit(solution)/shard_map/settle/pallas_call | solution.py:455
  179.3 10.2 %all-to-all-done.1 = bf16[128,32,128]{2,1,0:T(8,128)(2,1)} async-done(((bf16[128,32,128]{2,1,0:T(8,128)(2,1)}), bf16[128,32,128]{2,1,0:T(8,128)(2,1)}, u32[]{:S(2)}, u32[]{:S(2)}) %all-to-all-start.1) | async-done | bytes 1048608 | tf_op jit(solution)/shard_map/all_to_all | solution.py:539
  189.5 5.1 %blend.1 = bf16[512,1280]{1,0:T(8,128)(2,1)} custom-call(bf16[16,8,32,128]{3,2,1,0:T(8,128)(2,1)} %bitcast.9.mixed_hbm, f32[512,128]{1,0:T(8,128)} %get-tuple-element.51.share_hbm, f32[512,1280]{1,0:T(8,128)} %get-tuple-element.52.base_hbm, bf16[1024,1280]{1,0:T(8,128)(2,1)} %w_hbm.1), custom_call_target="tpu_custom_call" | custom-call | flops 1879048192 | bytes 6553600 | tf_op jit(solution)/shard_map/blend/pallas_call | solution.py:516
  (38 shorter events, 1.7 us)
Async XLA Ops:
  2.4 14.8 %collective-permute-start.1 = (bf16[32,8,1280]{2,1,0:T(8,128)(2,1)}, bf16[32,8,1280]{2,1,0:T(8,128)(2,1)S(1)}, u32[]{:S(2)}, u32[]{:S(2)}) collective-permute-start(bf16[32,8,1280]{2,1,0:T(8,128)(2,1)} %get-tuple-element.59), channel_id=1, source_target_pairs={{1,2},{3,4},{5,6},{7,8},{9,10},{11,12},{13,14},{2,1},{4,3},{6,5},{... | collective-permute-start | bytes 1966088 | tf_op jit(solution)/shard_map/ppermute | solution.py:547
  3.1 19.7 %collective-permute-start = (bf16[32,8,1280]{2,1,0:T(8,128)(2,1)}, bf16[32,8,1280]{2,1,0:T(8,128)(2,1)S(1)}, u32[]{:S(2)}, u32[]{:S(2)}) collective-permute-start(bf16[32,8,1280]{2,1,0:T(8,128)(2,1)} %get-tuple-element.60), channel_id=1, source_target_pairs={{0,1},{2,3},{4,5},{6,7},{8,9},{10,11},{12,13},{14,15},{1,0},{3,2},... | collective-permute-start | bytes 1966088 | tf_op jit(solution)/shard_map/ppermute | solution.py:547
  8.5 8.7 %copy-start = (bf16[32,16,1280]{2,1,0:T(8,128)(2,1)S(1)}, bf16[32,16,1280]{2,1,0:T(8,128)(2,1)}, u32[]{:S(2)}) copy-start(bf16[32,16,1280]{2,1,0:T(8,128)(2,1)} %mid_hbm.1) | copy-start | bytes 3932164
  17.3 5.7 %copy-start.1 = (bf16[32,8,1280]{2,1,0:T(8,128)(2,1)}, bf16[32,8,1280]{2,1,0:T(8,128)(2,1)S(1)}, u32[]{:S(2)}) copy-start(bf16[32,8,1280]{2,1,0:T(8,128)(2,1)S(1)} %collective-permute-done.1.cols_2_ref) | copy-start | bytes 1966084
  22.9 0.8 copy-start.2
  24.3 15.7 %collective-permute-start.3 = (bf16[8,32,1280]{2,1,0:T(8,128)(2,1)S(1)}, bf16[8,32,1280]{2,1,0:T(8,128)(2,1)S(1)}, u32[]{:S(2)}, u32[]{:S(2)}) collective-permute-start(bf16[8,32,1280]{2,1,0:T(8,128)(2,1)S(1)} %get-tuple-element.53), channel_id=1, source_target_pairs={{16,32},{48,64},{80,96},{32,16},{64,48},{96,80},{17,33},{49,65},{8... | collective-permute-start | bytes 1966088 | tf_op jit(solution)/shard_map/ppermute | solution.py:547
  28.8 11.1 %collective-permute-start.2 = (bf16[8,32,1280]{2,1,0:T(8,128)(2,1)S(1)}, bf16[8,32,1280]{2,1,0:T(8,128)(2,1)S(1)}, u32[]{:S(2)}, u32[]{:S(2)}) collective-permute-start(bf16[8,32,1280]{2,1,0:T(8,128)(2,1)S(1)} %get-tuple-element.54), channel_id=1, source_target_pairs={{0,16},{32,48},{64,80},{96,112},{16,0},{48,32},{80,64},{112,96},{1... | collective-permute-start | bytes 1966088 | tf_op jit(solution)/shard_map/ppermute | solution.py:547
  28.9 51.6 %all-to-all-start = ((bf16[128,32,384]{2,1,0:T(8,128)(2,1)}), bf16[128,32,384]{2,1,0:T(8,128)(2,1)}, u32[]{:S(2)}, u32[]{:S(2)}) async-start(bf16[128,32,384]{2,1,0:T(8,128)(2,1)} %bitcast.1), calls=%async_computation | async-start | bytes 6291456 | tf_op jit(solution)/shard_map/all_to_all | solution.py:539
  40.0 0.9 copy-start.7
  40.0 1.1 copy-start.8
  70.2 48.9 %collective-permute-start.6 = (bf16[16,8,1152]{2,1,0:T(8,128)(2,1)}, bf16[16,8,1152]{2,1,0:T(8,128)(2,1)S(1)}, u32[]{:S(2)}, u32[]{:S(2)}) collective-permute-start(bf16[16,8,1152]{2,1,0:T(8,128)(2,1)} %get-tuple-element.34), channel_id=1, source_target_pairs={{0,1},{2,3},{4,5},{6,7},{8,9},{10,11},{12,13},{14,15},{1,0},{3,2},... | collective-permute-start | bytes 884744 | tf_op jit(solution)/shard_map/ppermute | solution.py:547
  70.3 48.8 %collective-permute-start.7 = (bf16[16,8,1152]{2,1,0:T(8,128)(2,1)}, bf16[16,8,1152]{2,1,0:T(8,128)(2,1)S(1)}, u32[]{:S(2)}, u32[]{:S(2)}) collective-permute-start(bf16[16,8,1152]{2,1,0:T(8,128)(2,1)} %get-tuple-element.35), channel_id=1, source_target_pairs={{1,2},{3,4},{5,6},{7,8},{9,10},{11,12},{13,14},{2,1},{4,3},{6,5},{... | collective-permute-start | bytes 884744 | tf_op jit(solution)/shard_map/ppermute | solution.py:547
  70.9 48.1 %collective-permute-start.4 = (bf16[8,32,1152]{2,1,0:T(8,128)(2,1)}, bf16[8,32,1152]{2,1,0:T(8,128)(2,1)S(1)}, u32[]{:S(2)}, u32[]{:S(2)}) collective-permute-start(bf16[8,32,1152]{2,1,0:T(8,128)(2,1)} %get-tuple-element.32), channel_id=1, source_target_pairs={{0,16},{32,48},{64,80},{96,112},{16,0},{48,32},{80,64},{112,96},{1... | collective-permute-start | bytes 1769480 | tf_op jit(solution)/shard_map/ppermute | solution.py:547
  71.0 48.0 %collective-permute-start.5 = (bf16[8,32,1152]{2,1,0:T(8,128)(2,1)}, bf16[8,32,1152]{2,1,0:T(8,128)(2,1)S(1)}, u32[]{:S(2)}, u32[]{:S(2)}) collective-permute-start(bf16[8,32,1152]{2,1,0:T(8,128)(2,1)} %get-tuple-element.33), channel_id=1, source_target_pairs={{16,32},{48,64},{80,96},{32,16},{64,48},{96,80},{17,33},{49,65},{8... | collective-permute-start | bytes 1769480 | tf_op jit(solution)/shard_map/ppermute | solution.py:547
  119.0 1.1 copy-start.5
  119.0 1.4 copy-start.6
  119.0 0.8 copy-start.3
  119.1 1.0 copy-start.4
  120.6 40.1 %collective-permute-start.8 = (bf16[16,8,1152]{2,1,0:T(8,128)(2,1)S(1)}, bf16[16,8,1152]{2,1,0:T(8,128)(2,1)S(1)}, u32[]{:S(2)}, u32[]{:S(2)}) collective-permute-start(bf16[16,8,1152]{2,1,0:T(8,128)(2,1)S(1)} %get-tuple-element.43), channel_id=1, source_target_pairs={{0,1},{2,3},{4,5},{6,7},{8,9},{10,11},{12,13},{14,15},{1,0},{3,2},... | collective-permute-start | bytes 884744 | tf_op jit(solution)/shard_map/ppermute | solution.py:547
  120.7 40.0 %collective-permute-start.9 = (bf16[16,8,1152]{2,1,0:T(8,128)(2,1)S(1)}, bf16[16,8,1152]{2,1,0:T(8,128)(2,1)S(1)}, u32[]{:S(2)}, u32[]{:S(2)}) collective-permute-start(bf16[16,8,1152]{2,1,0:T(8,128)(2,1)S(1)} %get-tuple-element.44), channel_id=1, source_target_pairs={{1,2},{3,4},{5,6},{7,8},{9,10},{11,12},{13,14},{2,1},{4,3},{6,5},{... | collective-permute-start | bytes 884744 | tf_op jit(solution)/shard_map/ppermute | solution.py:547
  160.7 28.9 %all-to-all-start.1 = ((bf16[128,32,128]{2,1,0:T(8,128)(2,1)}), bf16[128,32,128]{2,1,0:T(8,128)(2,1)}, u32[]{:S(2)}, u32[]{:S(2)}) async-start(bf16[128,32,128]{2,1,0:T(8,128)(2,1)} %bitcast.16), calls=%async_computation.1 | async-start | bytes 2097152 | tf_op jit(solution)/shard_map/all_to_all | solution.py:539

commit v9 on v8

--- a/solution.py
+++ b/solution.py
@@ -445,7 +445,7 @@
     for c in range(0, base_ref.shape[1], width):
         cols = slice(c, c + width)
         y = x_ref[:, cols].astype(F32) + dot(own[...], w_ref[:, cols])
-        base_ref[:, cols] = jnp.where(known_cell, known_ref[:, cols].astype(F32), y)
+        base_ref[:, cols] = jnp.where(known_cell, known_ref[:, cols].astype(F32), y).astype(BF16)
 
 
 def settle(even, mid, rim_1, rim_2, beside, mask, x, known, w_out):
@@ -457,7 +457,7 @@
         in_specs=[pl.BlockSpec(memory_space=pltpu.SMEM)] + [vmem] * 8,
         out_specs=[vmem] * 2,
         out_shape=[
-            jax.ShapeDtypeStruct((count, channels), F32),
+            jax.ShapeDtypeStruct((count, channels), BF16),
             jax.ShapeDtypeStruct((count, LANES), F32),
         ],
         scratch_shapes=[pltpu.VMEM((count, wide - LANES), BF16)],
@@ -499,7 +499,7 @@
         part = dot(blended[...], w_ref[:, cols])
         if i == 0:
             copies[3].wait()
-        out_ref[:, cols] = (base_ref[:, cols] + part).astype(BF16)
+        out_ref[:, cols] = (base_ref[:, cols].astype(F32) + part).astype(BF16)
         outs.append(
             pltpu.make_async_copy(out_ref.at[:, cols], out_hbm.at[:, cols], out_sems.at[i])
         )

time: 196 us -> 196 us (level)
  starting transfers between devices: 39.2 us -> 50.4 us
  Pallas kernels: 127 us -> 116 us
    ppermute x10, starting transfers between devices: 17.9 us -> 28.7 us  [meet(): met.append(lax.ppermute(array, axis, pairs + [(j, i) for i, j in pairs]))]
    pallas_call x1, Pallas kernels: 29.1 us -> 18.2 us  [windows(): pl.pallas_call(windows_kernel, in_specs=[smem] * 3 + [free] * 3 + [vmem]...]
  transfers between devices with their start and end apart: 12 -> 12, of which waited for: 3 -> 3; matrix products, arithmetic and copies ran while one was open for 1% -> 1% of each run, Pallas kernels for 62% -> 57%
where the time goes in v9:
time: 196 us; the launch traced here: 195 us
  Pallas kernels  116 us (59%)
  starting transfers between devices  50.4 us (26%)
  waiting for transfers between devices  20.5 us (10%)
  local copies, waits for them, and re-layouts  5.51 us (3%)
  other arithmetic  2.77 us (1%)
    pallas_call x2, Pallas kernels, lattice_attend(): pl.pallas_call(functools.partial(lattice_kernel, head), grid=(count // QB...  77.5 us
    ppermute x10, starting transfers between devices, meet(): met.append(lax.ppermute(array, axis, pairs + [(j, i) for i, j in pairs]))  28.7 us
    all_to_all x2, starting transfers between devices, exchange(): lax.all_to_all(pieces, ('row', 'col'), split_axis=0, concat_axis=0, tiled...  21.6 us
    pallas_call x1, Pallas kernels, windows(): pl.pallas_call(windows_kernel, in_specs=[smem] * 3 + [free] * 3 + [vmem]...  18.2 us
    all_to_all x2, waiting for transfers between devices, exchange(): lax.all_to_all(pieces, ('row', 'col'), split_axis=0, concat_axis=0, tiled...  14.9 us
    pallas_call x1, Pallas kernels, project(): pl.pallas_call(project_kernel, in_specs=[free] * 3, out_specs=free, out_s...  8.09 us
    pallas_call x1, Pallas kernels, settle(): pl.pallas_call(settle_kernel, in_specs=[pl.BlockSpec(memory_space=pltpu.S...  6.66 us
    ppermute x10, waiting for transfers between devices, meet(): met.append(lax.ppermute(array, axis, pairs + [(j, i) for i, j in pairs]))  5.62 us
  transfers between devices with their start and end apart: 12, of which 3 were waited for; matrix products, arithmetic and copies ran while one was open for 1% of the time, Pallas kernels for 57%

profile of v9, /device:TPU:1, one launch (start us, length us, event | category | flops | bytes accessed | tf_op | source)
XLA Modules:
  0.0 195.2 jit_solution(11143461638320975613)
XLA Ops:
  0.0 2.4 %constant_dynamic-slice_fusion = (bf16[32,8,1280]{2,1,0:T(8,128)(2,1)}, bf16[32,8,1280]{2,1,0:T(8,128)(2,1)}) fusion(bf16[32,16,1280]{2,1,0:T(8,128)(2,1)} %mid_hbm.1, s32[]{:T(128)S(6)} %select_n.88, s32[]{:T(128)S(6)} %select_n.87), kind=kLoop, calls=%fused_computation.31 | loop fusion | bytes 2621448 | tf_op jit(solution)/shard_map/dynamic_slice | solution.py:569
  2.4 0.7 collective-permute-start.1
  3.1 5.4 %collective-permute-start = (bf16[32,8,1280]{2,1,0:T(8,128)(2,1)}, bf16[32,8,1280]{2,1,0:T(8,128)(2,1)S(1)}, u32[]{:S(2)}, u32[]{:S(2)}) collective-permute-start(bf16[32,8,1280]{2,1,0:T(8,128)(2,1)} %get-tuple-element.60), channel_id=1, source_target_pairs={{0,1},{2,3},{4,5},{6,7},{8,9},{10,11},{12,13},{14,15},{1,0},{3,2},... | collective-permute-start | bytes 1966088 | tf_op jit(solution)/shard_map/ppermute | solution.py:547
  8.5 8.1 %project.1 = bf16[16,8,32,384]{3,2,1,0:T(8,128)(2,1)} custom-call(bf16[512,1280]{1,0:T(8,128)(2,1)} %bitcast.14, bf16[1280,1024]{1,0:T(8,128)(2,1)} %wq_hbm.3, bf16[1280,2048]{1,0:T(8,128)(2,1)} %wkv_hbm.3), custom_call_target="tpu_custom_call" | custom-call | flops 4026531840 | bytes 12320768 | tf_op jit(solution)/shard_map/project/pallas_call | solution.py:114
  16.6 0.6 add_convert_fusion.even
  17.3 5.6 %collective-permute-done.cols_1_ref = bf16[32,8,1280]{2,1,0:T(8,128)(2,1)S(1)} collective-permute-done((bf16[32,8,1280]{2,1,0:T(8,128)(2,1)}, bf16[32,8,1280]{2,1,0:T(8,128)(2,1)S(1)}, u32[]{:S(2)}, u32[]{:S(2)}) %collective-permute-start) | collective-permute-done | bytes 655392 | tf_op jit(solution)/shard_map/ppermute | solution.py:547
  23.0 0.7 copy-done.2
  24.3 4.6 %collective-permute-start.3 = (bf16[8,32,1280]{2,1,0:T(8,128)(2,1)S(1)}, bf16[8,32,1280]{2,1,0:T(8,128)(2,1)S(1)}, u32[]{:S(2)}, u32[]{:S(2)}) collective-permute-start(bf16[8,32,1280]{2,1,0:T(8,128)(2,1)S(1)} %get-tuple-element.53), channel_id=1, source_target_pairs={{16,32},{48,64},{80,96},{32,16},{64,48},{96,80},{17,33},{49,65},{8... | collective-permute-start | bytes 1966088 | tf_op jit(solution)/shard_map/ppermute | solution.py:547
  28.9 11.0 %all-to-all-start = ((bf16[128,32,384]{2,1,0:T(8,128)(2,1)}), bf16[128,32,384]{2,1,0:T(8,128)(2,1)}, u32[]{:S(2)}, u32[]{:S(2)}) async-start(bf16[128,32,384]{2,1,0:T(8,128)(2,1)} %bitcast.1), calls=%async_computation | async-start | bytes 6291456 | tf_op jit(solution)/shard_map/all_to_all | solution.py:539
  40.0 0.9 copy-done.7
  41.1 18.2 %windows.1 = (bf16[8,32,1152]{2,1,0:T(8,128)(2,1)}, bf16[8,32,1152]{2,1,0:T(8,128)(2,1)}, bf16[32,16,1152]{2,1,0:T(8,128)(2,1)}, bf16[16,8,1152]{2,1,0:T(8,128)(...) custom-call(s32[2]{0:T(128)} %add_convert_fusion.even, ...), custom_call_target="tpu_custom_call" | custom-call | flops 135291469824 | bytes 11796480 | tf_op jit(solution)/shard_map/windows/pallas_call | solution.py:388
  59.4 0.7 collective-permute-start.7
  60.1 12.1 %collective-permute-start.4 = (bf16[8,32,1152]{2,1,0:T(8,128)(2,1)}, bf16[8,32,1152]{2,1,0:T(8,128)(2,1)S(1)}, u32[]{:S(2)}, u32[]{:S(2)}) collective-permute-start(bf16[8,32,1152]{2,1,0:T(8,128)(2,1)} %get-tuple-element.32), channel_id=1, source_target_pairs={{0,16},{32,48},{64,80},{96,112},{16,0},{48,32},{80,64},{112,96},{1... | collective-permute-start | bytes 1769480 | tf_op jit(solution)/shard_map/ppermute | solution.py:547
  72.2 4.2 %collective-permute-start.5 = (bf16[8,32,1152]{2,1,0:T(8,128)(2,1)}, bf16[8,32,1152]{2,1,0:T(8,128)(2,1)S(1)}, u32[]{:S(2)}, u32[]{:S(2)}) collective-permute-start(bf16[8,32,1152]{2,1,0:T(8,128)(2,1)} %get-tuple-element.33), channel_id=1, source_target_pairs={{16,32},{48,64},{80,96},{32,16},{64,48},{96,80},{17,33},{49,65},{8... | collective-permute-start | bytes 1769480 | tf_op jit(solution)/shard_map/ppermute | solution.py:547
  76.3 4.2 %all-to-all-done = bf16[128,32,384]{2,1,0:T(8,128)(2,1)} async-done(((bf16[128,32,384]{2,1,0:T(8,128)(2,1)}), bf16[128,32,384]{2,1,0:T(8,128)(2,1)}, u32[]{:S(2)}, u32[]{:S(2)}) %all-to-all-start) | async-done | bytes 3145760 | tf_op jit(solution)/shard_map/all_to_all | solution.py:539
  80.5 38.5 %lattice_attend_0.1.refs_0_ = bf16[64,4096]{1,0:T(8,128)(2,1)} custom-call(bf16[4096,384]{1,0:T(8,128)(2,1)} %bitcast.2.qk_ref.v_ref, bf16[4096,384]{1,0:T(8,128)(2,1)} %bitcast.2.qk_ref.v_ref), custom_call_target="tpu_custom_call" | custom-call | flops 17179869184 | bytes 3145728 | tf_op jit(solution)/shard_map/lattice_attend_0/pallas_call | solution.py:236
  119.2 0.6 copy-done.3
  120.7 0.9 collective-permute-start.9
  121.6 39.0 %lattice_attend_1.1 = bf16[4096,128]{1,0:T(8,128)(2,1)} custom-call(bf16[4096,384]{1,0:T(8,128)(2,1)} %bitcast.2.qk_ref.v_ref, bf16[4096,384]{1,0:T(8,128)(2,1)} %bitcast.2.qk_ref.v_ref, bf16[64,4096]{1,0:T(8,128)(2,1)} %lattice_attend_0.1.refs_0_), custom_call_target="tpu_custom_call" | custom-call | flops 17179869184 | bytes 3145728 | tf_op jit(solution)/shard_map/lattice_attend_1/pallas_call | solution.py:236
  160.7 10.6 %all-to-all-start.1 = ((bf16[128,32,128]{2,1,0:T(8,128)(2,1)}), bf16[128,32,128]{2,1,0:T(8,128)(2,1)}, u32[]{:S(2)}, u32[]{:S(2)}) async-start(bf16[128,32,128]{2,1,0:T(8,128)(2,1)} %bitcast.16), calls=%async_computation.1 | async-start | bytes 2097152 | tf_op jit(solution)/shard_map/all_to_all | solution.py:539
  171.4 1.1 fusion.3.beside_ref
  172.5 6.7 %settle.1 = (bf16[512,1280]{1,0:T(8,128)(2,1)}, f32[512,128]{1,0:T(8,128)}) custom-call(s32[2]{0:T(128)} %add_convert_fusion.even, bf16[32,16,1152]{2,1,0:T(8,128)(2,1)} %get-tuple-element.46.mid_ref, bf16[8,32,1152]{2,1,0:T(8,128)(2,1)} %copy-done.3, bf16[8,32,1152]{2,1,0:T(8,128)(2,1)} %copy-done.4, bf16[32,16,1152]{2,1,0:T(8,128)(2,1)} %fusion.3.beside_ref, ...), custom_call_target="tpu_custom_call" | custom-call | flops 77309411328 | bytes 7077888 | tf_op jit(solution)/shard_map/settle/pallas_call | solution.py:455
  179.2 10.7 %all-to-all-done.1 = bf16[128,32,128]{2,1,0:T(8,128)(2,1)} async-done(((bf16[128,32,128]{2,1,0:T(8,128)(2,1)}), bf16[128,32,128]{2,1,0:T(8,128)(2,1)}, u32[]{:S(2)}, u32[]{:S(2)}) %all-to-all-start.1) | async-done | bytes 1048608 | tf_op jit(solution)/shard_map/all_to_all | solution.py:539
  189.9 5.1 %blend.1 = bf16[512,1280]{1,0:T(8,128)(2,1)} custom-call(bf16[16,8,32,128]{3,2,1,0:T(8,128)(2,1)} %bitcast.9.mixed_hbm, f32[512,128]{1,0:T(8,128)} %get-tuple-element.51.share_hbm, bf16[512,1280]{1,0:T(8,128)(2,1)} %get-tuple-element.52.base_hbm, bf16[1024,1280]{1,0:T(8,128)(2,1)} %w_hbm.1), custom_call_target="tpu_custom_call" | custom-call | flops 1879048192 | bytes 6553600 | tf_op jit(solution)/shard_map/blend/pallas_call | solution.py:516
  (38 shorter events, 2.2 us)
Async XLA Ops:
  2.4 14.8 %collective-permute-start.1 = (bf16[32,8,1280]{2,1,0:T(8,128)(2,1)}, bf16[32,8,1280]{2,1,0:T(8,128)(2,1)S(1)}, u32[]{:S(2)}, u32[]{:S(2)}) collective-permute-start(bf16[32,8,1280]{2,1,0:T(8,128)(2,1)} %get-tuple-element.59), channel_id=1, source_target_pairs={{1,2},{3,4},{5,6},{7,8},{9,10},{11,12},{13,14},{2,1},{4,3},{6,5},{... | collective-permute-start | bytes 1966088 | tf_op jit(solution)/shard_map/ppermute | solution.py:547
  3.1 19.7 %collective-permute-start = (bf16[32,8,1280]{2,1,0:T(8,128)(2,1)}, bf16[32,8,1280]{2,1,0:T(8,128)(2,1)S(1)}, u32[]{:S(2)}, u32[]{:S(2)}) collective-permute-start(bf16[32,8,1280]{2,1,0:T(8,128)(2,1)} %get-tuple-element.60), channel_id=1, source_target_pairs={{0,1},{2,3},{4,5},{6,7},{8,9},{10,11},{12,13},{14,15},{1,0},{3,2},... | collective-permute-start | bytes 1966088 | tf_op jit(solution)/shard_map/ppermute | solution.py:547
  8.5 8.7 %copy-start = (bf16[32,16,1280]{2,1,0:T(8,128)(2,1)S(1)}, bf16[32,16,1280]{2,1,0:T(8,128)(2,1)}, u32[]{:S(2)}) copy-start(bf16[32,16,1280]{2,1,0:T(8,128)(2,1)} %mid_hbm.1) | copy-start | bytes 3932164
  17.3 5.7 %copy-start.1 = (bf16[32,8,1280]{2,1,0:T(8,128)(2,1)}, bf16[32,8,1280]{2,1,0:T(8,128)(2,1)S(1)}, u32[]{:S(2)}) copy-start(bf16[32,8,1280]{2,1,0:T(8,128)(2,1)S(1)} %collective-permute-done.1.cols_2_ref) | copy-start | bytes 1966084
  22.9 0.8 copy-start.2
  24.3 15.7 %collective-permute-start.3 = (bf16[8,32,1280]{2,1,0:T(8,128)(2,1)S(1)}, bf16[8,32,1280]{2,1,0:T(8,128)(2,1)S(1)}, u32[]{:S(2)}, u32[]{:S(2)}) collective-permute-start(bf16[8,32,1280]{2,1,0:T(8,128)(2,1)S(1)} %get-tuple-element.53), channel_id=1, source_target_pairs={{16,32},{48,64},{80,96},{32,16},{64,48},{96,80},{17,33},{49,65},{8... | collective-permute-start | bytes 1966088 | tf_op jit(solution)/shard_map/ppermute | solution.py:547
  28.8 11.1 %collective-permute-start.2 = (bf16[8,32,1280]{2,1,0:T(8,128)(2,1)S(1)}, bf16[8,32,1280]{2,1,0:T(8,128)(2,1)S(1)}, u32[]{:S(2)}, u32[]{:S(2)}) collective-permute-start(bf16[8,32,1280]{2,1,0:T(8,128)(2,1)S(1)} %get-tuple-element.54), channel_id=1, source_target_pairs={{0,16},{32,48},{64,80},{96,112},{16,0},{48,32},{80,64},{112,96},{1... | collective-permute-start | bytes 1966088 | tf_op jit(solution)/shard_map/ppermute | solution.py:547
  28.9 51.6 %all-to-all-start = ((bf16[128,32,384]{2,1,0:T(8,128)(2,1)}), bf16[128,32,384]{2,1,0:T(8,128)(2,1)}, u32[]{:S(2)}, u32[]{:S(2)}) async-start(bf16[128,32,384]{2,1,0:T(8,128)(2,1)} %bitcast.1), calls=%async_computation | async-start | bytes 6291456 | tf_op jit(solution)/shard_map/all_to_all | solution.py:539
  40.0 0.9 copy-start.7
  40.0 1.1 copy-start.8
  59.3 59.7 %collective-permute-start.6 = (bf16[16,8,1152]{2,1,0:T(8,128)(2,1)}, bf16[16,8,1152]{2,1,0:T(8,128)(2,1)S(1)}, u32[]{:S(2)}, u32[]{:S(2)}) collective-permute-start(bf16[16,8,1152]{2,1,0:T(8,128)(2,1)} %get-tuple-element.34), channel_id=1, source_target_pairs={{0,1},{2,3},{4,5},{6,7},{8,9},{10,11},{12,13},{14,15},{1,0},{3,2},... | collective-permute-start | bytes 884744 | tf_op jit(solution)/shard_map/ppermute | solution.py:547
  59.4 59.6 %collective-permute-start.7 = (bf16[16,8,1152]{2,1,0:T(8,128)(2,1)}, bf16[16,8,1152]{2,1,0:T(8,128)(2,1)S(1)}, u32[]{:S(2)}, u32[]{:S(2)}) collective-permute-start(bf16[16,8,1152]{2,1,0:T(8,128)(2,1)} %get-tuple-element.35), channel_id=1, source_target_pairs={{1,2},{3,4},{5,6},{7,8},{9,10},{11,12},{13,14},{2,1},{4,3},{6,5},{... | collective-permute-start | bytes 884744 | tf_op jit(solution)/shard_map/ppermute | solution.py:547
  60.1 59.0 %collective-permute-start.4 = (bf16[8,32,1152]{2,1,0:T(8,128)(2,1)}, bf16[8,32,1152]{2,1,0:T(8,128)(2,1)S(1)}, u32[]{:S(2)}, u32[]{:S(2)}) collective-permute-start(bf16[8,32,1152]{2,1,0:T(8,128)(2,1)} %get-tuple-element.32), channel_id=1, source_target_pairs={{0,16},{32,48},{64,80},{96,112},{16,0},{48,32},{80,64},{112,96},{1... | collective-permute-start | bytes 1769480 | tf_op jit(solution)/shard_map/ppermute | solution.py:547
  72.2 46.9 %collective-permute-start.5 = (bf16[8,32,1152]{2,1,0:T(8,128)(2,1)}, bf16[8,32,1152]{2,1,0:T(8,128)(2,1)S(1)}, u32[]{:S(2)}, u32[]{:S(2)}) collective-permute-start(bf16[8,32,1152]{2,1,0:T(8,128)(2,1)} %get-tuple-element.33), channel_id=1, source_target_pairs={{16,32},{48,64},{80,96},{32,16},{64,48},{96,80},{17,33},{49,65},{8... | collective-permute-start | bytes 1769480 | tf_op jit(solution)/shard_map/ppermute | solution.py:547
  119.0 1.1 copy-start.5
  119.0 1.4 copy-start.6
  119.1 0.8 copy-start.3
  119.1 1.0 copy-start.4
  120.6 40.1 %collective-permute-start.8 = (bf16[16,8,1152]{2,1,0:T(8,128)(2,1)S(1)}, bf16[16,8,1152]{2,1,0:T(8,128)(2,1)S(1)}, u32[]{:S(2)}, u32[]{:S(2)}) collective-permute-start(bf16[16,8,1152]{2,1,0:T(8,128)(2,1)S(1)} %get-tuple-element.43), channel_id=1, source_target_pairs={{0,1},{2,3},{4,5},{6,7},{8,9},{10,11},{12,13},{14,15},{1,0},{3,2},... | collective-permute-start | bytes 884744 | tf_op jit(solution)/shard_map/ppermute | solution.py:547
  120.7 40.0 %collective-permute-start.9 = (bf16[16,8,1152]{2,1,0:T(8,128)(2,1)S(1)}, bf16[16,8,1152]{2,1,0:T(8,128)(2,1)S(1)}, u32[]{:S(2)}, u32[]{:S(2)}) collective-permute-start(bf16[16,8,1152]{2,1,0:T(8,128)(2,1)S(1)} %get-tuple-element.44), channel_id=1, source_target_pairs={{1,2},{3,4},{5,6},{7,8},{9,10},{11,12},{13,14},{2,1},{4,3},{6,5},{... | collective-permute-start | bytes 884744 | tf_op jit(solution)/shard_map/ppermute | solution.py:547
  160.7 29.2 %all-to-all-start.1 = ((bf16[128,32,128]{2,1,0:T(8,128)(2,1)}), bf16[128,32,128]{2,1,0:T(8,128)(2,1)}, u32[]{:S(2)}, u32[]{:S(2)}) async-start(bf16[128,32,128]{2,1,0:T(8,128)(2,1)} %bitcast.16), calls=%async_computation.1 | async-start | bytes 2097152 | tf_op jit(solution)/shard_map/all_to_all | solution.py:539
